TPU v7x, 512 devices: a whole 4x8x8 slice. The times are simulated.
512 devices in a mesh: dp: 64 (over y, z), tensor: 8 (over x, core).
Axes of the slice: x: 4, y: 8, z: 8, core: 2. Of those that a mesh axis runs over, the one named last changes fastest.
Arguments:
- acts: bfloat16 [131072, 1024], P(('dp', 'tensor')), may hold values from -6 to 6
- grads_out: bfloat16 [131072, 4096], P('dp', 'tensor'), may hold values from -0.125 to 0.125
- error_buffer: bfloat16 [64, 1024, 4096], P('dp', None, 'tensor'), may hold values from -3 to 3
- prior_q: bfloat16 [4096, 32], P('tensor'), may hold values from -6 to 6
Outputs:
- residual: bfloat16 [64, 1024, 4096], P('dp', None, 'tensor')
- p_basis: float32 [1024, 32], replicated
- q_factor: float32 [4096, 32], P('tensor')
All inputs are finite; a program needn't handle non-finite values.
Results may differ from a plain program's by a relative error of at most 0.001.
Values may be sent and summed in bfloat16 or wider, within the bound.
No kernel may reach another device: no remote copies, remote signals or barrier semaphores. Data moves between devices by JAX's collectives and lax.ppermute only.
A program may use at most 64 MiB of HBM per device.

v0:
```python
import jax
import jax.numpy as jnp
from jax import lax
from jax.sharding import PartitionSpec as P


def sum_left(partial_value):
    return lax.psum(partial_value, ("dp", "tensor"))


def per_device(acts, grads_out, error_buffer, prior_q):
    high = lax.Precision.HIGHEST
    q_local = prior_q.astype(jnp.float32)
    error = error_buffer[0].astype(jnp.float32)
    contract_rows = (((0,), (0,)), ((), ()))
    merged = (
        lax.dot_general(
            lax.all_gather(acts, "tensor", axis=0, tiled=True),
            grads_out,
            contract_rows,
            preferred_element_type=jnp.float32,
        )
        + error
    )
    partial_value = jnp.dot(merged, q_local, precision=high)
    p_sum = sum_left(partial_value)
    gram = jnp.dot(p_sum.T, p_sum, precision=high)
    chol = jnp.linalg.cholesky(gram)
    p_basis = jax.scipy.linalg.solve_triangular(chol, p_sum.T, lower=True).T
    q_partial = lax.dot_general(merged, p_basis, contract_rows, precision=high)
    q_factor = lax.psum(q_partial, "dp") / lax.axis_size("dp")
    rebuilt = merged - jnp.dot(p_basis, q_factor.T, precision=high)
    residual = rebuilt.astype(jnp.bfloat16)[None]
    return (residual, p_basis, q_factor)


def solution(mesh):
    in_specs = (
        P(("dp", "tensor"), None),
        P("dp", "tensor"),
        P("dp", None, "tensor"),
        P("tensor", None),
    )
    out_specs = (P("dp", None, "tensor"), P(), P("tensor", None))
    return jax.shard_map(
        per_device, mesh=mesh, in_specs=in_specs, out_specs=out_specs, check_vma=False
    )
```

profile of v0, /device:TPU:2, one launch (start us, length us, event | category | flops | bytes accessed | tf_op | source)
XLA Modules:
  0.0 489.7 jit_solution(15276024345995951342)
XLA Ops:
  7.2 0.0 copy-start
  7.2 0.0 all-gather.2.cloned.1.call-start
  7.2 0.7 all-gather.2.cloned.1.call-update
  7.9 0.0 copy-start.4
  7.9 0.0 all-reduce.3.cloned.1.call-start
  8.0 43.3 %all-gather.2.cloned.1.call-done = bf16[2048,1024]{1,0:T(8,128)(2,1)} async-done(((bf16[256,1024]{1,0:T(8,128)(2,1)}), bf16[2048,1024]{1,0:T(8,128)(2,1)}) %all-gather.2.cloned.1.call-update) | async-done | bytes 4194320 | tf_op jit(solution)/shard_map/all_gather | solution.py:18
  51.3 0.0 copy-done
  51.3 4.8 convert_add_fusion
  56.1 0.0 copy-start.1
  56.1 1.3 copy-done.1
  57.5 0.0 copy-done.4
  57.5 1.8 fusion.5
  59.3 0.0 all-reduce.3.cloned.1.call-update
  59.3 0.0 all-reduce.5.cloned.1.call-start
  59.3 260.6 %all-reduce.3.cloned.1.call-done = f32[1024,32]{0,1:T(8,128)} async-done(((f32[1024,32]{0,1:T(8,128)}), f32[1024,32]{0,1:T(8,128)}) %all-reduce.3.cloned.1.call-update) | async-done | bytes 131088 | tf_op jit(solution)/shard_map/psum | solution.py:8
  320.0 1.2 fusion.6
  321.2 0.1 copy.7
  321.3 2.9 cholesky.16
  324.2 0.6 compare_reduce_fusion
  324.9 0.7 fusion.1
  325.5 2.4 custom-call.7
  328.0 1.2 fusion.2
  329.2 0.0 copy-start.2
  329.2 3.6 fusion.7
  332.8 0.0 all-reduce.5.cloned.1.call-update
  332.9 145.1 %all-reduce.5.cloned.1.call-done = f32[512,32]{0,1:T(8,128)} async-done(((f32[512,32]{0,1:T(8,128)}), f32[512,32]{0,1:T(8,128)}) %all-reduce.5.cloned.1.call-update) | async-done | bytes 65552 | tf_op jit(solution)/shard_map/psum | solution.py:31
  477.9 0.8 broadcast_multiply_fusion
  478.8 0.0 copy-start.3
  478.8 4.4 fusion
  483.2 0.0 copy-done.2
  483.2 0.0 copy-done.3
  (2 shorter events, 0.0 us)
Async XLA Ops:
  7.2 44.1 %copy-start = (bf16[2048,512]{1,0:T(8,128)(2,1)S(1)}, bf16[2048,512]{1,0:T(8,128)(2,1)}, u32[]{:S(2)}) copy-start(bf16[2048,512]{1,0:T(8,128)(2,1)} %param.5) | copy-start | bytes 6291460
  7.2 44.1 %all-gather.2.cloned.1.call-start = ((), (), s32[]{:S(2)}) async-start(), calls=%async_computation | async-start | bytes 4718592 | tf_op jit(solution)/shard_map/all_gather | solution.py:18
  7.9 49.5 %copy-start.4 = (bf16[512,32]{0,1:T(8,128)(2,1)S(1)}, bf16[512,32]{0,1:T(8,128)(2,1)}, u32[]{:S(2)}) copy-start(bf16[512,32]{0,1:T(8,128)(2,1)} %param.7) | copy-start | bytes 98308
  7.9 312.0 %all-reduce.3.cloned.1.call-start = ((), (), s32[]{:S(2)}) async-start(), calls=%async_computation.1 | async-start | bytes 262144 | tf_op jit(solution)/shard_map/psum | solution.py:8
  56.1 1.3 copy-start.1
  59.3 418.6 %all-reduce.5.cloned.1.call-start = ((), (), s32[]{:S(2)}) async-start(), calls=%async_computation.2 | async-start | bytes 131072 | tf_op jit(solution)/shard_map/psum | solution.py:31
  329.2 154.0 %copy-start.2 = (f32[32,1024]{1,0:T(8,128)}, f32[32,1024]{1,0:T(8,128)S(1)}, u32[]{:S(2)}) copy-start(f32[32,1024]{1,0:T(8,128)S(1)} %fusion.2) | copy-start | bytes 393220
  478.8 4.5 copy-start.3
Sparse Core Ops, SparseCore 0:
  10.2 41.0 all-gather.1
  59.4 260.5 all-reduce.2
  333.0 144.8 all-reduce.4
where the time goes:
time: 490 us
  waiting for transfers between devices  450 us (92%)
  matrix products  17.2 us (4%)
  between operations  13.8 us (3%)
  other arithmetic  7.54 us (2%)
    psum x1, waiting for transfers between devices, sum_left(): return lax.psum(partial_value, ('dp', 'tensor'))  261 us
    psum x1, waiting for transfers between devices, per_device(): q_factor = lax.psum(q_partial, 'dp') / lax.axis_size('dp')  145 us
    all_gather x1, waiting for transfers between devices, per_device(): lax.all_gather(acts, 'tensor', axis=0, tiled=True)  43.3 us
  transfers between devices with their start and end apart: 3, of which 3 were waited for; matrix products, arithmetic and copies ran while one was open for 0% of the time, Pallas kernels for 0%

commit v1 on v0

v1 whole, which is shorter than its diff:
```python
import math

import jax
import jax.numpy as jnp
from jax import lax
from jax.experimental import pallas as pl
from jax.experimental.pallas import tpu as pltpu
from jax.sharding import PartitionSpec as P

F32 = jnp.float32
BF16 = jnp.bfloat16
VMEM = pl.BlockSpec(memory_space=pltpu.VMEM)
PARAMS = pltpu.CompilerParams(vmem_limit_bytes=32 * 1024 * 1024)
STREAM = pltpu.CompilerParams(vmem_limit_bytes=60 * 1024 * 1024)


def parts_of(x, n):
    out = []
    for _ in range(n):
        part = x.astype(BF16)
        out.append(part)
        x = x - part.astype(F32)
    return out


def dot(a, b, a_dim=1, b_dim=0):
    return lax.dot_general(
        a, b, (((a_dim,), (b_dim,)), ((), ())), preferred_element_type=F32
    )


def cost(flops, moved):
    return pl.CostEstimate(flops=flops, bytes_accessed=moved, transcendentals=0)


def y_kernel(q_ref, g_ref, out_ref, q_buf, g_buf, q_sem, g_sems):
    n, _, rows = out_ref.shape
    q_copy = pltpu.make_async_copy(q_ref, q_buf, q_sem)
    copies = [
        pltpu.make_async_copy(
            g_ref.at[pl.ds(s * rows, rows), :],
            g_buf.at[pl.ds(s * rows, rows), :],
            g_sems.at[s],
        )
        for s in range(n)
    ]
    q_copy.start()
    for copy in copies:
        copy.start()
    q_copy.wait()
    for s in range(n):
        copies[s].wait()
        out_ref[s] = dot(q_buf[...], g_buf[s * rows : (s + 1) * rows, :], 1, 1)


def y_chunks(q_t, grads, n):
    rank, cols = q_t.shape
    rows = grads.shape[0] // n
    hbm = pl.BlockSpec(memory_space=pltpu.HBM)
    return pl.pallas_call(
        y_kernel,
        in_specs=[hbm, hbm],
        out_specs=VMEM,
        out_shape=jax.ShapeDtypeStruct((n, rank, rows), F32),
        scratch_shapes=[
            pltpu.VMEM(q_t.shape, BF16),
            pltpu.VMEM(grads.shape, BF16),
            pltpu.SemaphoreType.DMA,
            pltpu.SemaphoreType.DMA((n,)),
        ],
        compiler_params=STREAM,
        cost_estimate=cost(2 * grads.size * rank * 8, grads.size * 2),
        name="y_chunks",
    )(q_t, grads)


def e_kernel(q_ref, e_ref, out_ref):
    out_ref[...] = dot(q_ref[...], e_ref[...], 1, 1)


def error_term(q_t, error):
    return pl.pallas_call(
        e_kernel,
        in_specs=[VMEM] * 2,
        out_specs=VMEM,
        out_shape=jax.ShapeDtypeStruct((q_t.shape[0], error.shape[0]), F32),
        compiler_params=PARAMS,
        cost_estimate=cost(2 * error.size * 32 * 8, error.size * 2),
        name="error_term",
    )(q_t, error)


def p_kernel(y_ref, acts_ref, e_ref, out_ref):
    n, rank, width = out_ref.shape
    y = y_ref[0]
    for s in range(1, n):
        y = y + y_ref[s]
    stack = jnp.concatenate(parts_of(y, 3), axis=0)
    p = dot(stack, acts_ref[...])
    p = (p[:rank] + e_ref[...]) + (p[rank : 2 * rank] + p[2 * rank :])
    for s in range(n):
        out_ref[s] = p[:, s * width : (s + 1) * width]


def p_chunks(y_all, acts, e_term):
    n, rank, _ = y_all.shape
    width = acts.shape[1] // n
    return pl.pallas_call(
        p_kernel,
        in_specs=[VMEM] * 3,
        out_specs=VMEM,
        out_shape=jax.ShapeDtypeStruct((n, rank, width), F32),
        compiler_params=PARAMS,
        cost_estimate=cost(2 * acts.size * rank * 8, acts.size * 2),
        name="p_chunks",
    )(y_all, acts, e_term)


def merged_kernel(a_ref, g_ref, e_ref, after_ref, hi_ref, lo_ref):
    del after_ref
    merged = dot(a_ref[...], g_ref[...], 0, 0) + e_ref[...].astype(F32)
    hi, lo = parts_of(merged, 2)
    hi_ref[...] = hi
    lo_ref[...] = lo


def merged_parts(acts_all, grads, error, after):
    tokens, width = acts_all.shape
    cols = grads.shape[1]
    block = 256
    shape = jax.ShapeDtypeStruct((width, cols), BF16)
    out = pl.BlockSpec((block, cols), lambda i: (i, 0))
    return pl.pallas_call(
        merged_kernel,
        grid=(width // block,),
        in_specs=[
            pl.BlockSpec((tokens, block), lambda i: (0, i)),
            pl.BlockSpec((tokens, cols), lambda i: (0, 0)),
            out,
            pl.BlockSpec(memory_space=pl.ANY),
        ],
        out_specs=[out, out],
        out_shape=[shape, shape],
        compiler_params=PARAMS,
        cost_estimate=cost(2 * tokens * width * cols, acts_all.size * 2 + grads.size * 2),
        name="merged_parts",
    )(acts_all, grads, error, after)


def q_kernel(p_ref, hi_ref, lo_ref, out_ref):
    n, rank, width = p_ref.shape
    pieces, rows, _ = out_ref.shape
    total = None
    for s in range(n):
        high, low = parts_of(p_ref[s], 2)
        span = slice(s * width, (s + 1) * width)
        both = dot(jnp.concatenate([high, low], axis=0), hi_ref[span, :])
        term = both[:rank] + (both[rank:] + dot(high, lo_ref[span, :]))
        total = term if total is None else total + term
    for k in range(pieces):
        out_ref[k] = total[k * rows : (k + 1) * rows, :]


def q_pieces(p_all, hi, lo, pieces):
    n, rank, width = p_all.shape
    cols = hi.shape[1]
    return pl.pallas_call(
        q_kernel,
        in_specs=[VMEM] * 3,
        out_specs=VMEM,
        out_shape=jax.ShapeDtypeStruct((pieces, rank // pieces, cols), F32),
        compiler_params=PARAMS,
        cost_estimate=cost(2 * hi.size * rank * 8, hi.size * 4),
        name="q_pieces",
    )(p_all, hi, lo)


def basis_kernel(p_ref, after_ref, inv_ref, basis_ref, stack_ref, full_ref):
    del after_ref
    n, rank, width = p_ref.shape
    for s in range(n):
        full_ref[:, s * width : (s + 1) * width] = p_ref[s]
    p = full_ref[...]
    gram = lax.dot_general(
        p,
        p,
        (((1,), (1,)), ((), ())),
        precision=lax.Precision.HIGHEST,
        preferred_element_type=F32,
    )
    row = lax.broadcasted_iota(jnp.int32, (rank, rank), 0)
    col = lax.broadcasted_iota(jnp.int32, (rank, rank), 1)
    eye = (row == col).astype(F32)
    work = jnp.concatenate([gram, eye], axis=1)
    below = lax.broadcasted_iota(jnp.int32, (rank, 1), 0)
    for j in range(rank - 1):
        pivot = work[j : j + 1, :]
        factor = jnp.where(below > j, work[:, j : j + 1] / pivot[:, j : j + 1], 0.0)
        work = work - factor * pivot
    upper = work[:, :rank]
    pivots = jnp.sum(jnp.where(row == col, upper, 0.0), axis=1, keepdims=True)
    inverse = work[:, rank:] / jnp.sqrt(pivots)
    inv_ref[...] = inverse
    basis = jnp.dot(
        inverse, p, precision=lax.Precision.HIGHEST, preferred_element_type=F32
    )
    basis_ref[...] = basis
    high = basis.astype(BF16).astype(F32)
    low = basis - high
    wide = jnp.concatenate([high, high, low, jnp.zeros_like(low)], axis=0)
    stack_ref[...] = wide.T.astype(BF16)


def basis_of(p_all, after):
    n, rank, width = p_all.shape
    size = n * width
    return pl.pallas_call(
        basis_kernel,
        in_specs=[VMEM, pl.BlockSpec(memory_space=pl.ANY)],
        out_specs=[VMEM] * 3,
        out_shape=[
            jax.ShapeDtypeStruct((rank, rank), F32),
            jax.ShapeDtypeStruct((rank, size), F32),
            jax.ShapeDtypeStruct((size, 4 * rank), BF16),
        ],
        scratch_shapes=[pltpu.VMEM((rank, size), F32)],
        compiler_params=PARAMS,
        cost_estimate=cost(4_000_000_000, 4_000_000),
        name="basis",
    )(p_all, after)


def residual_kernel(scale, q_ref, inv_ref, stack_ref, hi_ref, lo_ref, out_ref, factor_ref, raw, tall):
    @pl.when(pl.program_id(0) == 0)
    def _():
        pieces, rows, _ = q_ref.shape
        for k in range(pieces):
            raw[k * rows : (k + 1) * rows, :] = q_ref[k]
        factor = scale * jnp.dot(
            inv_ref[...],
            raw[...],
            precision=lax.Precision.HIGHEST,
            preferred_element_type=F32,
        )
        factor_ref[...] = factor
        high, low = parts_of(factor, 2)
        tall[...] = jnp.concatenate([high, low, high, jnp.zeros_like(low)], axis=0)

    merged = hi_ref[...].astype(F32) + lo_ref[...].astype(F32)
    out_ref[...] = (merged - dot(stack_ref[...], tall[...])).astype(BF16)


def residual_of(q_all, inverse, stack, hi, lo, replicas):
    rank = inverse.shape[0]
    height, cols = hi.shape
    block = 256
    part = pl.BlockSpec((block, cols), lambda i: (i, 0))
    whole = lambda shape: pl.BlockSpec(shape, lambda i: (0,) * len(shape))
    return pl.pallas_call(
        lambda *refs: residual_kernel(1.0 / replicas, *refs),
        grid=(height // block,),
        in_specs=[
            whole(q_all.shape),
            whole(inverse.shape),
            pl.BlockSpec((block, stack.shape[1]), lambda i: (i, 0)),
            part,
            part,
        ],
        out_specs=[part, whole((rank, cols))],
        out_shape=[
            jax.ShapeDtypeStruct((height, cols), BF16),
            jax.ShapeDtypeStruct((rank, cols), F32),
        ],
        scratch_shapes=[
            pltpu.VMEM((rank, cols), F32),
            pltpu.VMEM((4 * rank, cols), BF16),
        ],
        compiler_params=PARAMS,
        name="residual",
    )(q_all, inverse, stack, hi, lo)


def total_kernel(x_ref, out_ref):
    total = x_ref[0]
    for s in range(1, x_ref.shape[0]):
        total = total + x_ref[s]
    for s in range(out_ref.shape[0]):
        out_ref[s] = total


def total_for(x, n):
    return pl.pallas_call(
        total_kernel,
        in_specs=[VMEM],
        out_specs=VMEM,
        out_shape=jax.ShapeDtypeStruct((n,) + x.shape[1:], F32),
        compiler_params=PARAMS,
        cost_estimate=cost(x.size, 4 * x.size),
        name="total",
    )(x)


def per_device(acts, grads_out, error_buffer, prior_q):
    tensor = lax.axis_size("tensor")
    replicas = lax.axis_size("dp")
    side = math.isqrt(replicas)
    along_y = [[y * side + z for y in range(side)] for z in range(side)]
    along_z = [[y * side + z for z in range(side)] for y in range(side)]

    def over_tensor(x):
        return lax.all_to_all(x, "tensor", 0, 0)

    def over_y(x):
        return lax.all_to_all(x, "dp", 0, 0, axis_index_groups=along_y)

    def over_z(x):
        return lax.all_to_all(x, "dp", 0, 0, axis_index_groups=along_z)

    error = error_buffer[0]
    q_t = prior_q.T
    acts_all = lax.all_gather(acts, "tensor", axis=0, tiled=True)

    y_all = over_tensor(y_chunks(q_t, grads_out, tensor))
    p_terms = over_tensor(p_chunks(y_all, acts, error_term(q_t, error)))
    p_row = total_for(over_y(total_for(p_terms, side)), side)
    p_all = over_tensor(total_for(over_z(p_row), tensor))

    hi, lo = merged_parts(acts_all, grads_out, error, p_row)
    pieces = q_pieces(p_all, hi, lo, side)
    q_sum = total_for(over_z(total_for(over_y(pieces), side)), side)
    q_all = over_y(q_sum)
    inverse, basis, stack = basis_of(p_all, pieces)
    residual, factor = residual_of(q_all, inverse, stack, hi, lo, replicas)
    return (residual[None], basis.T, factor.T)


def solution(mesh):
    in_specs = (
        P(("dp", "tensor"), None),
        P("dp", "tensor"),
        P("dp", None, "tensor"),
        P("tensor", None),
    )
    out_specs = (P("dp", None, "tensor"), P(), P("tensor", None))
    return jax.shard_map(
        per_device, mesh=mesh, in_specs=in_specs, out_specs=out_specs, check_vma=False
    )
```

time: 490 us -> 126 us (0.26)
  waiting for transfers between devices: 450 us -> 8.72 us
  blocking collectives: 0 us -> 62.5 us
  starting transfers between devices: 0.12 us -> 17.4 us
  matrix products: 17.2 us -> 0 us
  Pallas kernels: 0 us -> 16.5 us
  other arithmetic: 7.54 us -> 0 us
    psum x2 -> x0, waiting for transfers between devices: 406 us -> none  [the longest x1 261 us: sum_left(): return lax.psum(partial_value, ('dp', 'tensor'))]
    all_to_all x0 -> x5, blocking collectives: none -> 62.5 us  [the longest x2 30.2 us: over_z(): return lax.all_to_all(x, 'dp', 0, 0, axis_index_groups=along_z)]
    all_gather x1, waiting for transfers between devices: 43.3 us -> 0.01 us  [per_device(): acts_all = lax.all_gather(acts, 'tensor', axis=0, tiled=True)]
    all_to_all x0 -> x3, starting transfers between devices: none -> 17.3 us  [the longest x2 14 us: over_tensor(): return lax.all_to_all(x, 'tensor', 0, 0)]
    pallas_call x0 -> x12, Pallas kernels: none -> 16.5 us  [the longest x1 4.14 us: y_chunks(): pl.pallas_call(y_kernel, in_specs=[hbm, hbm], out_specs=VMEM, out_shape=j...]
    dot_general x5 -> x0, matrix products: 15.9 us -> none  [the longest x1 4.84 us: per_device(): lax.dot_general(lax.all_gather(acts, 'tensor', axis=0, tiled=True), grads...]
    all_to_all x0 -> x3, waiting for transfers between devices: none -> 8.04 us  [the longest x1 4.31 us: over_y(): return lax.all_to_all(x, 'dp', 0, 0, axis_index_groups=along_y)]
    another operation x5 -> x0, other arithmetic: 6.68 us -> none  [the longest x3 3.6 us: per_device(): chol = jnp.linalg.cholesky(gram)]
  transfers between devices with their start and end apart: 3 -> 4, of which waited for: 3 -> 2; matrix products, arithmetic and copies ran while one was open for 0% -> 0% of each run, Pallas kernels for 0% -> 10%
where the time goes in v1:
time: 126 us; the launch traced here: 125 us
  blocking collectives  62.5 us (50%)
  starting transfers between devices  17.4 us (14%)
  Pallas kernels  16.5 us (13%)
  between operations  14.1 us (11%)
  waiting for transfers between devices  8.72 us (7%)
  local copies, waits for them, and re-layouts  5.77 us (5%)
    all_to_all x2, blocking collectives, over_z(): return lax.all_to_all(x, 'dp', 0, 0, axis_index_groups=along_z)  30.2 us
    all_to_all x2, blocking collectives, over_y(): return lax.all_to_all(x, 'dp', 0, 0, axis_index_groups=along_y)  22.2 us
    all_to_all x2, starting transfers between devices, over_tensor(): return lax.all_to_all(x, 'tensor', 0, 0)  14 us
    all_to_all x1, blocking collectives, over_tensor(): return lax.all_to_all(x, 'tensor', 0, 0)  10.1 us
    unnamed x12, local copies, waits for them, and re-layouts  5.77 us
    all_to_all x1, waiting for transfers between devices, over_y(): return lax.all_to_all(x, 'dp', 0, 0, axis_index_groups=along_y)  4.31 us
    pallas_call x1, Pallas kernels, y_chunks(): pl.pallas_call(y_kernel, in_specs=[hbm, hbm], out_specs=VMEM, out_shape=j...  4.14 us
    pallas_call x1, Pallas kernels, basis_of(): pl.pallas_call(basis_kernel, in_specs=[VMEM, pl.BlockSpec(memory_space=pl...  3.99 us
  transfers between devices with their start and end apart: 4, of which 2 were waited for; matrix products, arithmetic and copies ran while one was open for 0% of the time, Pallas kernels for 10%

profile of v1, /device:TPU:2, one launch (start us, length us, event | category | flops | bytes accessed | tf_op | source)
XLA Modules:
  0.0 124.9 jit_solution(14881710576059937007)
XLA Ops:
  7.2 0.0 copy-start.1
  7.2 0.0 copy-start.3
  7.2 0.0 all-gather.2.cloned.1.call-start
  7.2 0.7 all-gather.2.cloned.1.call-update
  7.9 4.1 %y_chunks.1 = f32[8,32,256]{2,1,0:T(8,128)} custom-call(bf16[32,512]{1,0:T(8,128)(2,1)} %bitcast.7, bf16[2048,512]{1,0:T(8,128)(2,1)} %g_ref.3), custom_call_target="tpu_custom_call" | custom-call | flops 536870912 | bytes 2097152 | tf_op jit(solution)/shard_map/y_chunks/pallas_call | solution.py:60
  12.1 9.2 %all-to-all-start = ((f32[8,32,256]{2,1,0:T(8,128)}), f32[8,32,256]{2,1,0:T(8,128)S(1)}, u32[]{:S(2)}, u32[]{:S(2)}) async-start(f32[8,32,256]{2,1,0:T(8,128)} %y_chunks.1), calls=%async_computation | async-start | bytes 524288 | tf_op jit(solution)/shard_map/all_to_all | solution.py:311
  21.3 0.0 copy-start.2
  21.3 1.2 copy-done.2
  22.5 0.0 copy-start.4
  22.5 0.8 copy-done.4
  23.3 0.4 error_term.1.e_ref
  23.7 3.7 %all-to-all-done.y_ref = f32[8,32,256]{2,1,0:T(8,128)S(1)} async-done(((f32[8,32,256]{2,1,0:T(8,128)}), f32[8,32,256]{2,1,0:T(8,128)S(1)}, u32[]{:S(2)}, u32[]{:S(2)}) %all-to-all-start) | async-done | bytes 262176 | tf_op jit(solution)/shard_map/all_to_all | solution.py:311
  27.4 0.0 copy-done.1
  27.4 0.2 p_chunks.1
  27.6 10.1 %all_to_all.40.x_ref = f32[8,32,128]{2,1,0:T(8,128)S(1)} all-to-all(f32[8,32,128]{2,1,0:T(8,128)S(1)} %p_chunks.1), channel_id=1, replica_groups=mesh['dp'=64,'tensor'=8] {'tensor'}, dimensions={0} | all-to-all | bytes 262144 | tf_op jit(solution)/shard_map/all_to_all | solution.py:311
  37.7 11.5 %all_to_all.41.x_ref = f32[8,32,128]{2,1,0:T(8,128)S(1)} all-to-all(f32[8,32,128]{2,1,0:T(8,128)S(1)} %total.5), channel_id=1, replica_groups={{0,64,128,192,256,320,384,448},{8,72,136,200,264,328,392,456},{16,80,14..., dimensions={0} | all-to-all | bytes 262144 | tf_op jit(solution)/shard_map/all_to_all | solution.py:314
  49.2 19.4 %all_to_all.42.x_ref = f32[8,32,128]{2,1,0:T(8,128)S(1)} all-to-all(f32[8,32,128]{2,1,0:T(8,128)S(1)} %total.6.after_ref), channel_id=1, replica_groups={{0,8,16,24,32,40,48,56},{64,72,80,88,96,104,112,120},{128,136,144,152,1..., dimensions={0} | all-to-all | bytes 262144 | tf_op jit(solution)/shard_map/all_to_all | solution.py:317
  68.7 0.7 total.7
  69.4 4.7 %all-to-all-start.4 = ((f32[8,32,128]{2,1,0:T(8,128)}), f32[8,32,128]{2,1,0:T(8,128)S(1)}, u32[]{:S(2)}, u32[]{:S(2)}) async-start(f32[8,32,128]{2,1,0:T(8,128)} %total.7), calls=%async_computation.4 | async-start | bytes 262144 | tf_op jit(solution)/shard_map/all_to_all | solution.py:311
  74.1 0.0 all-gather.2.cloned.1.call-done.a_ref
  74.1 0.0 copy-done.3
  74.1 0.0 copy-start
  74.1 1.6 %copy-done = bf16[2048,512]{1,0:T(8,128)(2,1)S(1)} copy-done((bf16[2048,512]{1,0:T(8,128)(2,1)S(1)}, bf16[2048,512]{1,0:T(8,128)(2,1)}, u32[]{:S(2)}) %copy-start) | copy-done | bytes 2097176
  75.7 0.0 copy-start.5
  75.7 2.2 %copy-done.5 = bf16[2048,1024]{1,0:T(8,128)(2,1)S(1)} copy-done((bf16[2048,1024]{1,0:T(8,128)(2,1)S(1)}, bf16[2048,1024]{1,0:T(8,128)(2,1)}, u32[]{:S(2)}) %copy-start.5) | copy-done | bytes 4194328
  77.9 3.7 %merged_parts.1 = (bf16[1024,512]{1,0:T(8,128)(2,1)S(1)}, bf16[1024,512]{1,0:T(8,128)(2,1)S(1)}) custom-call(bf16[2048,1024]{1,0:T(8,128)(2,1)S(1)} %copy-done.5, bf16[2048,512]{1,0:T(8,128)(2,1)S(1)} %copy-done, bf16[1024,512]{1,0:T(8,128)(2,1)S(1)} %bitcast.6, f32[8,32,128]{2,1,0:T(8,128)S(1)} %total.6.after_ref), custom_call_target="tpu_custom_call" | custom-call | flops 2147483648 | bytes 6291456 | tf_op jit(solution)/shard_map/merged_parts/pallas_call | solution.py:133
  81.6 0.0 all-to-all-done.4.p_ref
  81.6 0.4 q_pieces.1.after_ref
  82.0 10.8 %all_to_all.43.x_ref = f32[8,4,512]{2,1,0:T(4,128)S(1)} all-to-all(f32[8,4,512]{2,1,0:T(4,128)S(1)} %q_pieces.1.after_ref), channel_id=1, replica_groups={{0,64,128,192,256,320,384,448},{8,72,136,200,264,328,392,456},{16,80,14..., dimensions={0} | all-to-all | bytes 131072 | tf_op jit(solution)/shard_map/all_to_all | solution.py:314
  92.8 10.8 %all_to_all.44.x_ref = f32[8,4,512]{2,1,0:T(4,128)S(1)} all-to-all(f32[8,4,512]{2,1,0:T(4,128)S(1)} %total.8), channel_id=1, replica_groups={{0,8,16,24,32,40,48,56},{64,72,80,88,96,104,112,120},{128,136,144,152,1..., dimensions={0} | all-to-all | bytes 131072 | tf_op jit(solution)/shard_map/all_to_all | solution.py:317
  103.5 0.6 total.9
  104.2 3.4 %all-to-all-start.7 = ((f32[8,4,512]{2,1,0:T(4,128)}), f32[8,4,512]{2,1,0:T(4,128)S(1)}, u32[]{:S(2)}, u32[]{:S(2)}) async-start(f32[8,4,512]{2,1,0:T(4,128)} %total.9), calls=%async_computation.7 | async-start | bytes 131072 | tf_op jit(solution)/shard_map/all_to_all | solution.py:314
  107.5 4.0 %basis.1 = (f32[32,32]{1,0:T(8,128)S(1)}, f32[32,1024]{1,0:T(8,128)}, bf16[1024,128]{1,0:T(8,128)(2,1)S(1)}) custom-call(f32[8,32,128]{2,1,0:T(8,128)S(1)} %all-to-all-done.4.p_ref, f32[8,4,512]{2,1,0:T(4,128)S(1)} %q_pieces.1.after_ref), custom_call_target="tpu_custom_call" | custom-call | flops 4000000000 | bytes 4000000 | tf_op jit(solution)/shard_map/basis/pallas_call | solution.py:217
  111.5 4.3 %all-to-all-done.7.refs_0_ = f32[8,4,512]{2,1,0:T(4,128)S(1)} async-done(((f32[8,4,512]{2,1,0:T(4,128)}), f32[8,4,512]{2,1,0:T(4,128)S(1)}, u32[]{:S(2)}, u32[]{:S(2)}) %all-to-all-start.7) | async-done | bytes 65568 | tf_op jit(solution)/shard_map/all_to_all | solution.py:314
  115.8 2.3 %residual.1 = (bf16[1024,512]{1,0:T(8,128)(2,1)}, f32[32,512]{1,0:T(8,128)}) custom-call(f32[8,4,512]{2,1,0:T(4,128)S(1)} %all-to-all-done.7.refs_0_, f32[32,32]{1,0:T(8,128)S(1)} %get-tuple-element.12.refs_1_, bf16[1024,128]{1,0:T(8,128)(2,1)S(1)} %get-tuple-element.13.refs_2_, bf16[1024,512]{1,0:T(8,128)(2,1)S(1)} %get-tuple-element.10.hi_ref.refs_3_, ...), custom_call_target="tpu_custom_call" | custom-call | tf_op jit(solution)/shard_map/residual/pallas_call | solution.py:259
  (3 shorter events, 0.0 us)
Async XLA Ops:
  7.2 20.3 %copy-start.1 = (bf16[256,1024]{1,0:T(8,128)(2,1)S(1)}, bf16[256,1024]{1,0:T(8,128)(2,1)}, u32[]{:S(2)}) copy-start(bf16[256,1024]{1,0:T(8,128)(2,1)} %acts_ref.1) | copy-start | bytes 1572868
  7.2 66.9 %copy-start.3 = (bf16[1,1024,512]{2,1,0:T(8,128)(2,1)S(1)}, bf16[1,1024,512]{2,1,0:T(8,128)(2,1)}, u32[]{:S(2)}) copy-start(bf16[1,1024,512]{2,1,0:T(8,128)(2,1)} %param.6) | copy-start | bytes 3145732
  7.2 66.9 %all-gather.2.cloned.1.call-start = ((), (), s32[]{:S(2)}) async-start(), calls=%async_computation.8 | async-start | bytes 4718592 | tf_op jit(solution)/shard_map/all_gather | solution.py:321
  12.1 15.3 %all-to-all-start = ((f32[8,32,256]{2,1,0:T(8,128)}), f32[8,32,256]{2,1,0:T(8,128)S(1)}, u32[]{:S(2)}, u32[]{:S(2)}) async-start(f32[8,32,256]{2,1,0:T(8,128)} %y_chunks.1), calls=%async_computation | async-start | bytes 524288 | tf_op jit(solution)/shard_map/all_to_all | solution.py:311
  21.3 1.2 copy-start.2
  22.5 0.8 copy-start.4
  69.4 12.2 %all-to-all-start.4 = ((f32[8,32,128]{2,1,0:T(8,128)}), f32[8,32,128]{2,1,0:T(8,128)S(1)}, u32[]{:S(2)}, u32[]{:S(2)}) async-start(f32[8,32,128]{2,1,0:T(8,128)} %total.7), calls=%async_computation.4 | async-start | bytes 262144 | tf_op jit(solution)/shard_map/all_to_all | solution.py:311
  74.1 1.6 %copy-start = (bf16[2048,512]{1,0:T(8,128)(2,1)S(1)}, bf16[2048,512]{1,0:T(8,128)(2,1)}, u32[]{:S(2)}) copy-start(bf16[2048,512]{1,0:T(8,128)(2,1)} %g_ref.3) | copy-start | bytes 6291460
  75.7 2.2 %copy-start.5 = (bf16[2048,1024]{1,0:T(8,128)(2,1)S(1)}, bf16[2048,1024]{1,0:T(8,128)(2,1)}, u32[]{:S(2)}) copy-start(bf16[2048,1024]{1,0:T(8,128)(2,1)} %all-gather.2.cloned.1.call-done.a_ref) | copy-start | bytes 12582916
  104.2 11.7 %all-to-all-start.7 = ((f32[8,4,512]{2,1,0:T(4,128)}), f32[8,4,512]{2,1,0:T(4,128)S(1)}, u32[]{:S(2)}, u32[]{:S(2)}) async-start(f32[8,4,512]{2,1,0:T(4,128)} %total.9), calls=%async_computation.7 | async-start | bytes 131072 | tf_op jit(solution)/shard_map/all_to_all | solution.py:314
Sparse Core Ops, SparseCore 0:
  10.2 42.5 all-gather.1

commit v2 on v1

--- a/solution.py
+++ b/solution.py
@@ -9,6 +9,7 @@
 
 F32 = jnp.float32
 BF16 = jnp.bfloat16
+LANES = 128
 VMEM = pl.BlockSpec(memory_space=pltpu.VMEM)
 PARAMS = pltpu.CompilerParams(vmem_limit_bytes=32 * 1024 * 1024)
 STREAM = pltpu.CompilerParams(vmem_limit_bytes=60 * 1024 * 1024)
@@ -90,29 +91,44 @@
     )(q_t, error)
 
 
+def write_pieces(out_ref, x):
+    pieces, rows, _ = out_ref.shape
+    across = x.shape[1] // LANES
+    for k in range(pieces):
+        r, c = k // across, k % across
+        out_ref[k] = x[r * rows : (r + 1) * rows, c * LANES : (c + 1) * LANES]
+
+
+def read_pieces(in_ref, full_ref):
+    pieces, rows, _ = in_ref.shape
+    across = full_ref.shape[1] // LANES
+    for k in range(pieces):
+        r, c = k // across, k % across
+        full_ref[r * rows : (r + 1) * rows, c * LANES : (c + 1) * LANES] = in_ref[k]
+
+
 def p_kernel(y_ref, acts_ref, e_ref, out_ref):
-    n, rank, width = out_ref.shape
+    n, rank, _ = y_ref.shape
     y = y_ref[0]
     for s in range(1, n):
         y = y + y_ref[s]
     stack = jnp.concatenate(parts_of(y, 3), axis=0)
     p = dot(stack, acts_ref[...])
-    p = (p[:rank] + e_ref[...]) + (p[rank : 2 * rank] + p[2 * rank :])
-    for s in range(n):
-        out_ref[s] = p[:, s * width : (s + 1) * width]
-
-
-def p_chunks(y_all, acts, e_term):
-    n, rank, _ = y_all.shape
-    width = acts.shape[1] // n
+    write_pieces(
+        out_ref, (p[:rank] + e_ref[...]) + (p[rank : 2 * rank] + p[2 * rank :])
+    )
+
+
+def p_pieces(y_all, acts, e_term, pieces):
+    rows = e_term.size // (pieces * LANES)
     return pl.pallas_call(
         p_kernel,
         in_specs=[VMEM] * 3,
         out_specs=VMEM,
-        out_shape=jax.ShapeDtypeStruct((n, rank, width), F32),
-        compiler_params=PARAMS,
-        cost_estimate=cost(2 * acts.size * rank * 8, acts.size * 2),
-        name="p_chunks",
+        out_shape=jax.ShapeDtypeStruct((pieces, rows, LANES), F32),
+        compiler_params=PARAMS,
+        cost_estimate=cost(2 * acts.size * 256, acts.size * 2),
+        name="p_pieces",
     )(y_all, acts, e_term)
 
 
@@ -147,28 +163,24 @@
     )(acts_all, grads, error, after)
 
 
-def q_kernel(p_ref, hi_ref, lo_ref, out_ref):
-    n, rank, width = p_ref.shape
-    pieces, rows, _ = out_ref.shape
-    total = None
-    for s in range(n):
-        high, low = parts_of(p_ref[s], 2)
-        span = slice(s * width, (s + 1) * width)
-        both = dot(jnp.concatenate([high, low], axis=0), hi_ref[span, :])
-        term = both[:rank] + (both[rank:] + dot(high, lo_ref[span, :]))
-        total = term if total is None else total + term
-    for k in range(pieces):
-        out_ref[k] = total[k * rows : (k + 1) * rows, :]
+def q_kernel(p_ref, hi_ref, lo_ref, out_ref, full_ref):
+    read_pieces(p_ref, full_ref)
+    rank = full_ref.shape[0]
+    high, low = parts_of(full_ref[...], 2)
+    both = dot(jnp.concatenate([high, low], axis=0), hi_ref[...])
+    write_pieces(out_ref, both[:rank] + (both[rank:] + dot(high, lo_ref[...])))
 
 
 def q_pieces(p_all, hi, lo, pieces):
-    n, rank, width = p_all.shape
-    cols = hi.shape[1]
+    height, cols = hi.shape
+    rank = p_all.size // height
+    rows = rank * cols // (pieces * LANES)
     return pl.pallas_call(
         q_kernel,
         in_specs=[VMEM] * 3,
         out_specs=VMEM,
-        out_shape=jax.ShapeDtypeStruct((pieces, rank // pieces, cols), F32),
+        out_shape=jax.ShapeDtypeStruct((pieces, rows, LANES), F32),
+        scratch_shapes=[pltpu.VMEM((rank, height), F32)],
         compiler_params=PARAMS,
         cost_estimate=cost(2 * hi.size * rank * 8, hi.size * 4),
         name="q_pieces",
@@ -177,10 +189,9 @@
 
 def basis_kernel(p_ref, after_ref, inv_ref, basis_ref, stack_ref, full_ref):
     del after_ref
-    n, rank, width = p_ref.shape
-    for s in range(n):
-        full_ref[:, s * width : (s + 1) * width] = p_ref[s]
+    read_pieces(p_ref, full_ref)
     p = full_ref[...]
+    rank = p.shape[0]
     gram = lax.dot_general(
         p,
         p,
@@ -211,9 +222,8 @@
     stack_ref[...] = wide.T.astype(BF16)
 
 
-def basis_of(p_all, after):
-    n, rank, width = p_all.shape
-    size = n * width
+def basis_of(p_all, after, rank):
+    size = p_all.size // rank
     return pl.pallas_call(
         basis_kernel,
         in_specs=[VMEM, pl.BlockSpec(memory_space=pl.ANY)],
@@ -233,9 +243,7 @@
 def residual_kernel(scale, q_ref, inv_ref, stack_ref, hi_ref, lo_ref, out_ref, factor_ref, raw, tall):
     @pl.when(pl.program_id(0) == 0)
     def _():
-        pieces, rows, _ = q_ref.shape
-        for k in range(pieces):
-            raw[k * rows : (k + 1) * rows, :] = q_ref[k]
+        read_pieces(q_ref, raw)
         factor = scale * jnp.dot(
             inv_ref[...],
             raw[...],
@@ -284,52 +292,73 @@
     total = x_ref[0]
     for s in range(1, x_ref.shape[0]):
         total = total + x_ref[s]
-    for s in range(out_ref.shape[0]):
-        out_ref[s] = total
-
-
-def total_for(x, n):
+    out_ref[...] = total
+
+
+def total_of(x):
     return pl.pallas_call(
         total_kernel,
         in_specs=[VMEM],
         out_specs=VMEM,
-        out_shape=jax.ShapeDtypeStruct((n,) + x.shape[1:], F32),
+        out_shape=jax.ShapeDtypeStruct(x.shape[1:], F32),
         compiler_params=PARAMS,
         cost_estimate=cost(x.size, 4 * x.size),
         name="total",
     )(x)
+
+
+def exchange(x, axis, groups):
+    return lax.all_to_all(x, axis, 0, 0, axis_index_groups=groups)
+
+
+def to_all(x, axis, groups):
+    n = len(groups[0])
+    return exchange(jnp.broadcast_to(x[None], (n,) + x.shape), axis, groups)
+
+
+def add_partner(x, distance):
+    pairs = [(i, i ^ distance) for i in range(lax.axis_size("dp"))]
+    return x + lax.ppermute(x, "dp", pairs)
 
 
 def per_device(acts, grads_out, error_buffer, prior_q):
     tensor = lax.axis_size("tensor")
     replicas = lax.axis_size("dp")
     side = math.isqrt(replicas)
+    half = side // 2
     along_y = [[y * side + z for y in range(side)] for z in range(side)]
-    along_z = [[y * side + z for z in range(side)] for y in range(side)]
-
-    def over_tensor(x):
-        return lax.all_to_all(x, "tensor", 0, 0)
-
-    def over_y(x):
-        return lax.all_to_all(x, "dp", 0, 0, axis_index_groups=along_y)
-
-    def over_z(x):
-        return lax.all_to_all(x, "dp", 0, 0, axis_index_groups=along_z)
+    for_p = [
+        [(y * side + h * half + z) * tensor + t for h in range(2) for t in range(tensor)]
+        for y in range(side)
+        for z in range(half)
+    ]
+    for_q = [
+        [y * side + 2 * h + z for y in range(side) for h in range(half)]
+        for z in range(2)
+    ]
+    both = ("dp", "tensor")
 
     error = error_buffer[0]
     q_t = prior_q.T
+    rank = q_t.shape[0]
     acts_all = lax.all_gather(acts, "tensor", axis=0, tiled=True)
 
-    y_all = over_tensor(y_chunks(q_t, grads_out, tensor))
-    p_terms = over_tensor(p_chunks(y_all, acts, error_term(q_t, error)))
-    p_row = total_for(over_y(total_for(p_terms, side)), side)
-    p_all = over_tensor(total_for(over_z(p_row), tensor))
-
-    hi, lo = merged_parts(acts_all, grads_out, error, p_row)
-    pieces = q_pieces(p_all, hi, lo, side)
-    q_sum = total_for(over_z(total_for(over_y(pieces), side)), side)
-    q_all = over_y(q_sum)
-    inverse, basis, stack = basis_of(p_all, pieces)
+    y_all = lax.all_to_all(y_chunks(q_t, grads_out, tensor), "tensor", 0, 0)
+    p_mine = p_pieces(y_all, acts, error_term(q_t, error), 2 * tensor)
+    p_mine = total_of(exchange(p_mine, both, for_p))
+    p_mine = lax.psum(p_mine, "dp", axis_index_groups=along_y)
+    after = p_mine
+    distance = 1
+    while distance < half:
+        p_mine = add_partner(p_mine, distance)
+        distance *= 2
+    p_all = to_all(p_mine, both, for_p)
+
+    hi, lo = merged_parts(acts_all, grads_out, error, after)
+    pieces = q_pieces(p_all, hi, lo, side * half)
+    q_mine = add_partner(total_of(exchange(pieces, "dp", for_q)), 1)
+    q_all = to_all(q_mine, "dp", for_q)
+    inverse, basis, stack = basis_of(p_all, q_mine, rank)
     residual, factor = residual_of(q_all, inverse, stack, hi, lo, replicas)
     return (residual[None], basis.T, factor.T)
 

time: 126 us -> 143 us (1.13)
  waiting for transfers between devices: 8.72 us -> 21.3 us
  starting transfers between devices: 17.4 us -> 29.4 us
  blocking collectives: 62.5 us -> 55.1 us
    all_to_all x5 -> x2, blocking collectives: 62.5 us -> 37.3 us  [exchange(): return lax.all_to_all(x, axis, 0, 0, axis_index_groups=groups)]
    psum x0 -> x1, blocking collectives: none -> 17.9 us  [per_device(): p_mine = lax.psum(p_mine, 'dp', axis_index_groups=along_y)]
    ppermute x0 -> x3, starting transfers between devices: none -> 11.3 us  [add_partner(): return x + lax.ppermute(x, 'dp', pairs)]
    ppermute x0 -> x3, waiting for transfers between devices: none -> 7.18 us  [add_partner(): return x + lax.ppermute(x, 'dp', pairs)]
    all_to_all x3, waiting for transfers between devices: 8.04 us -> 13.4 us  [the longest x2 9.65 us: exchange(): return lax.all_to_all(x, axis, 0, 0, axis_index_groups=groups)]
  transfers between devices with their start and end apart: 4 -> 7, of which waited for: 2 -> 6; matrix products, arithmetic and copies ran while one was open for 0% -> 0% of each run, Pallas kernels for 10% -> 9%
where the time goes in v2:
time: 143 us; the launch traced here: 142 us
  blocking collectives  55.1 us (39%)
  starting transfers between devices  29.4 us (21%)
  waiting for transfers between devices  21.3 us (15%)
  Pallas kernels  15.2 us (11%)
  between operations  14.1 us (10%)
  local copies, waits for them, and re-layouts  7.07 us (5%)
    all_to_all x2, blocking collectives, exchange(): return lax.all_to_all(x, axis, 0, 0, axis_index_groups=groups)  37.3 us
    psum x1, blocking collectives, per_device(): p_mine = lax.psum(p_mine, 'dp', axis_index_groups=along_y)  17.9 us
    ppermute x3, starting transfers between devices, add_partner(): return x + lax.ppermute(x, 'dp', pairs)  11.3 us
    all_to_all x2, waiting for transfers between devices, exchange(): return lax.all_to_all(x, axis, 0, 0, axis_index_groups=groups)  9.65 us
    all_to_all x1, starting transfers between devices, per_device(): y_all = lax.all_to_all(y_chunks(q_t, grads_out, tensor), 'tensor', 0, 0)  9.24 us
    all_to_all x2, starting transfers between devices, exchange(): return lax.all_to_all(x, axis, 0, 0, axis_index_groups=groups)  8.88 us
    ppermute x3, waiting for transfers between devices, add_partner(): return x + lax.ppermute(x, 'dp', pairs)  7.18 us
    unnamed x12, local copies, waits for them, and re-layouts  5.77 us
  transfers between devices with their start and end apart: 7, of which 6 were waited for; matrix products, arithmetic and copies ran while one was open for 0% of the time, Pallas kernels for 9%

profile of v2, /device:TPU:2, one launch (start us, length us, event | category | flops | bytes accessed | tf_op | source)
XLA Modules:
  0.0 142.2 jit_solution(10901502715580750972)
XLA Ops:
  7.2 0.0 copy-start.1
  7.2 0.0 copy-start.3
  7.2 0.0 all-gather.2.cloned.1.call-start
  7.2 0.7 all-gather.2.cloned.1.call-update
  7.9 4.1 %y_chunks.1 = f32[8,32,256]{2,1,0:T(8,128)} custom-call(bf16[32,512]{1,0:T(8,128)(2,1)} %bitcast.7, bf16[2048,512]{1,0:T(8,128)(2,1)} %g_ref.3), custom_call_target="tpu_custom_call" | custom-call | flops 536870912 | bytes 2097152 | tf_op jit(solution)/shard_map/y_chunks/pallas_call | solution.py:61
  12.1 9.2 %all-to-all-start = ((f32[8,32,256]{2,1,0:T(8,128)}), f32[8,32,256]{2,1,0:T(8,128)S(1)}, u32[]{:S(2)}, u32[]{:S(2)}) async-start(f32[8,32,256]{2,1,0:T(8,128)} %y_chunks.1), calls=%async_computation | async-start | bytes 524288 | tf_op jit(solution)/shard_map/all_to_all | solution.py:346
  21.3 0.0 copy-start.2
  21.3 1.2 copy-done.2
  22.5 0.0 copy-start.4
  22.5 0.8 copy-done.4
  23.3 0.4 error_term.1.e_ref
  23.7 3.7 %all-to-all-done.y_ref = f32[8,32,256]{2,1,0:T(8,128)S(1)} async-done(((f32[8,32,256]{2,1,0:T(8,128)}), f32[8,32,256]{2,1,0:T(8,128)S(1)}, u32[]{:S(2)}, u32[]{:S(2)}) %all-to-all-start) | async-done | bytes 262176 | tf_op jit(solution)/shard_map/all_to_all | solution.py:346
  27.4 0.0 copy-done.1
  27.4 0.2 p_pieces.1
  27.6 16.5 %all_to_all.25.x_ref = f32[16,16,128]{2,1,0:T(8,128)S(1)} all-to-all(f32[16,16,128]{2,1,0:T(8,128)S(1)} %p_pieces.1), channel_id=1, replica_groups={{0,1,2,3,4,5,6,7,32,33,34,35,36,37,38,39},{8,9,10,11,12,13,14,15,40,41,..., dimensions={0} | all-to-all | bytes 262144 | tf_op jit(solution)/shard_map/all_to_all | solution.py:311
  44.1 17.9 %psum.7.after_ref = f32[16,128]{1,0:T(8,128)S(1)} all-reduce(f32[16,128]{1,0:T(8,128)S(1)} %total.2), channel_id=1, replica_groups={{0,64,128,192,256,320,384,448},{8,72,136,200,264,328,392,456},{16,80,14..., use_global_device_ids=true, to_apply=%region_0.0 | all-reduce | flops 2048 | bytes 16384 | tf_op jit(solution)/shard_map/psum | solution.py:349
  62.0 3.4 %collective-permute-start = (f32[16,128]{1,0:T(8,128)S(1)}, f32[16,128]{1,0:T(8,128)S(1)}, u32[]{:S(2)}, u32[]{:S(2)}) collective-permute-start(f32[16,128]{1,0:T(8,128)S(1)} %psum.7.after_ref), channel_id=1, source_target_pairs={{0,8},{8,0},{16,24},{24,16},{32,40},{40,32},{48,56},{56,48},{64,72... | collective-permute-start | bytes 24584 | tf_op jit(solution)/shard_map/ppermute | solution.py:321
  65.5 2.1 %collective-permute-done = f32[16,128]{1,0:T(8,128)S(1)} collective-permute-done((f32[16,128]{1,0:T(8,128)S(1)}, f32[16,128]{1,0:T(8,128)S(1)}, u32[]{:S(2)}, u32[]{:S(2)}) %collective-permute-start) | collective-permute-done | bytes 8224 | tf_op jit(solution)/shard_map/ppermute | solution.py:321
  67.6 5.8 %collective-permute-start.1 = (f32[16,128]{1,0:T(8,128)S(1)}, f32[16,128]{1,0:T(8,128)S(1)}, u32[]{:S(2)}, u32[]{:S(2)}) collective-permute-start(f32[16,128]{1,0:T(8,128)S(1)} %add.11), channel_id=1, source_target_pairs={{0,16},{8,24},{16,0},{24,8},{32,48},{40,56},{48,32},{56,40},{64,80... | collective-permute-start | bytes 24584 | tf_op jit(solution)/shard_map/ppermute | solution.py:321
  73.4 1.6 %collective-permute-done.1 = f32[16,128]{1,0:T(8,128)S(1)} collective-permute-done((f32[16,128]{1,0:T(8,128)S(1)}, f32[16,128]{1,0:T(8,128)S(1)}, u32[]{:S(2)}, u32[]{:S(2)}) %collective-permute-start.1) | collective-permute-done | bytes 8224 | tf_op jit(solution)/shard_map/ppermute | solution.py:321
  75.1 0.7 broadcast_in_dim.6
  75.7 5.0 %all-to-all-start.2 = ((f32[16,16,128]{2,1,0:T(8,128)}), f32[16,16,128]{2,1,0:T(8,128)S(1)}, u32[]{:S(2)}, u32[]{:S(2)}) async-start(f32[16,16,128]{2,1,0:T(8,128)} %broadcast_in_dim.6), calls=%async_computation.2 | async-start | bytes 262144 | tf_op jit(solution)/shard_map/all_to_all | solution.py:311
  80.7 0.0 all-gather.2.cloned.1.call-done.a_ref
  80.8 0.0 copy-done.3
  80.8 0.0 copy-start
  80.8 1.6 %copy-done = bf16[2048,512]{1,0:T(8,128)(2,1)S(1)} copy-done((bf16[2048,512]{1,0:T(8,128)(2,1)S(1)}, bf16[2048,512]{1,0:T(8,128)(2,1)}, u32[]{:S(2)}) %copy-start) | copy-done | bytes 2097176
  82.4 0.0 copy-start.5
  82.4 2.2 %copy-done.5 = bf16[2048,1024]{1,0:T(8,128)(2,1)S(1)} copy-done((bf16[2048,1024]{1,0:T(8,128)(2,1)S(1)}, bf16[2048,1024]{1,0:T(8,128)(2,1)}, u32[]{:S(2)}) %copy-start.5) | copy-done | bytes 4194328
  84.6 3.7 %merged_parts.1 = (bf16[1024,512]{1,0:T(8,128)(2,1)S(1)}, bf16[1024,512]{1,0:T(8,128)(2,1)S(1)}) custom-call(bf16[2048,1024]{1,0:T(8,128)(2,1)S(1)} %copy-done.5, bf16[2048,512]{1,0:T(8,128)(2,1)S(1)} %copy-done, bf16[1024,512]{1,0:T(8,128)(2,1)S(1)} %bitcast.6, f32[16,128]{1,0:T(8,128)S(1)} %psum.7.after_ref), custom_call_target="tpu_custom_call" | custom-call | flops 2147483648 | bytes 6291456 | tf_op jit(solution)/shard_map/merged_parts/pallas_call | solution.py:149
  88.3 1.4 %all-to-all-done.2.p_ref = f32[16,16,128]{2,1,0:T(8,128)S(1)} async-done(((f32[16,16,128]{2,1,0:T(8,128)}), f32[16,16,128]{2,1,0:T(8,128)S(1)}, u32[]{:S(2)}, u32[]{:S(2)}) %all-to-all-start.2) | async-done | bytes 131104 | tf_op jit(solution)/shard_map/all_to_all | solution.py:311
  89.7 0.5 q_pieces.1
  90.1 20.8 %all_to_all.26.x_ref = f32[32,4,128]{2,1,0:T(4,128)S(1)} all-to-all(f32[32,4,128]{2,1,0:T(4,128)S(1)} %q_pieces.1), channel_id=1, replica_groups={{0,16,32,48,64,80,96,112,128,144,160,176,192,208,224,240,256,272,288,30..., dimensions={0} | all-to-all | bytes 131072 | tf_op jit(solution)/shard_map/all_to_all | solution.py:311
  110.9 2.0 %collective-permute-start.2 = (f32[4,128]{1,0:T(4,128)S(1)}, f32[4,128]{1,0:T(4,128)S(1)}, u32[]{:S(2)}, u32[]{:S(2)}) collective-permute-start(f32[4,128]{1,0:T(4,128)S(1)} %total.3), channel_id=1, source_target_pairs={{0,8},{8,0},{16,24},{24,16},{32,40},{40,32},{48,56},{56,48},{64,72... | collective-permute-start | bytes 6152 | tf_op jit(solution)/shard_map/ppermute | solution.py:321
  113.0 3.4 %collective-permute-done.2 = f32[4,128]{1,0:T(4,128)S(1)} collective-permute-done((f32[4,128]{1,0:T(4,128)S(1)}, f32[4,128]{1,0:T(4,128)S(1)}, u32[]{:S(2)}, u32[]{:S(2)}) %collective-permute-start.2) | collective-permute-done | bytes 2080 | tf_op jit(solution)/shard_map/ppermute | solution.py:321
  116.4 0.6 broadcast_in_dim.7
  117.0 3.9 %all-to-all-start.4 = ((f32[32,4,128]{2,1,0:T(4,128)}), f32[32,4,128]{2,1,0:T(4,128)S(1)}, u32[]{:S(2)}, u32[]{:S(2)}) async-start(f32[32,4,128]{2,1,0:T(4,128)} %broadcast_in_dim.7), calls=%async_computation.4 | async-start | bytes 131072 | tf_op jit(solution)/shard_map/all_to_all | solution.py:311
  120.9 4.0 %basis.1 = (f32[32,32]{1,0:T(8,128)S(1)}, f32[32,1024]{1,0:T(8,128)}, bf16[1024,128]{1,0:T(8,128)(2,1)S(1)}) custom-call(f32[16,16,128]{2,1,0:T(8,128)S(1)} %all-to-all-done.2.p_ref, f32[4,128]{1,0:T(4,128)S(1)} %add.13.after_ref), custom_call_target="tpu_custom_call" | custom-call | flops 4000000000 | bytes 4000000 | tf_op jit(solution)/shard_map/basis/pallas_call | solution.py:227
  124.9 8.2 %all-to-all-done.4.refs_0_ = f32[32,4,128]{2,1,0:T(4,128)S(1)} async-done(((f32[32,4,128]{2,1,0:T(4,128)}), f32[32,4,128]{2,1,0:T(4,128)S(1)}, u32[]{:S(2)}, u32[]{:S(2)}) %all-to-all-start.4) | async-done | bytes 65568 | tf_op jit(solution)/shard_map/all_to_all | solution.py:311
  133.1 2.3 %residual.1 = (bf16[1024,512]{1,0:T(8,128)(2,1)}, f32[32,512]{1,0:T(8,128)}) custom-call(f32[32,4,128]{2,1,0:T(4,128)S(1)} %all-to-all-done.4.refs_0_, f32[32,32]{1,0:T(8,128)S(1)} %get-tuple-element.12.refs_1_, bf16[1024,128]{1,0:T(8,128)(2,1)S(1)} %get-tuple-element.13.refs_2_, bf16[1024,512]{1,0:T(8,128)(2,1)S(1)} %get-tuple-element.10.hi_ref.refs_3_, ...), custom_call_target="tpu_custom_call" | custom-call | tf_op jit(solution)/shard_map/residual/pallas_call | solution.py:267
  (5 shorter events, 0.1 us)
Async XLA Ops:
  7.2 20.3 %copy-start.1 = (bf16[256,1024]{1,0:T(8,128)(2,1)S(1)}, bf16[256,1024]{1,0:T(8,128)(2,1)}, u32[]{:S(2)}) copy-start(bf16[256,1024]{1,0:T(8,128)(2,1)} %acts_ref.1) | copy-start | bytes 1572868
  7.2 73.6 %copy-start.3 = (bf16[1,1024,512]{2,1,0:T(8,128)(2,1)S(1)}, bf16[1,1024,512]{2,1,0:T(8,128)(2,1)}, u32[]{:S(2)}) copy-start(bf16[1,1024,512]{2,1,0:T(8,128)(2,1)} %param.6) | copy-start | bytes 3145732
  7.2 73.6 %all-gather.2.cloned.1.call-start = ((), (), s32[]{:S(2)}) async-start(), calls=%async_computation.5 | async-start | bytes 4718592 | tf_op jit(solution)/shard_map/all_gather | solution.py:344
  12.1 15.3 %all-to-all-start = ((f32[8,32,256]{2,1,0:T(8,128)}), f32[8,32,256]{2,1,0:T(8,128)S(1)}, u32[]{:S(2)}, u32[]{:S(2)}) async-start(f32[8,32,256]{2,1,0:T(8,128)} %y_chunks.1), calls=%async_computation | async-start | bytes 524288 | tf_op jit(solution)/shard_map/all_to_all | solution.py:346
  21.3 1.2 copy-start.2
  22.5 0.8 copy-start.4
  62.0 5.5 %collective-permute-start = (f32[16,128]{1,0:T(8,128)S(1)}, f32[16,128]{1,0:T(8,128)S(1)}, u32[]{:S(2)}, u32[]{:S(2)}) collective-permute-start(f32[16,128]{1,0:T(8,128)S(1)} %psum.7.after_ref), channel_id=1, source_target_pairs={{0,8},{8,0},{16,24},{24,16},{32,40},{40,32},{48,56},{56,48},{64,72... | collective-permute-start | bytes 24584 | tf_op jit(solution)/shard_map/ppermute | solution.py:321
  67.6 7.5 %collective-permute-start.1 = (f32[16,128]{1,0:T(8,128)S(1)}, f32[16,128]{1,0:T(8,128)S(1)}, u32[]{:S(2)}, u32[]{:S(2)}) collective-permute-start(f32[16,128]{1,0:T(8,128)S(1)} %add.11), channel_id=1, source_target_pairs={{0,16},{8,24},{16,0},{24,8},{32,48},{40,56},{48,32},{56,40},{64,80... | collective-permute-start | bytes 24584 | tf_op jit(solution)/shard_map/ppermute | solution.py:321
  75.7 14.0 %all-to-all-start.2 = ((f32[16,16,128]{2,1,0:T(8,128)}), f32[16,16,128]{2,1,0:T(8,128)S(1)}, u32[]{:S(2)}, u32[]{:S(2)}) async-start(f32[16,16,128]{2,1,0:T(8,128)} %broadcast_in_dim.6), calls=%async_computation.2 | async-start | bytes 262144 | tf_op jit(solution)/shard_map/all_to_all | solution.py:311
  80.8 1.6 %copy-start = (bf16[2048,512]{1,0:T(8,128)(2,1)S(1)}, bf16[2048,512]{1,0:T(8,128)(2,1)}, u32[]{:S(2)}) copy-start(bf16[2048,512]{1,0:T(8,128)(2,1)} %g_ref.3) | copy-start | bytes 6291460
  82.4 2.2 %copy-start.5 = (bf16[2048,1024]{1,0:T(8,128)(2,1)S(1)}, bf16[2048,1024]{1,0:T(8,128)(2,1)}, u32[]{:S(2)}) copy-start(bf16[2048,1024]{1,0:T(8,128)(2,1)} %all-gather.2.cloned.1.call-done.a_ref) | copy-start | bytes 12582916
  110.9 5.5 %collective-permute-start.2 = (f32[4,128]{1,0:T(4,128)S(1)}, f32[4,128]{1,0:T(4,128)S(1)}, u32[]{:S(2)}, u32[]{:S(2)}) collective-permute-start(f32[4,128]{1,0:T(4,128)S(1)} %total.3), channel_id=1, source_target_pairs={{0,8},{8,0},{16,24},{24,16},{32,40},{40,32},{48,56},{56,48},{64,72... | collective-permute-start | bytes 6152 | tf_op jit(solution)/shard_map/ppermute | solution.py:321
  117.0 16.1 %all-to-all-start.4 = ((f32[32,4,128]{2,1,0:T(4,128)}), f32[32,4,128]{2,1,0:T(4,128)S(1)}, u32[]{:S(2)}, u32[]{:S(2)}) async-start(f32[32,4,128]{2,1,0:T(4,128)} %broadcast_in_dim.7), calls=%async_computation.4 | async-start | bytes 131072 | tf_op jit(solution)/shard_map/all_to_all | solution.py:311
Sparse Core Ops, SparseCore 0:
  10.2 42.5 all-gather.1

commit v3 on v1

--- a/solution.py
+++ b/solution.py
@@ -9,7 +9,10 @@
 
 F32 = jnp.float32
 BF16 = jnp.bfloat16
+LANES = 128
 VMEM = pl.BlockSpec(memory_space=pltpu.VMEM)
+HBM = pl.BlockSpec(memory_space=pltpu.HBM)
+ANY = pl.BlockSpec(memory_space=pl.ANY)
 PARAMS = pltpu.CompilerParams(vmem_limit_bytes=32 * 1024 * 1024)
 STREAM = pltpu.CompilerParams(vmem_limit_bytes=60 * 1024 * 1024)
 
@@ -33,39 +36,41 @@
     return pl.CostEstimate(flops=flops, bytes_accessed=moved, transcendentals=0)
 
 
-def y_kernel(q_ref, g_ref, out_ref, q_buf, g_buf, q_sem, g_sems):
+def y_kernel(q_ref, g_ref, out_ref, q_buf, g_buf, y_buf, q_sem, g_sems, y_sems):
     n, _, rows = out_ref.shape
     q_copy = pltpu.make_async_copy(q_ref, q_buf, q_sem)
-    copies = [
-        pltpu.make_async_copy(
-            g_ref.at[pl.ds(s * rows, rows), :],
-            g_buf.at[pl.ds(s * rows, rows), :],
-            g_sems.at[s],
+    q_copy.start()
+    loads, stores = [], []
+    for s in range(n):
+        span = pl.ds(s * rows, rows)
+        loads.append(
+            pltpu.make_async_copy(g_ref.at[span, :], g_buf.at[span, :], g_sems.at[s])
         )
-        for s in range(n)
-    ]
-    q_copy.start()
-    for copy in copies:
-        copy.start()
+        stores.append(pltpu.make_async_copy(y_buf.at[s], out_ref.at[s], y_sems.at[s]))
+        loads[s].start()
     q_copy.wait()
     for s in range(n):
-        copies[s].wait()
-        out_ref[s] = dot(q_buf[...], g_buf[s * rows : (s + 1) * rows, :], 1, 1)
+        loads[s].wait()
+        y_buf[s] = dot(q_buf[...], g_buf[s * rows : (s + 1) * rows, :], 1, 1)
+        stores[s].start()
+    for s in range(n):
+        stores[s].wait()
 
 
 def y_chunks(q_t, grads, n):
     rank, cols = q_t.shape
     rows = grads.shape[0] // n
-    hbm = pl.BlockSpec(memory_space=pltpu.HBM)
     return pl.pallas_call(
         y_kernel,
-        in_specs=[hbm, hbm],
-        out_specs=VMEM,
+        in_specs=[HBM, HBM],
+        out_specs=HBM,
         out_shape=jax.ShapeDtypeStruct((n, rank, rows), F32),
         scratch_shapes=[
             pltpu.VMEM(q_t.shape, BF16),
             pltpu.VMEM(grads.shape, BF16),
+            pltpu.VMEM((n, rank, rows), F32),
             pltpu.SemaphoreType.DMA,
+            pltpu.SemaphoreType.DMA((n,)),
             pltpu.SemaphoreType.DMA((n,)),
         ],
         compiler_params=STREAM,
@@ -137,11 +142,11 @@
             pl.BlockSpec((tokens, block), lambda i: (0, i)),
             pl.BlockSpec((tokens, cols), lambda i: (0, 0)),
             out,
-            pl.BlockSpec(memory_space=pl.ANY),
+            ANY,
         ],
         out_specs=[out, out],
         out_shape=[shape, shape],
-        compiler_params=PARAMS,
+        compiler_params=STREAM,
         cost_estimate=cost(2 * tokens * width * cols, acts_all.size * 2 + grads.size * 2),
         name="merged_parts",
     )(acts_all, grads, error, after)
@@ -157,18 +162,21 @@
         both = dot(jnp.concatenate([high, low], axis=0), hi_ref[span, :])
         term = both[:rank] + (both[rank:] + dot(high, lo_ref[span, :]))
         total = term if total is None else total + term
+    across = total.shape[1] // LANES
     for k in range(pieces):
-        out_ref[k] = total[k * rows : (k + 1) * rows, :]
+        r, c = k // across, k % across
+        out_ref[k] = total[r * rows : (r + 1) * rows, c * LANES : (c + 1) * LANES]
 
 
 def q_pieces(p_all, hi, lo, pieces):
     n, rank, width = p_all.shape
     cols = hi.shape[1]
+    rows = rank * cols // (pieces * LANES)
     return pl.pallas_call(
         q_kernel,
         in_specs=[VMEM] * 3,
         out_specs=VMEM,
-        out_shape=jax.ShapeDtypeStruct((pieces, rank // pieces, cols), F32),
+        out_shape=jax.ShapeDtypeStruct((pieces, rows, LANES), F32),
         compiler_params=PARAMS,
         cost_estimate=cost(2 * hi.size * rank * 8, hi.size * 4),
         name="q_pieces",
@@ -216,7 +224,7 @@
     size = n * width
     return pl.pallas_call(
         basis_kernel,
-        in_specs=[VMEM, pl.BlockSpec(memory_space=pl.ANY)],
+        in_specs=[VMEM, ANY],
         out_specs=[VMEM] * 3,
         out_shape=[
             jax.ShapeDtypeStruct((rank, rank), F32),
@@ -230,57 +238,61 @@
     )(p_all, after)
 
 
-def residual_kernel(scale, q_ref, inv_ref, stack_ref, hi_ref, lo_ref, out_ref, factor_ref, raw, tall):
-    @pl.when(pl.program_id(0) == 0)
-    def _():
-        pieces, rows, _ = q_ref.shape
-        for k in range(pieces):
-            raw[k * rows : (k + 1) * rows, :] = q_ref[k]
-        factor = scale * jnp.dot(
-            inv_ref[...],
-            raw[...],
-            precision=lax.Precision.HIGHEST,
-            preferred_element_type=F32,
+def residual_kernel(scale, q_ref, inv_ref, stack_ref, hi_ref, lo_ref, out_ref, factor_ref, raw, factor, out_buf, sems, factor_sem):
+    pieces, rows, _ = q_ref.shape
+    across = raw.shape[1] // LANES
+    for k in range(pieces):
+        r, c = k // across, k % across
+        raw[r * rows : (r + 1) * rows, c * LANES : (c + 1) * LANES] = q_ref[k]
+    factor[...] = scale * jnp.dot(
+        inv_ref[...],
+        raw[...],
+        precision=lax.Precision.HIGHEST,
+        preferred_element_type=F32,
+    )
+    copies = [pltpu.make_async_copy(factor, factor_ref, factor_sem)]
+    copies[0].start()
+    high, low = parts_of(factor[...], 2)
+    tall = jnp.concatenate([high, low, high, jnp.zeros_like(low)], axis=0)
+    blocks = sems.shape[0]
+    block = out_ref.shape[0] // blocks
+    for i in range(blocks):
+        span = pl.ds(i * block, block)
+        merged = hi_ref[span, :].astype(F32) + lo_ref[span, :].astype(F32)
+        out_buf[span, :] = (merged - dot(stack_ref[span, :], tall)).astype(BF16)
+        copies.append(
+            pltpu.make_async_copy(out_buf.at[span, :], out_ref.at[span, :], sems.at[i])
         )
-        factor_ref[...] = factor
-        high, low = parts_of(factor, 2)
-        tall[...] = jnp.concatenate([high, low, high, jnp.zeros_like(low)], axis=0)
-
-    merged = hi_ref[...].astype(F32) + lo_ref[...].astype(F32)
-    out_ref[...] = (merged - dot(stack_ref[...], tall[...])).astype(BF16)
+        copies[-1].start()
+    for copy in copies:
+        copy.wait()
 
 
 def residual_of(q_all, inverse, stack, hi, lo, replicas):
     rank = inverse.shape[0]
-    height, cols = hi.shape
-    block = 256
-    part = pl.BlockSpec((block, cols), lambda i: (i, 0))
-    whole = lambda shape: pl.BlockSpec(shape, lambda i: (0,) * len(shape))
+    cols = hi.shape[1]
     return pl.pallas_call(
         lambda *refs: residual_kernel(1.0 / replicas, *refs),
-        grid=(height // block,),
-        in_specs=[
-            whole(q_all.shape),
-            whole(inverse.shape),
-            pl.BlockSpec((block, stack.shape[1]), lambda i: (i, 0)),
-            part,
-            part,
-        ],
-        out_specs=[part, whole((rank, cols))],
+        in_specs=[VMEM] * 5,
+        out_specs=[HBM, HBM],
         out_shape=[
-            jax.ShapeDtypeStruct((height, cols), BF16),
+            jax.ShapeDtypeStruct(hi.shape, BF16),
             jax.ShapeDtypeStruct((rank, cols), F32),
         ],
         scratch_shapes=[
             pltpu.VMEM((rank, cols), F32),
-            pltpu.VMEM((4 * rank, cols), BF16),
+            pltpu.VMEM((rank, cols), F32),
+            pltpu.VMEM(hi.shape, BF16),
+            pltpu.SemaphoreType.DMA((8,)),
+            pltpu.SemaphoreType.DMA,
         ],
         compiler_params=PARAMS,
         name="residual",
     )(q_all, inverse, stack, hi, lo)
 
 
-def total_kernel(x_ref, out_ref):
+def total_kernel(x_ref, *refs):
+    out_ref = refs[-1]
     total = x_ref[0]
     for s in range(1, x_ref.shape[0]):
         total = total + x_ref[s]
@@ -288,16 +300,16 @@
         out_ref[s] = total
 
 
-def total_for(x, n):
+def total_for(x, n, *after):
     return pl.pallas_call(
         total_kernel,
-        in_specs=[VMEM],
+        in_specs=[VMEM] + [ANY] * len(after),
         out_specs=VMEM,
         out_shape=jax.ShapeDtypeStruct((n,) + x.shape[1:], F32),
         compiler_params=PARAMS,
         cost_estimate=cost(x.size, 4 * x.size),
         name="total",
-    )(x)
+    )(x, *after)
 
 
 def per_device(acts, grads_out, error_buffer, prior_q):
@@ -316,6 +328,9 @@
     def over_z(x):
         return lax.all_to_all(x, "dp", 0, 0, axis_index_groups=along_z)
 
+    def over_replicas(x):
+        return lax.all_to_all(x, "dp", 0, 0)
+
     error = error_buffer[0]
     q_t = prior_q.T
     acts_all = lax.all_gather(acts, "tensor", axis=0, tiled=True)
@@ -323,13 +338,13 @@
     y_all = over_tensor(y_chunks(q_t, grads_out, tensor))
     p_terms = over_tensor(p_chunks(y_all, acts, error_term(q_t, error)))
     p_row = total_for(over_y(total_for(p_terms, side)), side)
-    p_all = over_tensor(total_for(over_z(p_row), tensor))
-
     hi, lo = merged_parts(acts_all, grads_out, error, p_row)
-    pieces = q_pieces(p_all, hi, lo, side)
-    q_sum = total_for(over_z(total_for(over_y(pieces), side)), side)
-    q_all = over_y(q_sum)
-    inverse, basis, stack = basis_of(p_all, pieces)
+    p_all = over_tensor(total_for(over_z(p_row), tensor, hi))
+
+    pieces = q_pieces(p_all, hi, lo, replicas)
+    q_sum = total_for(over_replicas(pieces), replicas)
+    q_all = over_replicas(q_sum)
+    inverse, basis, stack = basis_of(p_all, q_sum)
     residual, factor = residual_of(q_all, inverse, stack, hi, lo, replicas)
     return (residual[None], basis.T, factor.T)
 

time: 126 us -> 126 us (level)
  blocking collectives: 62.5 us -> 48.4 us
  starting transfers between devices: 17.4 us -> 24.5 us
  waiting for transfers between devices: 8.72 us -> 14.6 us
  Pallas kernels: 16.5 us -> 19.1 us
  local copies, waits for them, and re-layouts: 5.77 us -> 4.45 us
    all_to_all x2 -> x1, blocking collectives: 30.2 us -> 18.3 us  [over_replicas(): return lax.all_to_all(x, 'dp', 0, 0)]
    all_to_all x1 -> x2, starting transfers between devices: 3.35 us -> 15.2 us  [the longest x1 10.6 us: over_z(): return lax.all_to_all(x, 'dp', 0, 0, axis_index_groups=along_z)]
    all_to_all x2 -> x1, blocking collectives: 22.2 us -> 11.5 us  [over_y(): return lax.all_to_all(x, 'dp', 0, 0, axis_index_groups=along_y)]
    all_to_all x1 -> x2, blocking collectives: 10.1 us -> 18.6 us  [over_tensor(): return lax.all_to_all(x, 'tensor', 0, 0)]
    all_to_all x1 -> x2, waiting for transfers between devices: 4.31 us -> 10.2 us  [the longest x1 8.24 us: over_replicas(): return lax.all_to_all(x, 'dp', 0, 0)]
    all_to_all x2 -> x1, starting transfers between devices: 14 us -> 9.24 us  [over_tensor(): return lax.all_to_all(x, 'tensor', 0, 0)]
    pallas_call x1, Pallas kernels: 3.67 us -> 7.08 us  [merged_parts(): pl.pallas_call(merged_kernel, grid=(width // block,), in_specs=[pl.BlockS...]
    unnamed x12 -> x14, local copies, waits for them, and re-layouts: 5.77 us -> 4.45 us
  transfers between devices with their start and end apart: 4 -> 4, of which waited for: 2 -> 3; matrix products, arithmetic and copies ran while one was open for 0% -> 0% of each run, Pallas kernels for 10% -> 13%
where the time goes in v3:
time: 126 us; the launch traced here: 125 us
  blocking collectives  48.4 us (38%)
  starting transfers between devices  24.5 us (19%)
  Pallas kernels  19.1 us (15%)
  waiting for transfers between devices  14.6 us (12%)
  between operations  14.1 us (11%)
  local copies, waits for them, and re-layouts  4.45 us (4%)
    all_to_all x2, blocking collectives, over_tensor(): return lax.all_to_all(x, 'tensor', 0, 0)  18.6 us
    all_to_all x1, blocking collectives, over_replicas(): return lax.all_to_all(x, 'dp', 0, 0)  18.3 us
    all_to_all x1, blocking collectives, over_y(): return lax.all_to_all(x, 'dp', 0, 0, axis_index_groups=along_y)  11.5 us
    all_to_all x1, starting transfers between devices, over_z(): return lax.all_to_all(x, 'dp', 0, 0, axis_index_groups=along_z)  10.6 us
    all_to_all x1, starting transfers between devices, over_tensor(): return lax.all_to_all(x, 'tensor', 0, 0)  9.24 us
    all_to_all x1, waiting for transfers between devices, over_replicas(): return lax.all_to_all(x, 'dp', 0, 0)  8.24 us
    pallas_call x1, Pallas kernels, merged_parts(): pl.pallas_call(merged_kernel, grid=(width // block,), in_specs=[pl.BlockS...  7.08 us
    all_to_all x1, starting transfers between devices, over_replicas(): return lax.all_to_all(x, 'dp', 0, 0)  4.62 us
  transfers between devices with their start and end apart: 4, of which 3 were waited for; matrix products, arithmetic and copies ran while one was open for 0% of the time, Pallas kernels for 13%

profile of v3, /device:TPU:2, one launch (start us, length us, event | category | flops | bytes accessed | tf_op | source)
XLA Modules:
  0.0 125.2 jit_solution(11489391710761170183)
XLA Ops:
  7.2 0.0 copy-start.4
  7.2 0.0 all-gather.2.cloned.1.call-start
  7.2 0.7 all-gather.2.cloned.1.call-update
  7.9 4.1 %y_chunks.1 = f32[8,32,256]{2,1,0:T(8,128)} custom-call(bf16[32,512]{1,0:T(8,128)(2,1)} %bitcast.7, bf16[2048,512]{1,0:T(8,128)(2,1)} %g_ref.3), custom_call_target="tpu_custom_call" | custom-call | flops 536870912 | bytes 2097152 | tf_op jit(solution)/shard_map/y_chunks/pallas_call | solution.py:63
  12.0 9.2 %all-to-all-start = ((f32[8,32,256]{2,1,0:T(8,128)}), f32[8,32,256]{2,1,0:T(8,128)S(1)}, u32[]{:S(2)}, u32[]{:S(2)}) async-start(f32[8,32,256]{2,1,0:T(8,128)} %y_chunks.1), calls=%async_computation | async-start | bytes 524288 | tf_op jit(solution)/shard_map/all_to_all | solution.py:323
  21.3 0.0 copy-start.5
  21.3 1.2 copy-done.5
  22.5 0.0 copy-start.6
  22.5 0.8 copy-done.6
  23.3 0.4 error_term.1.e_ref
  23.7 3.7 %all-to-all-done.y_ref = f32[8,32,256]{2,1,0:T(8,128)S(1)} async-done(((f32[8,32,256]{2,1,0:T(8,128)}), f32[8,32,256]{2,1,0:T(8,128)S(1)}, u32[]{:S(2)}, u32[]{:S(2)}) %all-to-all-start) | async-done | bytes 262176 | tf_op jit(solution)/shard_map/all_to_all | solution.py:323
  27.4 0.0 copy-done.4
  27.4 0.2 p_chunks.1
  27.6 10.1 %all_to_all.35.x_ref = f32[8,32,128]{2,1,0:T(8,128)S(1)} all-to-all(f32[8,32,128]{2,1,0:T(8,128)S(1)} %p_chunks.1), channel_id=1, replica_groups=mesh['dp'=64,'tensor'=8] {'tensor'}, dimensions={0} | all-to-all | bytes 262144 | tf_op jit(solution)/shard_map/all_to_all | solution.py:323
  37.7 11.5 %all_to_all.36.x_ref = f32[8,32,128]{2,1,0:T(8,128)S(1)} all-to-all(f32[8,32,128]{2,1,0:T(8,128)S(1)} %total.4), channel_id=1, replica_groups={{0,64,128,192,256,320,384,448},{8,72,136,200,264,328,392,456},{16,80,14..., dimensions={0} | all-to-all | bytes 262144 | tf_op jit(solution)/shard_map/all_to_all | solution.py:326
  49.2 0.7 total.5.after_ref
  49.8 10.6 %all-to-all-start.3 = ((f32[8,32,128]{2,1,0:T(8,128)}), f32[8,32,128]{2,1,0:T(8,128)S(1)}, u32[]{:S(2)}, u32[]{:S(2)}) async-start(f32[8,32,128]{2,1,0:T(8,128)} %total.5.after_ref), calls=%async_computation.3 | async-start | bytes 262144 | tf_op jit(solution)/shard_map/all_to_all | solution.py:329
  60.4 0.0 all-gather.2.cloned.1.call-done.a_ref
  60.4 7.1 %merged_parts.1 = (bf16[1024,512]{1,0:T(8,128)(2,1)}, bf16[1024,512]{1,0:T(8,128)(2,1)}) custom-call(bf16[2048,1024]{1,0:T(8,128)(2,1)} %all-gather.2.cloned.1.call-done.a_ref, bf16[2048,512]{1,0:T(8,128)(2,1)} %g_ref.3, bf16[1024,512]{1,0:T(8,128)(2,1)} %bitcast.5, f32[8,32,128]{2,1,0:T(8,128)} %total.5.after_ref), custom_call_target="tpu_custom_call" | custom-call | flops 2147483648 | bytes 6291456 | tf_op jit(solution)/shard_map/merged_parts/pallas_call | solution.py:138
  67.5 2.0 %all-to-all-done.3.x_ref = f32[8,32,128]{2,1,0:T(8,128)S(1)} async-done(((f32[8,32,128]{2,1,0:T(8,128)}), f32[8,32,128]{2,1,0:T(8,128)S(1)}, u32[]{:S(2)}, u32[]{:S(2)}) %all-to-all-start.3) | async-done | bytes 131104 | tf_op jit(solution)/shard_map/all_to_all | solution.py:329
  69.5 0.0 copy-start
  69.5 1.2 copy-done
  70.7 8.5 %all_to_all.37.p_ref = f32[8,32,128]{2,1,0:T(8,128)S(1)} all-to-all(f32[8,32,128]{2,1,0:T(8,128)S(1)} %total.6), channel_id=1, replica_groups=mesh['dp'=64,'tensor'=8] {'tensor'}, dimensions={0} | all-to-all | bytes 262144 | tf_op jit(solution)/shard_map/all_to_all | solution.py:323
  79.3 0.0 copy-start.2
  79.3 1.2 copy-done.2
  80.5 0.5 q_pieces.1
  81.0 18.3 %all_to_all.38.x_ref = f32[64,2,128]{2,1,0:T(2,128)S(1)} all-to-all(f32[64,2,128]{2,1,0:T(2,128)S(1)} %q_pieces.1), channel_id=1, replica_groups=mesh['dp'=64,'tensor'=8] {'dp'}, dimensions={0} | all-to-all | bytes 131072 | tf_op jit(solution)/shard_map/all_to_all | solution.py:332
  99.3 0.7 total.7.after_ref
  100.0 4.6 %all-to-all-start.6 = ((f32[64,2,128]{2,1,0:T(2,128)}), f32[64,2,128]{2,1,0:T(2,128)S(1)}, u32[]{:S(2)}, u32[]{:S(2)}) async-start(f32[64,2,128]{2,1,0:T(2,128)} %total.7.after_ref), calls=%async_computation.6 | async-start | bytes 131072 | tf_op jit(solution)/shard_map/all_to_all | solution.py:332
  104.6 0.0 copy-start.1
  104.6 0.0 copy-start.3
  104.6 4.0 %basis.1 = (f32[32,32]{1,0:T(8,128)S(1)}, f32[32,1024]{1,0:T(8,128)}, bf16[1024,128]{1,0:T(8,128)(2,1)S(1)}) custom-call(f32[8,32,128]{2,1,0:T(8,128)S(1)} %all_to_all.37.p_ref, f32[64,2,128]{2,1,0:T(2,128)} %total.7.after_ref), custom_call_target="tpu_custom_call" | custom-call | flops 4000000000 | bytes 4000000 | tf_op jit(solution)/shard_map/basis/pallas_call | solution.py:225
  108.6 8.2 %all-to-all-done.6.refs_0_ = f32[64,2,128]{2,1,0:T(2,128)S(1)} async-done(((f32[64,2,128]{2,1,0:T(2,128)}), f32[64,2,128]{2,1,0:T(2,128)S(1)}, u32[]{:S(2)}, u32[]{:S(2)}) %all-to-all-start.6) | async-done | bytes 65568 | tf_op jit(solution)/shard_map/all_to_all | solution.py:332
  116.8 0.0 copy-done.1
  116.9 0.0 copy-done.3
  116.9 1.5 %residual.1 = (bf16[1024,512]{1,0:T(8,128)(2,1)}, f32[32,512]{1,0:T(8,128)}) custom-call(f32[64,2,128]{2,1,0:T(2,128)S(1)} %all-to-all-done.6.refs_0_, f32[32,32]{1,0:T(8,128)S(1)} %get-tuple-element.12.refs_1_, bf16[1024,128]{1,0:T(8,128)(2,1)S(1)} %get-tuple-element.13.refs_2_, bf16[1024,512]{1,0:T(8,128)(2,1)S(1)} %copy-done.1, ...), custom_call_target="tpu_custom_call" | custom-call | tf_op jit(solution)/shard_map/residual/pallas_call | solution.py:274
  (2 shorter events, 0.0 us)
Async XLA Ops:
  7.2 20.2 %copy-start.4 = (bf16[256,1024]{1,0:T(8,128)(2,1)S(1)}, bf16[256,1024]{1,0:T(8,128)(2,1)}, u32[]{:S(2)}) copy-start(bf16[256,1024]{1,0:T(8,128)(2,1)} %acts_ref.1) | copy-start | bytes 1572868
  7.2 53.3 %all-gather.2.cloned.1.call-start = ((), (), s32[]{:S(2)}) async-start(), calls=%async_computation.7 | async-start | bytes 4718592 | tf_op jit(solution)/shard_map/all_gather | solution.py:336
  12.0 15.3 %all-to-all-start = ((f32[8,32,256]{2,1,0:T(8,128)}), f32[8,32,256]{2,1,0:T(8,128)S(1)}, u32[]{:S(2)}, u32[]{:S(2)}) async-start(f32[8,32,256]{2,1,0:T(8,128)} %y_chunks.1), calls=%async_computation | async-start | bytes 524288 | tf_op jit(solution)/shard_map/all_to_all | solution.py:323
  21.3 1.2 copy-start.5
  22.5 0.8 copy-start.6
  49.8 19.7 %all-to-all-start.3 = ((f32[8,32,128]{2,1,0:T(8,128)}), f32[8,32,128]{2,1,0:T(8,128)S(1)}, u32[]{:S(2)}, u32[]{:S(2)}) async-start(f32[8,32,128]{2,1,0:T(8,128)} %total.5.after_ref), calls=%async_computation.3 | async-start | bytes 262144 | tf_op jit(solution)/shard_map/all_to_all | solution.py:329
  69.5 1.2 copy-start
  79.3 1.2 copy-start.2
  100.0 16.9 %all-to-all-start.6 = ((f32[64,2,128]{2,1,0:T(2,128)}), f32[64,2,128]{2,1,0:T(2,128)S(1)}, u32[]{:S(2)}, u32[]{:S(2)}) async-start(f32[64,2,128]{2,1,0:T(2,128)} %total.7.after_ref), calls=%async_computation.6 | async-start | bytes 131072 | tf_op jit(solution)/shard_map/all_to_all | solution.py:332
  104.6 12.3 %copy-start.1 = (bf16[1024,512]{1,0:T(8,128)(2,1)S(1)}, bf16[1024,512]{1,0:T(8,128)(2,1)}, u32[]{:S(2)}) copy-start(bf16[1024,512]{1,0:T(8,128)(2,1)} %get-tuple-element.10.refs_0_.hi_ref.refs_3_) | copy-start | bytes 3145732
  104.6 12.2 %copy-start.3 = (bf16[1024,512]{1,0:T(8,128)(2,1)S(1)}, bf16[1024,512]{1,0:T(8,128)(2,1)}, u32[]{:S(2)}) copy-start(bf16[1024,512]{1,0:T(8,128)(2,1)} %get-tuple-element.11.lo_ref.refs_4_) | copy-start | bytes 3145732
Sparse Core Ops, SparseCore 0:
  10.2 42.5 all-gather.1

commit v4 on v3

--- a/solution.py
+++ b/solution.py
@@ -9,7 +9,6 @@
 
 F32 = jnp.float32
 BF16 = jnp.bfloat16
-LANES = 128
 VMEM = pl.BlockSpec(memory_space=pltpu.VMEM)
 HBM = pl.BlockSpec(memory_space=pltpu.HBM)
 ANY = pl.BlockSpec(memory_space=pl.ANY)
@@ -123,30 +122,27 @@
 
 def merged_kernel(a_ref, g_ref, e_ref, after_ref, hi_ref, lo_ref):
     del after_ref
-    merged = dot(a_ref[...], g_ref[...], 0, 0) + e_ref[...].astype(F32)
-    hi, lo = parts_of(merged, 2)
-    hi_ref[...] = hi
-    lo_ref[...] = lo
+    block = 256
+
+    @pl.loop(0, a_ref.shape[1] // block)
+    def _(i):
+        span = pl.ds(pl.multiple_of(i * block, block), block)
+        merged = dot(a_ref[:, span], g_ref[...], 0, 0) + e_ref[span, :].astype(F32)
+        hi, lo = parts_of(merged, 2)
+        hi_ref[span, :] = hi
+        lo_ref[span, :] = lo
 
 
 def merged_parts(acts_all, grads, error, after):
     tokens, width = acts_all.shape
     cols = grads.shape[1]
-    block = 256
     shape = jax.ShapeDtypeStruct((width, cols), BF16)
-    out = pl.BlockSpec((block, cols), lambda i: (i, 0))
     return pl.pallas_call(
         merged_kernel,
-        grid=(width // block,),
-        in_specs=[
-            pl.BlockSpec((tokens, block), lambda i: (0, i)),
-            pl.BlockSpec((tokens, cols), lambda i: (0, 0)),
-            out,
-            ANY,
-        ],
-        out_specs=[out, out],
+        in_specs=[VMEM, VMEM, VMEM, ANY],
+        out_specs=[VMEM, VMEM],
         out_shape=[shape, shape],
-        compiler_params=STREAM,
+        compiler_params=PARAMS,
         cost_estimate=cost(2 * tokens * width * cols, acts_all.size * 2 + grads.size * 2),
         name="merged_parts",
     )(acts_all, grads, error, after)
@@ -162,21 +158,18 @@
         both = dot(jnp.concatenate([high, low], axis=0), hi_ref[span, :])
         term = both[:rank] + (both[rank:] + dot(high, lo_ref[span, :]))
         total = term if total is None else total + term
-    across = total.shape[1] // LANES
     for k in range(pieces):
-        r, c = k // across, k % across
-        out_ref[k] = total[r * rows : (r + 1) * rows, c * LANES : (c + 1) * LANES]
+        out_ref[k] = total[k * rows : (k + 1) * rows, :]
 
 
 def q_pieces(p_all, hi, lo, pieces):
     n, rank, width = p_all.shape
     cols = hi.shape[1]
-    rows = rank * cols // (pieces * LANES)
     return pl.pallas_call(
         q_kernel,
         in_specs=[VMEM] * 3,
         out_specs=VMEM,
-        out_shape=jax.ShapeDtypeStruct((pieces, rows, LANES), F32),
+        out_shape=jax.ShapeDtypeStruct((pieces, rank // pieces, cols), F32),
         compiler_params=PARAMS,
         cost_estimate=cost(2 * hi.size * rank * 8, hi.size * 4),
         name="q_pieces",
@@ -240,10 +233,8 @@
 
 def residual_kernel(scale, q_ref, inv_ref, stack_ref, hi_ref, lo_ref, out_ref, factor_ref, raw, factor, out_buf, sems, factor_sem):
     pieces, rows, _ = q_ref.shape
-    across = raw.shape[1] // LANES
     for k in range(pieces):
-        r, c = k // across, k % across
-        raw[r * rows : (r + 1) * rows, c * LANES : (c + 1) * LANES] = q_ref[k]
+        raw[k * rows : (k + 1) * rows, :] = q_ref[k]
     factor[...] = scale * jnp.dot(
         inv_ref[...],
         raw[...],
@@ -328,9 +319,6 @@
     def over_z(x):
         return lax.all_to_all(x, "dp", 0, 0, axis_index_groups=along_z)
 
-    def over_replicas(x):
-        return lax.all_to_all(x, "dp", 0, 0)
-
     error = error_buffer[0]
     q_t = prior_q.T
     acts_all = lax.all_gather(acts, "tensor", axis=0, tiled=True)
@@ -341,9 +329,9 @@
     hi, lo = merged_parts(acts_all, grads_out, error, p_row)
     p_all = over_tensor(total_for(over_z(p_row), tensor, hi))
 
-    pieces = q_pieces(p_all, hi, lo, replicas)
-    q_sum = total_for(over_replicas(pieces), replicas)
-    q_all = over_replicas(q_sum)
+    pieces = q_pieces(p_all, hi, lo, side)
+    q_sum = total_for(over_z(total_for(over_y(pieces), side)), side)
+    q_all = over_y(q_sum)
     inverse, basis, stack = basis_of(p_all, q_sum)
     residual, factor = residual_of(q_all, inverse, stack, hi, lo, replicas)
     return (residual[None], basis.T, factor.T)

time: 126 us -> 124 us (0.984)
  blocking collectives: 48.4 us -> 54.1 us
  Pallas kernels: 19.1 us -> 15.1 us
  waiting for transfers between devices: 14.6 us -> 10.8 us
  local copies, waits for them, and re-layouts: 4.45 us -> 5.77 us
  starting transfers between devices: 24.5 us -> 23.2 us
    all_to_all x1 -> x2, blocking collectives: 11.5 us -> 22.2 us  [over_y(): return lax.all_to_all(x, 'dp', 0, 0, axis_index_groups=along_y)]
    all_to_all x1, blocking collectives: 18.3 us -> 13.3 us  [over_z(): return lax.all_to_all(x, 'dp', 0, 0, axis_index_groups=along_z)]
    all_to_all x1, waiting for transfers between devices: 8.24 us -> 4.31 us  [over_y(): return lax.all_to_all(x, 'dp', 0, 0, axis_index_groups=along_y)]
    pallas_call x1, Pallas kernels: 7.08 us -> 3.16 us  [merged_parts(): pl.pallas_call(merged_kernel, in_specs=[VMEM, VMEM, VMEM, ANY], out_specs...]
    unnamed x14 -> x12, local copies, waits for them, and re-layouts: 4.45 us -> 5.77 us
    all_to_all x1, starting transfers between devices: 4.62 us -> 3.35 us  [over_y(): return lax.all_to_all(x, 'dp', 0, 0, axis_index_groups=along_y)]
  transfers between devices with their start and end apart: 4 -> 4, of which waited for: 3 -> 3; matrix products, arithmetic and copies ran while one was open for 0% -> 0% of each run, Pallas kernels for 13% -> 10%
where the time goes in v4:
time: 124 us; the launch traced here: 123 us
  blocking collectives  54.1 us (44%)
  starting transfers between devices  23.2 us (19%)
  Pallas kernels  15.1 us (12%)
  between operations  14.1 us (11%)
  waiting for transfers between devices  10.8 us (9%)
  local copies, waits for them, and re-layouts  5.77 us (5%)
    all_to_all x2, blocking collectives, over_y(): return lax.all_to_all(x, 'dp', 0, 0, axis_index_groups=along_y)  22.2 us
    all_to_all x2, blocking collectives, over_tensor(): return lax.all_to_all(x, 'tensor', 0, 0)  18.6 us
    all_to_all x1, blocking collectives, over_z(): return lax.all_to_all(x, 'dp', 0, 0, axis_index_groups=along_z)  13.3 us
    all_to_all x1, starting transfers between devices, over_z(): return lax.all_to_all(x, 'dp', 0, 0, axis_index_groups=along_z)  10.6 us
    all_to_all x1, starting transfers between devices, over_tensor(): return lax.all_to_all(x, 'tensor', 0, 0)  9.24 us
    unnamed x12, local copies, waits for them, and re-layouts  5.77 us
    all_to_all x1, waiting for transfers between devices, over_y(): return lax.all_to_all(x, 'dp', 0, 0, axis_index_groups=along_y)  4.31 us
    pallas_call x1, Pallas kernels, y_chunks(): pl.pallas_call(y_kernel, in_specs=[HBM, HBM], out_specs=HBM, out_shape=ja...  4.13 us
  transfers between devices with their start and end apart: 4, of which 3 were waited for; matrix products, arithmetic and copies ran while one was open for 0% of the time, Pallas kernels for 10%

profile of v4, /device:TPU:2, one launch (start us, length us, event | category | flops | bytes accessed | tf_op | source)
XLA Modules:
  0.0 123.1 jit_solution(8377974036824863086)
XLA Ops:
  7.2 0.0 copy-start.1
  7.2 0.0 copy-start.3
  7.2 0.0 all-gather.2.cloned.1.call-start
  7.2 0.7 all-gather.2.cloned.1.call-update
  7.9 4.1 %y_chunks.1 = f32[8,32,256]{2,1,0:T(8,128)} custom-call(bf16[32,512]{1,0:T(8,128)(2,1)} %bitcast.7, bf16[2048,512]{1,0:T(8,128)(2,1)} %g_ref.3), custom_call_target="tpu_custom_call" | custom-call | flops 536870912 | bytes 2097152 | tf_op jit(solution)/shard_map/y_chunks/pallas_call | solution.py:62
  12.1 9.2 %all-to-all-start = ((f32[8,32,256]{2,1,0:T(8,128)}), f32[8,32,256]{2,1,0:T(8,128)S(1)}, u32[]{:S(2)}, u32[]{:S(2)}) async-start(f32[8,32,256]{2,1,0:T(8,128)} %y_chunks.1), calls=%async_computation | async-start | bytes 524288 | tf_op jit(solution)/shard_map/all_to_all | solution.py:314
  21.3 0.0 copy-start.2
  21.3 1.2 copy-done.2
  22.5 0.0 copy-start.4
  22.5 0.8 copy-done.4
  23.3 0.4 error_term.1.e_ref
  23.7 3.7 %all-to-all-done.y_ref = f32[8,32,256]{2,1,0:T(8,128)S(1)} async-done(((f32[8,32,256]{2,1,0:T(8,128)}), f32[8,32,256]{2,1,0:T(8,128)S(1)}, u32[]{:S(2)}, u32[]{:S(2)}) %all-to-all-start) | async-done | bytes 262176 | tf_op jit(solution)/shard_map/all_to_all | solution.py:314
  27.4 0.0 copy-done.1
  27.4 0.2 p_chunks.1
  27.6 10.1 %all_to_all.40.x_ref = f32[8,32,128]{2,1,0:T(8,128)S(1)} all-to-all(f32[8,32,128]{2,1,0:T(8,128)S(1)} %p_chunks.1), channel_id=1, replica_groups=mesh['dp'=64,'tensor'=8] {'tensor'}, dimensions={0} | all-to-all | bytes 262144 | tf_op jit(solution)/shard_map/all_to_all | solution.py:314
  37.7 11.5 %all_to_all.41.x_ref = f32[8,32,128]{2,1,0:T(8,128)S(1)} all-to-all(f32[8,32,128]{2,1,0:T(8,128)S(1)} %total.5), channel_id=1, replica_groups={{0,64,128,192,256,320,384,448},{8,72,136,200,264,328,392,456},{16,80,14..., dimensions={0} | all-to-all | bytes 262144 | tf_op jit(solution)/shard_map/all_to_all | solution.py:317
  49.2 0.7 total.6.after_ref
  49.9 10.6 %all-to-all-start.3 = ((f32[8,32,128]{2,1,0:T(8,128)}), f32[8,32,128]{2,1,0:T(8,128)S(1)}, u32[]{:S(2)}, u32[]{:S(2)}) async-start(f32[8,32,128]{2,1,0:T(8,128)} %total.6.after_ref), calls=%async_computation.3 | async-start | bytes 262144 | tf_op jit(solution)/shard_map/all_to_all | solution.py:320
  60.4 0.0 all-gather.2.cloned.1.call-done.a_ref
  60.5 0.0 copy-done.3
  60.5 0.0 copy-start
  60.5 1.6 %copy-done = bf16[2048,512]{1,0:T(8,128)(2,1)S(1)} copy-done((bf16[2048,512]{1,0:T(8,128)(2,1)S(1)}, bf16[2048,512]{1,0:T(8,128)(2,1)}, u32[]{:S(2)}) %copy-start) | copy-done | bytes 2097176
  62.1 0.0 copy-start.5
  62.1 2.2 %copy-done.5 = bf16[2048,1024]{1,0:T(8,128)(2,1)S(1)} copy-done((bf16[2048,1024]{1,0:T(8,128)(2,1)S(1)}, bf16[2048,1024]{1,0:T(8,128)(2,1)}, u32[]{:S(2)}) %copy-start.5) | copy-done | bytes 4194328
  64.3 3.2 %merged_parts.1 = (bf16[1024,512]{1,0:T(8,128)(2,1)S(1)}, bf16[1024,512]{1,0:T(8,128)(2,1)S(1)}) custom-call(bf16[2048,1024]{1,0:T(8,128)(2,1)S(1)} %copy-done.5, bf16[2048,512]{1,0:T(8,128)(2,1)S(1)} %copy-done, bf16[1024,512]{1,0:T(8,128)(2,1)S(1)} %bitcast.6, f32[8,32,128]{2,1,0:T(8,128)} %total.6.after_ref), custom_call_target="tpu_custom_call" | custom-call | flops 2147483648 | bytes 6291456 | tf_op jit(solution)/shard_map/merged_parts/pallas_call | solution.py:140
  67.4 2.1 %all-to-all-done.3.x_ref = f32[8,32,128]{2,1,0:T(8,128)S(1)} async-done(((f32[8,32,128]{2,1,0:T(8,128)}), f32[8,32,128]{2,1,0:T(8,128)S(1)}, u32[]{:S(2)}, u32[]{:S(2)}) %all-to-all-start.3) | async-done | bytes 131104 | tf_op jit(solution)/shard_map/all_to_all | solution.py:320
  69.5 8.5 %all_to_all.42.p_ref = f32[8,32,128]{2,1,0:T(8,128)S(1)} all-to-all(f32[8,32,128]{2,1,0:T(8,128)S(1)} %total.7), channel_id=1, replica_groups=mesh['dp'=64,'tensor'=8] {'tensor'}, dimensions={0} | all-to-all | bytes 262144 | tf_op jit(solution)/shard_map/all_to_all | solution.py:314
  78.1 0.4 q_pieces.1
  78.5 10.8 %all_to_all.43.x_ref = f32[8,4,512]{2,1,0:T(4,128)S(1)} all-to-all(f32[8,4,512]{2,1,0:T(4,128)S(1)} %q_pieces.1), channel_id=1, replica_groups={{0,64,128,192,256,320,384,448},{8,72,136,200,264,328,392,456},{16,80,14..., dimensions={0} | all-to-all | bytes 131072 | tf_op jit(solution)/shard_map/all_to_all | solution.py:317
  89.3 13.3 %all_to_all.44.x_ref = f32[8,4,512]{2,1,0:T(4,128)S(1)} all-to-all(f32[8,4,512]{2,1,0:T(4,128)S(1)} %total.8), channel_id=1, replica_groups={{0,8,16,24,32,40,48,56},{64,72,80,88,96,104,112,120},{128,136,144,152,1..., dimensions={0} | all-to-all | bytes 131072 | tf_op jit(solution)/shard_map/all_to_all | solution.py:320
  102.5 0.6 total.9.after_ref
  103.2 3.4 %all-to-all-start.7 = ((f32[8,4,512]{2,1,0:T(4,128)}), f32[8,4,512]{2,1,0:T(4,128)S(1)}, u32[]{:S(2)}, u32[]{:S(2)}) async-start(f32[8,4,512]{2,1,0:T(4,128)} %total.9.after_ref), calls=%async_computation.7 | async-start | bytes 131072 | tf_op jit(solution)/shard_map/all_to_all | solution.py:317
  106.5 4.0 %basis.1 = (f32[32,32]{1,0:T(8,128)S(1)}, f32[32,1024]{1,0:T(8,128)}, bf16[1024,128]{1,0:T(8,128)(2,1)S(1)}) custom-call(f32[8,32,128]{2,1,0:T(8,128)S(1)} %all_to_all.42.p_ref, f32[8,4,512]{2,1,0:T(4,128)} %total.9.after_ref), custom_call_target="tpu_custom_call" | custom-call | flops 4000000000 | bytes 4000000 | tf_op jit(solution)/shard_map/basis/pallas_call | solution.py:218
  110.5 4.3 %all-to-all-done.7.refs_0_ = f32[8,4,512]{2,1,0:T(4,128)S(1)} async-done(((f32[8,4,512]{2,1,0:T(4,128)}), f32[8,4,512]{2,1,0:T(4,128)S(1)}, u32[]{:S(2)}, u32[]{:S(2)}) %all-to-all-start.7) | async-done | bytes 65568 | tf_op jit(solution)/shard_map/all_to_all | solution.py:317
  114.8 1.4 %residual.1 = (bf16[1024,512]{1,0:T(8,128)(2,1)}, f32[32,512]{1,0:T(8,128)}) custom-call(f32[8,4,512]{2,1,0:T(4,128)S(1)} %all-to-all-done.7.refs_0_, f32[32,32]{1,0:T(8,128)S(1)} %get-tuple-element.12.refs_1_, bf16[1024,128]{1,0:T(8,128)(2,1)S(1)} %get-tuple-element.13.refs_2_, bf16[1024,512]{1,0:T(8,128)(2,1)S(1)} %get-tuple-element.10.refs_0_.hi_ref.refs_3_, ...), custom_call_target="tpu_custom_call" | custom-call | tf_op jit(solution)/shard_map/residual/pallas_call | solution.py:265
  (3 shorter events, 0.0 us)
Async XLA Ops:
  7.2 20.2 %copy-start.1 = (bf16[256,1024]{1,0:T(8,128)(2,1)S(1)}, bf16[256,1024]{1,0:T(8,128)(2,1)}, u32[]{:S(2)}) copy-start(bf16[256,1024]{1,0:T(8,128)(2,1)} %acts_ref.1) | copy-start | bytes 1572868
  7.2 53.3 %copy-start.3 = (bf16[1,1024,512]{2,1,0:T(8,128)(2,1)S(1)}, bf16[1,1024,512]{2,1,0:T(8,128)(2,1)}, u32[]{:S(2)}) copy-start(bf16[1,1024,512]{2,1,0:T(8,128)(2,1)} %param.6) | copy-start | bytes 3145732
  7.2 53.3 %all-gather.2.cloned.1.call-start = ((), (), s32[]{:S(2)}) async-start(), calls=%async_computation.8 | async-start | bytes 4718592 | tf_op jit(solution)/shard_map/all_gather | solution.py:324
  12.1 15.3 %all-to-all-start = ((f32[8,32,256]{2,1,0:T(8,128)}), f32[8,32,256]{2,1,0:T(8,128)S(1)}, u32[]{:S(2)}, u32[]{:S(2)}) async-start(f32[8,32,256]{2,1,0:T(8,128)} %y_chunks.1), calls=%async_computation | async-start | bytes 524288 | tf_op jit(solution)/shard_map/all_to_all | solution.py:314
  21.3 1.2 copy-start.2
  22.5 0.8 copy-start.4
  49.9 19.7 %all-to-all-start.3 = ((f32[8,32,128]{2,1,0:T(8,128)}), f32[8,32,128]{2,1,0:T(8,128)S(1)}, u32[]{:S(2)}, u32[]{:S(2)}) async-start(f32[8,32,128]{2,1,0:T(8,128)} %total.6.after_ref), calls=%async_computation.3 | async-start | bytes 262144 | tf_op jit(solution)/shard_map/all_to_all | solution.py:320
  60.5 1.6 %copy-start = (bf16[2048,512]{1,0:T(8,128)(2,1)S(1)}, bf16[2048,512]{1,0:T(8,128)(2,1)}, u32[]{:S(2)}) copy-start(bf16[2048,512]{1,0:T(8,128)(2,1)} %g_ref.3) | copy-start | bytes 6291460
  62.1 2.2 %copy-start.5 = (bf16[2048,1024]{1,0:T(8,128)(2,1)S(1)}, bf16[2048,1024]{1,0:T(8,128)(2,1)}, u32[]{:S(2)}) copy-start(bf16[2048,1024]{1,0:T(8,128)(2,1)} %all-gather.2.cloned.1.call-done.a_ref) | copy-start | bytes 12582916
  103.2 11.7 %all-to-all-start.7 = ((f32[8,4,512]{2,1,0:T(4,128)}), f32[8,4,512]{2,1,0:T(4,128)S(1)}, u32[]{:S(2)}, u32[]{:S(2)}) async-start(f32[8,4,512]{2,1,0:T(4,128)} %total.9.after_ref), calls=%async_computation.7 | async-start | bytes 131072 | tf_op jit(solution)/shard_map/all_to_all | solution.py:317
Sparse Core Ops, SparseCore 0:
  10.2 42.5 all-gather.1

commit v5 on v4

--- a/solution.py
+++ b/solution.py
@@ -37,23 +37,30 @@
 
 def y_kernel(q_ref, g_ref, out_ref, q_buf, g_buf, y_buf, q_sem, g_sems, y_sems):
     n, _, rows = out_ref.shape
+    steps = g_sems.shape[0]
+    block = g_ref.shape[0] // steps
     q_copy = pltpu.make_async_copy(q_ref, q_buf, q_sem)
     q_copy.start()
     loads, stores = [], []
-    for s in range(n):
-        span = pl.ds(s * rows, rows)
+    for i in range(steps):
+        span = pl.ds(i * block, block)
         loads.append(
-            pltpu.make_async_copy(g_ref.at[span, :], g_buf.at[span, :], g_sems.at[s])
+            pltpu.make_async_copy(g_ref.at[span, :], g_buf.at[span, :], g_sems.at[i])
         )
-        stores.append(pltpu.make_async_copy(y_buf.at[s], out_ref.at[s], y_sems.at[s]))
-        loads[s].start()
+        loads[i].start()
     q_copy.wait()
-    for s in range(n):
-        loads[s].wait()
-        y_buf[s] = dot(q_buf[...], g_buf[s * rows : (s + 1) * rows, :], 1, 1)
-        stores[s].start()
-    for s in range(n):
-        stores[s].wait()
+    for i in range(steps):
+        loads[i].wait()
+        y = dot(q_buf[...], g_buf[i * block : (i + 1) * block, :], 1, 1)
+        for k in range(block // rows):
+            s = i * (block // rows) + k
+            y_buf[s] = y[:, k * rows : (k + 1) * rows]
+            stores.append(
+                pltpu.make_async_copy(y_buf.at[s], out_ref.at[s], y_sems.at[s])
+            )
+            stores[s].start()
+    for store in stores:
+        store.wait()
 
 
 def y_chunks(q_t, grads, n):
@@ -69,7 +76,7 @@
             pltpu.VMEM(grads.shape, BF16),
             pltpu.VMEM((n, rank, rows), F32),
             pltpu.SemaphoreType.DMA,
-            pltpu.SemaphoreType.DMA((n,)),
+            pltpu.SemaphoreType.DMA((2,)),
             pltpu.SemaphoreType.DMA((n,)),
         ],
         compiler_params=STREAM,
@@ -282,8 +289,7 @@
     )(q_all, inverse, stack, hi, lo)
 
 
-def total_kernel(x_ref, *refs):
-    out_ref = refs[-1]
+def total_kernel(x_ref, out_ref):
     total = x_ref[0]
     for s in range(1, x_ref.shape[0]):
         total = total + x_ref[s]
@@ -291,16 +297,16 @@
         out_ref[s] = total
 
 
-def total_for(x, n, *after):
+def total_for(x, n):
     return pl.pallas_call(
         total_kernel,
-        in_specs=[VMEM] + [ANY] * len(after),
+        in_specs=[VMEM],
         out_specs=VMEM,
         out_shape=jax.ShapeDtypeStruct((n,) + x.shape[1:], F32),
         compiler_params=PARAMS,
         cost_estimate=cost(x.size, 4 * x.size),
         name="total",
-    )(x, *after)
+    )(x)
 
 
 def per_device(acts, grads_out, error_buffer, prior_q):
@@ -326,8 +332,9 @@
     y_all = over_tensor(y_chunks(q_t, grads_out, tensor))
     p_terms = over_tensor(p_chunks(y_all, acts, error_term(q_t, error)))
     p_row = total_for(over_y(total_for(p_terms, side)), side)
-    hi, lo = merged_parts(acts_all, grads_out, error, p_row)
-    p_all = over_tensor(total_for(over_z(p_row), tensor, hi))
+    p_last = total_for(over_z(p_row), tensor)
+    p_all = over_tensor(p_last)
+    hi, lo = merged_parts(acts_all, grads_out, error, p_last)
 
     pieces = q_pieces(p_all, hi, lo, side)
     q_sum = total_for(over_z(total_for(over_y(pieces), side)), side)

time: 124 us -> 123 us (level)
  blocking collectives: 54.1 us -> 62.3 us
  starting transfers between devices: 23.2 us -> 17.5 us
  waiting for transfers between devices: 10.8 us -> 8.72 us
  Pallas kernels: 15.1 us -> 13.8 us
    all_to_all x1 -> x2, blocking collectives: 13.3 us -> 29.8 us  [over_z(): return lax.all_to_all(x, 'dp', 0, 0, axis_index_groups=along_z)]
    all_to_all x1 -> x0, starting transfers between devices: 10.6 us -> none  [over_z(): return lax.all_to_all(x, 'dp', 0, 0, axis_index_groups=along_z)]
    all_to_all x2 -> x1, blocking collectives: 18.6 us -> 9.96 us  [over_tensor(): return lax.all_to_all(x, 'tensor', 0, 0)]
    all_to_all x1 -> x2, starting transfers between devices: 9.24 us -> 14.1 us  [over_tensor(): return lax.all_to_all(x, 'tensor', 0, 0)]
    all_to_all x1 -> x0, waiting for transfers between devices: 2.1 us -> none  [over_z(): return lax.all_to_all(x, 'dp', 0, 0, axis_index_groups=along_z)]
    pallas_call x1, Pallas kernels: 4.13 us -> 2.78 us  [y_chunks(): pl.pallas_call(y_kernel, in_specs=[HBM, HBM], out_specs=HBM, out_shape=ja...]
    all_to_all x1 -> x2, waiting for transfers between devices: 3.73 us -> 3.73 us  [over_tensor(): return lax.all_to_all(x, 'tensor', 0, 0)]
  transfers between devices with their start and end apart: 4 -> 4, of which waited for: 3 -> 2; matrix products, arithmetic and copies ran while one was open for 0% -> 0% of each run, Pallas kernels for 10% -> 9%
where the time goes in v5:
time: 123 us; the launch traced here: 122 us
  blocking collectives  62.3 us (51%)
  starting transfers between devices  17.5 us (14%)
  between operations  14.1 us (11%)
  Pallas kernels  13.8 us (11%)
  waiting for transfers between devices  8.72 us (7%)
  local copies, waits for them, and re-layouts  5.77 us (5%)
    all_to_all x2, blocking collectives, over_z(): return lax.all_to_all(x, 'dp', 0, 0, axis_index_groups=along_z)  29.8 us
    all_to_all x2, blocking collectives, over_y(): return lax.all_to_all(x, 'dp', 0, 0, axis_index_groups=along_y)  22.5 us
    all_to_all x2, starting transfers between devices, over_tensor(): return lax.all_to_all(x, 'tensor', 0, 0)  14.1 us
    all_to_all x1, blocking collectives, over_tensor(): return lax.all_to_all(x, 'tensor', 0, 0)  9.96 us
    unnamed x12, local copies, waits for them, and re-layouts  5.77 us
    all_to_all x1, waiting for transfers between devices, over_y(): return lax.all_to_all(x, 'dp', 0, 0, axis_index_groups=along_y)  4.31 us
    pallas_call x1, Pallas kernels, basis_of(): pl.pallas_call(basis_kernel, in_specs=[VMEM, ANY], out_specs=[VMEM] * 3,...  3.99 us
    all_to_all x2, waiting for transfers between devices, over_tensor(): return lax.all_to_all(x, 'tensor', 0, 0)  3.73 us
  transfers between devices with their start and end apart: 4, of which 2 were waited for; matrix products, arithmetic and copies ran while one was open for 0% of the time, Pallas kernels for 9%

profile of v5, /device:TPU:2, one launch (start us, length us, event | category | flops | bytes accessed | tf_op | source)
XLA Modules:
  0.0 122.1 jit_solution(7969337343142479487)
XLA Ops:
  7.2 0.0 copy-start.1
  7.2 0.0 copy-start.3
  7.2 0.0 all-gather.2.cloned.1.call-start
  7.2 0.7 all-gather.2.cloned.1.call-update
  7.9 2.8 %y_chunks.1 = f32[8,32,256]{2,1,0:T(8,128)} custom-call(bf16[32,512]{1,0:T(8,128)(2,1)} %bitcast.7, bf16[2048,512]{1,0:T(8,128)(2,1)} %g_ref.3), custom_call_target="tpu_custom_call" | custom-call | flops 536870912 | bytes 2097152 | tf_op jit(solution)/shard_map/y_chunks/pallas_call | solution.py:69
  10.7 9.2 %all-to-all-start = ((f32[8,32,256]{2,1,0:T(8,128)}), f32[8,32,256]{2,1,0:T(8,128)S(1)}, u32[]{:S(2)}, u32[]{:S(2)}) async-start(f32[8,32,256]{2,1,0:T(8,128)} %y_chunks.1), calls=%async_computation | async-start | bytes 524288 | tf_op jit(solution)/shard_map/all_to_all | solution.py:320
  20.0 0.0 copy-start.2
  20.0 1.2 %copy-done.2 = bf16[1,1024,512]{2,1,0:T(8,128)(2,1)S(1)} copy-done((bf16[1,1024,512]{2,1,0:T(8,128)(2,1)S(1)}, bf16[1,1024,512]{2,1,0:T(8,128)(2,1)}, u32[]{:S(2)}) %copy-start.2) | copy-done | bytes 1048600
  21.2 0.0 copy-start.4
  21.2 0.8 copy-done.4
  21.9 0.4 error_term.1.e_ref
  22.3 3.7 %all-to-all-done.y_ref = f32[8,32,256]{2,1,0:T(8,128)S(1)} async-done(((f32[8,32,256]{2,1,0:T(8,128)}), f32[8,32,256]{2,1,0:T(8,128)S(1)}, u32[]{:S(2)}, u32[]{:S(2)}) %all-to-all-start) | async-done | bytes 262176 | tf_op jit(solution)/shard_map/all_to_all | solution.py:320
  26.1 0.0 copy-done.1
  26.1 0.2 p_chunks.1
  26.3 10.0 %all_to_all.40.x_ref = f32[8,32,128]{2,1,0:T(8,128)S(1)} all-to-all(f32[8,32,128]{2,1,0:T(8,128)S(1)} %p_chunks.1), channel_id=1, replica_groups=mesh['dp'=64,'tensor'=8] {'tensor'}, dimensions={0} | all-to-all | bytes 262144 | tf_op jit(solution)/shard_map/all_to_all | solution.py:320
  36.2 11.7 %all_to_all.41.x_ref = f32[8,32,128]{2,1,0:T(8,128)S(1)} all-to-all(f32[8,32,128]{2,1,0:T(8,128)S(1)} %total.5), channel_id=1, replica_groups={{0,64,128,192,256,320,384,448},{8,72,136,200,264,328,392,456},{16,80,14..., dimensions={0} | all-to-all | bytes 262144 | tf_op jit(solution)/shard_map/all_to_all | solution.py:323
  48.0 19.1 %all_to_all.42.x_ref = f32[8,32,128]{2,1,0:T(8,128)S(1)} all-to-all(f32[8,32,128]{2,1,0:T(8,128)S(1)} %total.6), channel_id=1, replica_groups={{0,8,16,24,32,40,48,56},{64,72,80,88,96,104,112,120},{128,136,144,152,1..., dimensions={0} | all-to-all | bytes 262144 | tf_op jit(solution)/shard_map/all_to_all | solution.py:326
  67.1 0.7 total.7.after_ref
  67.8 4.8 %all-to-all-start.4 = ((f32[8,32,128]{2,1,0:T(8,128)}), f32[8,32,128]{2,1,0:T(8,128)S(1)}, u32[]{:S(2)}, u32[]{:S(2)}) async-start(f32[8,32,128]{2,1,0:T(8,128)} %total.7.after_ref), calls=%async_computation.4 | async-start | bytes 262144 | tf_op jit(solution)/shard_map/all_to_all | solution.py:320
  72.6 0.0 all-gather.2.cloned.1.call-done.a_ref
  72.6 0.0 copy-done.3
  72.6 0.0 copy-start
  72.6 1.6 %copy-done = bf16[2048,512]{1,0:T(8,128)(2,1)S(1)} copy-done((bf16[2048,512]{1,0:T(8,128)(2,1)S(1)}, bf16[2048,512]{1,0:T(8,128)(2,1)}, u32[]{:S(2)}) %copy-start) | copy-done | bytes 2097176
  74.2 0.0 copy-start.5
  74.2 2.2 %copy-done.5 = bf16[2048,1024]{1,0:T(8,128)(2,1)S(1)} copy-done((bf16[2048,1024]{1,0:T(8,128)(2,1)S(1)}, bf16[2048,1024]{1,0:T(8,128)(2,1)}, u32[]{:S(2)}) %copy-start.5) | copy-done | bytes 4194328
  76.4 3.2 %merged_parts.1 = (bf16[1024,512]{1,0:T(8,128)(2,1)S(1)}, bf16[1024,512]{1,0:T(8,128)(2,1)S(1)}) custom-call(bf16[2048,1024]{1,0:T(8,128)(2,1)S(1)} %copy-done.5, bf16[2048,512]{1,0:T(8,128)(2,1)S(1)} %copy-done, bf16[1024,512]{1,0:T(8,128)(2,1)S(1)} %bitcast.6, f32[8,32,128]{2,1,0:T(8,128)} %total.7.after_ref), custom_call_target="tpu_custom_call" | custom-call | flops 2147483648 | bytes 6291456 | tf_op jit(solution)/shard_map/merged_parts/pallas_call | solution.py:147
  79.6 0.0 all-to-all-done.4.p_ref
  79.6 0.4 q_pieces.1
  80.0 10.8 %all_to_all.43.x_ref = f32[8,4,512]{2,1,0:T(4,128)S(1)} all-to-all(f32[8,4,512]{2,1,0:T(4,128)S(1)} %q_pieces.1), channel_id=1, replica_groups={{0,64,128,192,256,320,384,448},{8,72,136,200,264,328,392,456},{16,80,14..., dimensions={0} | all-to-all | bytes 131072 | tf_op jit(solution)/shard_map/all_to_all | solution.py:323
  90.8 10.8 %all_to_all.44.x_ref = f32[8,4,512]{2,1,0:T(4,128)S(1)} all-to-all(f32[8,4,512]{2,1,0:T(4,128)S(1)} %total.8), channel_id=1, replica_groups={{0,8,16,24,32,40,48,56},{64,72,80,88,96,104,112,120},{128,136,144,152,1..., dimensions={0} | all-to-all | bytes 131072 | tf_op jit(solution)/shard_map/all_to_all | solution.py:326
  101.5 0.6 total.9.after_ref
  102.2 3.4 %all-to-all-start.7 = ((f32[8,4,512]{2,1,0:T(4,128)}), f32[8,4,512]{2,1,0:T(4,128)S(1)}, u32[]{:S(2)}, u32[]{:S(2)}) async-start(f32[8,4,512]{2,1,0:T(4,128)} %total.9.after_ref), calls=%async_computation.7 | async-start | bytes 131072 | tf_op jit(solution)/shard_map/all_to_all | solution.py:323
  105.5 4.0 %basis.1 = (f32[32,32]{1,0:T(8,128)S(1)}, f32[32,1024]{1,0:T(8,128)}, bf16[1024,128]{1,0:T(8,128)(2,1)S(1)}) custom-call(f32[8,32,128]{2,1,0:T(8,128)S(1)} %all-to-all-done.4.p_ref, f32[8,4,512]{2,1,0:T(4,128)} %total.9.after_ref), custom_call_target="tpu_custom_call" | custom-call | flops 4000000000 | bytes 4000000 | tf_op jit(solution)/shard_map/basis/pallas_call | solution.py:225
  109.5 4.3 %all-to-all-done.7.refs_0_ = f32[8,4,512]{2,1,0:T(4,128)S(1)} async-done(((f32[8,4,512]{2,1,0:T(4,128)}), f32[8,4,512]{2,1,0:T(4,128)S(1)}, u32[]{:S(2)}, u32[]{:S(2)}) %all-to-all-start.7) | async-done | bytes 65568 | tf_op jit(solution)/shard_map/all_to_all | solution.py:323
  113.8 1.4 %residual.1 = (bf16[1024,512]{1,0:T(8,128)(2,1)}, f32[32,512]{1,0:T(8,128)}) custom-call(f32[8,4,512]{2,1,0:T(4,128)S(1)} %all-to-all-done.7.refs_0_, f32[32,32]{1,0:T(8,128)S(1)} %get-tuple-element.12.refs_1_, bf16[1024,128]{1,0:T(8,128)(2,1)S(1)} %get-tuple-element.13.refs_2_, bf16[1024,512]{1,0:T(8,128)(2,1)S(1)} %get-tuple-element.10.hi_ref.refs_3_, ...), custom_call_target="tpu_custom_call" | custom-call | tf_op jit(solution)/shard_map/residual/pallas_call | solution.py:272
  (3 shorter events, 0.0 us)
Async XLA Ops:
  7.2 18.9 %copy-start.1 = (bf16[256,1024]{1,0:T(8,128)(2,1)S(1)}, bf16[256,1024]{1,0:T(8,128)(2,1)}, u32[]{:S(2)}) copy-start(bf16[256,1024]{1,0:T(8,128)(2,1)} %acts_ref.1) | copy-start | bytes 1572868
  7.2 65.4 %copy-start.3 = (bf16[1,1024,512]{2,1,0:T(8,128)(2,1)S(1)}, bf16[1,1024,512]{2,1,0:T(8,128)(2,1)}, u32[]{:S(2)}) copy-start(bf16[1,1024,512]{2,1,0:T(8,128)(2,1)} %param.6) | copy-start | bytes 3145732
  7.2 65.4 %all-gather.2.cloned.1.call-start = ((), (), s32[]{:S(2)}) async-start(), calls=%async_computation.8 | async-start | bytes 4718592 | tf_op jit(solution)/shard_map/all_gather | solution.py:330
  10.7 15.3 %all-to-all-start = ((f32[8,32,256]{2,1,0:T(8,128)}), f32[8,32,256]{2,1,0:T(8,128)S(1)}, u32[]{:S(2)}, u32[]{:S(2)}) async-start(f32[8,32,256]{2,1,0:T(8,128)} %y_chunks.1), calls=%async_computation | async-start | bytes 524288 | tf_op jit(solution)/shard_map/all_to_all | solution.py:320
  20.0 1.2 %copy-start.2 = (bf16[1,1024,512]{2,1,0:T(8,128)(2,1)S(1)}, bf16[1,1024,512]{2,1,0:T(8,128)(2,1)}, u32[]{:S(2)}) copy-start(bf16[1,1024,512]{2,1,0:T(8,128)(2,1)} %param.6) | copy-start | bytes 3145732
  21.2 0.8 copy-start.4
  67.8 11.8 %all-to-all-start.4 = ((f32[8,32,128]{2,1,0:T(8,128)}), f32[8,32,128]{2,1,0:T(8,128)S(1)}, u32[]{:S(2)}, u32[]{:S(2)}) async-start(f32[8,32,128]{2,1,0:T(8,128)} %total.7.after_ref), calls=%async_computation.4 | async-start | bytes 262144 | tf_op jit(solution)/shard_map/all_to_all | solution.py:320
  72.6 1.6 %copy-start = (bf16[2048,512]{1,0:T(8,128)(2,1)S(1)}, bf16[2048,512]{1,0:T(8,128)(2,1)}, u32[]{:S(2)}) copy-start(bf16[2048,512]{1,0:T(8,128)(2,1)} %g_ref.3) | copy-start | bytes 6291460
  74.2 2.2 %copy-start.5 = (bf16[2048,1024]{1,0:T(8,128)(2,1)S(1)}, bf16[2048,1024]{1,0:T(8,128)(2,1)}, u32[]{:S(2)}) copy-start(bf16[2048,1024]{1,0:T(8,128)(2,1)} %all-gather.2.cloned.1.call-done.a_ref) | copy-start | bytes 12582916
  102.2 11.7 %all-to-all-start.7 = ((f32[8,4,512]{2,1,0:T(4,128)}), f32[8,4,512]{2,1,0:T(4,128)S(1)}, u32[]{:S(2)}, u32[]{:S(2)}) async-start(f32[8,4,512]{2,1,0:T(4,128)} %total.9.after_ref), calls=%async_computation.7 | async-start | bytes 131072 | tf_op jit(solution)/shard_map/all_to_all | solution.py:323
Sparse Core Ops, SparseCore 0:
  10.2 42.4 all-gather.1

commit v6 on v5

--- a/solution.py
+++ b/solution.py
@@ -127,15 +127,34 @@
     )(y_all, acts, e_term)
 
 
-def merged_kernel(a_ref, g_ref, e_ref, after_ref, hi_ref, lo_ref):
+def merged_kernel(a_ref, g_ref, e_ref, after_ref, hi_ref, lo_ref, a_buf, g_buf, e_buf, a_sems, g_sem, e_sem):
     del after_ref
-    block = 256
-
-    @pl.loop(0, a_ref.shape[1] // block)
+    blocks, _, block = a_buf.shape
+
+    def load(i):
+        span = pl.ds(pl.multiple_of(i * block, block), block)
+        return pltpu.make_async_copy(a_ref.at[:, span], a_buf.at[i], a_sems.at[i])
+
+    g_load = pltpu.make_async_copy(g_ref, g_buf, g_sem)
+    e_load = pltpu.make_async_copy(e_ref, e_buf, e_sem)
+    g_load.start()
+    load(0).start()
+    e_load.start()
+    for i in range(1, blocks):
+        load(i).start()
+    g_load.wait()
+
+    @pl.loop(0, blocks)
     def _(i):
+        load(i).wait()
+        grad = dot(a_buf[i], g_buf[...], 0, 0)
+
+        @pl.when(i == 0)
+        def _():
+            e_load.wait()
+
         span = pl.ds(pl.multiple_of(i * block, block), block)
-        merged = dot(a_ref[:, span], g_ref[...], 0, 0) + e_ref[span, :].astype(F32)
-        hi, lo = parts_of(merged, 2)
+        hi, lo = parts_of(grad + e_buf[span, :].astype(F32), 2)
         hi_ref[span, :] = hi
         lo_ref[span, :] = lo
 
@@ -143,16 +162,30 @@
 def merged_parts(acts_all, grads, error, after):
     tokens, width = acts_all.shape
     cols = grads.shape[1]
+    block = 256
+    blocks = width // block
     shape = jax.ShapeDtypeStruct((width, cols), BF16)
+    streamed = [
+        pltpu.with_memory_space_constraint(x, pltpu.HBM)
+        for x in (acts_all, grads, error)
+    ]
     return pl.pallas_call(
         merged_kernel,
-        in_specs=[VMEM, VMEM, VMEM, ANY],
+        in_specs=[HBM, HBM, HBM, ANY],
         out_specs=[VMEM, VMEM],
         out_shape=[shape, shape],
+        scratch_shapes=[
+            pltpu.VMEM((blocks, tokens, block), BF16),
+            pltpu.VMEM(grads.shape, BF16),
+            pltpu.VMEM(error.shape, BF16),
+            pltpu.SemaphoreType.DMA((blocks,)),
+            pltpu.SemaphoreType.DMA,
+            pltpu.SemaphoreType.DMA,
+        ],
         compiler_params=PARAMS,
         cost_estimate=cost(2 * tokens * width * cols, acts_all.size * 2 + grads.size * 2),
         name="merged_parts",
-    )(acts_all, grads, error, after)
+    )(*streamed, after)
 
 
 def q_kernel(p_ref, hi_ref, lo_ref, out_ref):

time: 123 us -> 122 us (level)
  local copies, waits for them, and re-layouts: 5.77 us -> 1.99 us
  Pallas kernels: 13.8 us -> 17.1 us
    unnamed x12 -> x6, local copies, waits for them, and re-layouts: 5.77 us -> 1.99 us
    pallas_call x1, Pallas kernels: 3.17 us -> 6.54 us  [merged_parts(): pl.pallas_call(merged_kernel, in_specs=[HBM, HBM, HBM, ANY], out_specs=[V...]
  transfers between devices with their start and end apart: 4 -> 4, of which waited for: 2 -> 2; matrix products, arithmetic and copies ran while one was open for 0% -> 0% of each run, Pallas kernels for 9% -> 12%
where the time goes in v6:
time: 122 us
  blocking collectives  62.3 us (51%)
  starting transfers between devices  17.5 us (14%)
  Pallas kernels  17.1 us (14%)
  between operations  14.1 us (12%)
  waiting for transfers between devices  8.72 us (7%)
  local copies, waits for them, and re-layouts  1.99 us (2%)
    all_to_all x2, blocking collectives, over_z(): return lax.all_to_all(x, 'dp', 0, 0, axis_index_groups=along_z)  29.8 us
    all_to_all x2, blocking collectives, over_y(): return lax.all_to_all(x, 'dp', 0, 0, axis_index_groups=along_y)  22.5 us
    all_to_all x2, starting transfers between devices, over_tensor(): return lax.all_to_all(x, 'tensor', 0, 0)  14.1 us
    all_to_all x1, blocking collectives, over_tensor(): return lax.all_to_all(x, 'tensor', 0, 0)  9.95 us
    pallas_call x1, Pallas kernels, merged_parts(): pl.pallas_call(merged_kernel, in_specs=[HBM, HBM, HBM, ANY], out_specs=[V...  6.54 us
    all_to_all x1, waiting for transfers between devices, over_y(): return lax.all_to_all(x, 'dp', 0, 0, axis_index_groups=along_y)  4.31 us
    pallas_call x1, Pallas kernels, basis_of(): pl.pallas_call(basis_kernel, in_specs=[VMEM, ANY], out_specs=[VMEM] * 3,...  3.99 us
    all_to_all x2, waiting for transfers between devices, over_tensor(): return lax.all_to_all(x, 'tensor', 0, 0)  3.73 us
  transfers between devices with their start and end apart: 4, of which 2 were waited for; matrix products, arithmetic and copies ran while one was open for 0% of the time, Pallas kernels for 12%

profile of v6, /device:TPU:2, one launch (start us, length us, event | category | flops | bytes accessed | tf_op | source)
XLA Modules:
  0.0 121.7 jit_solution(10398114167032731906)
XLA Ops:
  7.2 0.0 copy-start
  7.2 0.0 all-gather.2.cloned.1.call-start
  7.2 0.7 all-gather.2.cloned.1.call-update
  7.9 2.8 %y_chunks.1 = f32[8,32,256]{2,1,0:T(8,128)} custom-call(bf16[32,512]{1,0:T(8,128)(2,1)} %bitcast.7, bf16[2048,512]{1,0:T(8,128)(2,1)} %g_ref.3), custom_call_target="tpu_custom_call" | custom-call | flops 536870912 | bytes 2097152 | tf_op jit(solution)/shard_map/y_chunks/pallas_call | solution.py:69
  10.7 9.2 %all-to-all-start = ((f32[8,32,256]{2,1,0:T(8,128)}), f32[8,32,256]{2,1,0:T(8,128)S(1)}, u32[]{:S(2)}, u32[]{:S(2)}) async-start(f32[8,32,256]{2,1,0:T(8,128)} %y_chunks.1), calls=%async_computation | async-start | bytes 524288 | tf_op jit(solution)/shard_map/all_to_all | solution.py:353
  19.9 0.0 copy-start.1
  19.9 1.2 %copy-done.1 = bf16[1,1024,512]{2,1,0:T(8,128)(2,1)S(1)} copy-done((bf16[1,1024,512]{2,1,0:T(8,128)(2,1)S(1)}, bf16[1,1024,512]{2,1,0:T(8,128)(2,1)}, u32[]{:S(2)}) %copy-start.1) | copy-done | bytes 1048600
  21.2 0.0 copy-start.2
  21.2 0.8 copy-done.2
  21.9 0.4 error_term.1.e_ref
  22.3 3.7 %all-to-all-done.y_ref = f32[8,32,256]{2,1,0:T(8,128)S(1)} async-done(((f32[8,32,256]{2,1,0:T(8,128)}), f32[8,32,256]{2,1,0:T(8,128)S(1)}, u32[]{:S(2)}, u32[]{:S(2)}) %all-to-all-start) | async-done | bytes 262176 | tf_op jit(solution)/shard_map/all_to_all | solution.py:353
  26.1 0.0 copy-done
  26.1 0.2 p_chunks.1
  26.2 10.0 %all_to_all.40.x_ref = f32[8,32,128]{2,1,0:T(8,128)S(1)} all-to-all(f32[8,32,128]{2,1,0:T(8,128)S(1)} %p_chunks.1), channel_id=1, replica_groups=mesh['dp'=64,'tensor'=8] {'tensor'}, dimensions={0} | all-to-all | bytes 262144 | tf_op jit(solution)/shard_map/all_to_all | solution.py:353
  36.2 11.7 %all_to_all.41.x_ref = f32[8,32,128]{2,1,0:T(8,128)S(1)} all-to-all(f32[8,32,128]{2,1,0:T(8,128)S(1)} %total.5), channel_id=1, replica_groups={{0,64,128,192,256,320,384,448},{8,72,136,200,264,328,392,456},{16,80,14..., dimensions={0} | all-to-all | bytes 262144 | tf_op jit(solution)/shard_map/all_to_all | solution.py:356
  48.0 19.1 %all_to_all.42.x_ref = f32[8,32,128]{2,1,0:T(8,128)S(1)} all-to-all(f32[8,32,128]{2,1,0:T(8,128)S(1)} %total.6), channel_id=1, replica_groups={{0,8,16,24,32,40,48,56},{64,72,80,88,96,104,112,120},{128,136,144,152,1..., dimensions={0} | all-to-all | bytes 262144 | tf_op jit(solution)/shard_map/all_to_all | solution.py:359
  67.1 0.7 total.7.after_ref
  67.7 4.8 %all-to-all-start.4 = ((f32[8,32,128]{2,1,0:T(8,128)}), f32[8,32,128]{2,1,0:T(8,128)S(1)}, u32[]{:S(2)}, u32[]{:S(2)}) async-start(f32[8,32,128]{2,1,0:T(8,128)} %total.7.after_ref), calls=%async_computation.4 | async-start | bytes 262144 | tf_op jit(solution)/shard_map/all_to_all | solution.py:353
  72.6 0.0 all-gather.2.cloned.1.call-done.a_ref
  72.6 6.5 %merged_parts.1 = (bf16[1024,512]{1,0:T(8,128)(2,1)S(1)}, bf16[1024,512]{1,0:T(8,128)(2,1)S(1)}) custom-call(bf16[2048,1024]{1,0:T(8,128)(2,1)} %all-gather.2.cloned.1.call-done.a_ref, bf16[2048,512]{1,0:T(8,128)(2,1)} %g_ref.3, bf16[1024,512]{1,0:T(8,128)(2,1)} %bitcast.5, f32[8,32,128]{2,1,0:T(8,128)} %total.7.after_ref), custom_call_target="tpu_custom_call" | custom-call | flops 2147483648 | bytes 6291456 | tf_op jit(solution)/shard_map/merged_parts/pallas_call | solution.py:172
  79.1 0.0 all-to-all-done.4.p_ref
  79.1 0.4 q_pieces.1
  79.6 10.8 %all_to_all.43.x_ref = f32[8,4,512]{2,1,0:T(4,128)S(1)} all-to-all(f32[8,4,512]{2,1,0:T(4,128)S(1)} %q_pieces.1), channel_id=1, replica_groups={{0,64,128,192,256,320,384,448},{8,72,136,200,264,328,392,456},{16,80,14..., dimensions={0} | all-to-all | bytes 131072 | tf_op jit(solution)/shard_map/all_to_all | solution.py:356
  90.4 10.8 %all_to_all.44.x_ref = f32[8,4,512]{2,1,0:T(4,128)S(1)} all-to-all(f32[8,4,512]{2,1,0:T(4,128)S(1)} %total.8), channel_id=1, replica_groups={{0,8,16,24,32,40,48,56},{64,72,80,88,96,104,112,120},{128,136,144,152,1..., dimensions={0} | all-to-all | bytes 131072 | tf_op jit(solution)/shard_map/all_to_all | solution.py:359
  101.1 0.6 total.9.after_ref
  101.8 3.4 %all-to-all-start.7 = ((f32[8,4,512]{2,1,0:T(4,128)}), f32[8,4,512]{2,1,0:T(4,128)S(1)}, u32[]{:S(2)}, u32[]{:S(2)}) async-start(f32[8,4,512]{2,1,0:T(4,128)} %total.9.after_ref), calls=%async_computation.7 | async-start | bytes 131072 | tf_op jit(solution)/shard_map/all_to_all | solution.py:356
  105.1 4.0 %basis.1 = (f32[32,32]{1,0:T(8,128)S(1)}, f32[32,1024]{1,0:T(8,128)}, bf16[1024,128]{1,0:T(8,128)(2,1)S(1)}) custom-call(f32[8,32,128]{2,1,0:T(8,128)S(1)} %all-to-all-done.4.p_ref, f32[8,4,512]{2,1,0:T(4,128)} %total.9.after_ref), custom_call_target="tpu_custom_call" | custom-call | flops 4000000000 | bytes 4000000 | tf_op jit(solution)/shard_map/basis/pallas_call | solution.py:258
  109.1 4.3 %all-to-all-done.7.refs_0_ = f32[8,4,512]{2,1,0:T(4,128)S(1)} async-done(((f32[8,4,512]{2,1,0:T(4,128)}), f32[8,4,512]{2,1,0:T(4,128)S(1)}, u32[]{:S(2)}, u32[]{:S(2)}) %all-to-all-start.7) | async-done | bytes 65568 | tf_op jit(solution)/shard_map/all_to_all | solution.py:356
  113.4 1.4 %residual.1 = (bf16[1024,512]{1,0:T(8,128)(2,1)}, f32[32,512]{1,0:T(8,128)}) custom-call(f32[8,4,512]{2,1,0:T(4,128)S(1)} %all-to-all-done.7.refs_0_, f32[32,32]{1,0:T(8,128)S(1)} %get-tuple-element.12.refs_1_, bf16[1024,128]{1,0:T(8,128)(2,1)S(1)} %get-tuple-element.13.refs_2_, bf16[1024,512]{1,0:T(8,128)(2,1)S(1)} %get-tuple-element.10.hi_ref.refs_3_, ...), custom_call_target="tpu_custom_call" | custom-call | tf_op jit(solution)/shard_map/residual/pallas_call | solution.py:305
  (3 shorter events, 0.0 us)
Async XLA Ops:
  7.2 18.9 %copy-start = (bf16[256,1024]{1,0:T(8,128)(2,1)S(1)}, bf16[256,1024]{1,0:T(8,128)(2,1)}, u32[]{:S(2)}) copy-start(bf16[256,1024]{1,0:T(8,128)(2,1)} %acts_ref.1) | copy-start | bytes 1572868
  7.2 65.4 %all-gather.2.cloned.1.call-start = ((), (), s32[]{:S(2)}) async-start(), calls=%async_computation.8 | async-start | bytes 4718592 | tf_op jit(solution)/shard_map/all_gather | solution.py:363
  10.7 15.3 %all-to-all-start = ((f32[8,32,256]{2,1,0:T(8,128)}), f32[8,32,256]{2,1,0:T(8,128)S(1)}, u32[]{:S(2)}, u32[]{:S(2)}) async-start(f32[8,32,256]{2,1,0:T(8,128)} %y_chunks.1), calls=%async_computation | async-start | bytes 524288 | tf_op jit(solution)/shard_map/all_to_all | solution.py:353
  19.9 1.2 %copy-start.1 = (bf16[1,1024,512]{2,1,0:T(8,128)(2,1)S(1)}, bf16[1,1024,512]{2,1,0:T(8,128)(2,1)}, u32[]{:S(2)}) copy-start(bf16[1,1024,512]{2,1,0:T(8,128)(2,1)} %param.6) | copy-start | bytes 3145732
  21.2 0.8 copy-start.2
  67.7 11.4 %all-to-all-start.4 = ((f32[8,32,128]{2,1,0:T(8,128)}), f32[8,32,128]{2,1,0:T(8,128)S(1)}, u32[]{:S(2)}, u32[]{:S(2)}) async-start(f32[8,32,128]{2,1,0:T(8,128)} %total.7.after_ref), calls=%async_computation.4 | async-start | bytes 262144 | tf_op jit(solution)/shard_map/all_to_all | solution.py:353
  101.8 11.7 %all-to-all-start.7 = ((f32[8,4,512]{2,1,0:T(4,128)}), f32[8,4,512]{2,1,0:T(4,128)S(1)}, u32[]{:S(2)}, u32[]{:S(2)}) async-start(f32[8,4,512]{2,1,0:T(4,128)} %total.9.after_ref), calls=%async_computation.7 | async-start | bytes 131072 | tf_op jit(solution)/shard_map/all_to_all | solution.py:356
Sparse Core Ops, SparseCore 0:
  10.2 42.3 all-gather.1

commit v7 on v5

--- a/solution.py
+++ b/solution.py
@@ -127,15 +127,28 @@
     )(y_all, acts, e_term)
 
 
-def merged_kernel(a_ref, g_ref, e_ref, after_ref, hi_ref, lo_ref):
+def merged_kernel(a_ref, g_ref, e_ref, after_ref, hi_ref, lo_ref, a_buf, e_buf, a_sems, e_sems):
     del after_ref
-    block = 256
-
-    @pl.loop(0, a_ref.shape[1] // block)
-    def _(i):
-        span = pl.ds(pl.multiple_of(i * block, block), block)
-        merged = dot(a_ref[:, span], g_ref[...], 0, 0) + e_ref[span, :].astype(F32)
+    blocks, _, block = a_buf.shape
+
+    def loads(i):
+        span = pl.ds(i * block, block)
+        return (
+            pltpu.make_async_copy(a_ref.at[:, span], a_buf.at[i], a_sems.at[i]),
+            pltpu.make_async_copy(e_ref.at[span, :], e_buf.at[i], e_sems.at[i]),
+        )
+
+    for load in loads(0):
+        load.start()
+    for i in range(blocks):
+        for load in loads(i):
+            load.wait()
+        if i + 1 < blocks:
+            for load in loads(i + 1):
+                load.start()
+        merged = dot(a_buf[i], g_ref[...], 0, 0) + e_buf[i].astype(F32)
         hi, lo = parts_of(merged, 2)
+        span = slice(i * block, (i + 1) * block)
         hi_ref[span, :] = hi
         lo_ref[span, :] = lo
 
@@ -143,16 +156,29 @@
 def merged_parts(acts_all, grads, error, after):
     tokens, width = acts_all.shape
     cols = grads.shape[1]
+    blocks = 2
+    block = width // blocks
     shape = jax.ShapeDtypeStruct((width, cols), BF16)
     return pl.pallas_call(
         merged_kernel,
-        in_specs=[VMEM, VMEM, VMEM, ANY],
+        in_specs=[HBM, VMEM, HBM, ANY],
         out_specs=[VMEM, VMEM],
         out_shape=[shape, shape],
+        scratch_shapes=[
+            pltpu.VMEM((blocks, tokens, block), BF16),
+            pltpu.VMEM((blocks, block, cols), BF16),
+            pltpu.SemaphoreType.DMA((blocks,)),
+            pltpu.SemaphoreType.DMA((blocks,)),
+        ],
         compiler_params=PARAMS,
         cost_estimate=cost(2 * tokens * width * cols, acts_all.size * 2 + grads.size * 2),
         name="merged_parts",
-    )(acts_all, grads, error, after)
+    )(
+        pltpu.with_memory_space_constraint(acts_all, pltpu.HBM),
+        grads,
+        pltpu.with_memory_space_constraint(error, pltpu.HBM),
+        after,
+    )
 
 
 def q_kernel(p_ref, hi_ref, lo_ref, out_ref):

time: 123 us -> 122 us (level)
  local copies, waits for them, and re-layouts: 5.77 us -> 3.58 us
  Pallas kernels: 13.8 us -> 15.3 us
    unnamed x12 -> x8, local copies, waits for them, and re-layouts: 5.77 us -> 3.58 us
    pallas_call x1, Pallas kernels: 3.17 us -> 4.7 us  [merged_parts(): pl.pallas_call(merged_kernel, in_specs=[HBM, VMEM, HBM, ANY], out_specs=[...]
  transfers between devices with their start and end apart: 4 -> 4, of which waited for: 2 -> 2; matrix products, arithmetic and copies ran while one was open for 0% -> 0% of each run, Pallas kernels for 9% -> 11%
where the time goes in v7:
time: 122 us; the launch traced here: 121 us
  blocking collectives  62.3 us (51%)
  starting transfers between devices  17.5 us (14%)
  Pallas kernels  15.3 us (13%)
  between operations  14.1 us (12%)
  waiting for transfers between devices  8.72 us (7%)
  local copies, waits for them, and re-layouts  3.58 us (3%)
    all_to_all x2, blocking collectives, over_z(): return lax.all_to_all(x, 'dp', 0, 0, axis_index_groups=along_z)  29.8 us
    all_to_all x2, blocking collectives, over_y(): return lax.all_to_all(x, 'dp', 0, 0, axis_index_groups=along_y)  22.5 us
    all_to_all x2, starting transfers between devices, over_tensor(): return lax.all_to_all(x, 'tensor', 0, 0)  14.1 us
    all_to_all x1, blocking collectives, over_tensor(): return lax.all_to_all(x, 'tensor', 0, 0)  9.95 us
    pallas_call x1, Pallas kernels, merged_parts(): pl.pallas_call(merged_kernel, in_specs=[HBM, VMEM, HBM, ANY], out_specs=[...  4.7 us
    all_to_all x1, waiting for transfers between devices, over_y(): return lax.all_to_all(x, 'dp', 0, 0, axis_index_groups=along_y)  4.31 us
    pallas_call x1, Pallas kernels, basis_of(): pl.pallas_call(basis_kernel, in_specs=[VMEM, ANY], out_specs=[VMEM] * 3,...  3.99 us
    all_to_all x2, waiting for transfers between devices, over_tensor(): return lax.all_to_all(x, 'tensor', 0, 0)  3.73 us
  transfers between devices with their start and end apart: 4, of which 2 were waited for; matrix products, arithmetic and copies ran while one was open for 0% of the time, Pallas kernels for 11%

profile of v7, /device:TPU:2, one launch (start us, length us, event | category | flops | bytes accessed | tf_op | source)
XLA Modules:
  0.0 121.5 jit_solution(2279556648870163165)
XLA Ops:
  7.2 0.0 copy-start.1
  7.2 0.0 all-gather.2.cloned.1.call-start
  7.2 0.7 all-gather.2.cloned.1.call-update
  7.9 2.8 %y_chunks.1 = f32[8,32,256]{2,1,0:T(8,128)} custom-call(bf16[32,512]{1,0:T(8,128)(2,1)} %bitcast.7, bf16[2048,512]{1,0:T(8,128)(2,1)} %g_ref.3), custom_call_target="tpu_custom_call" | custom-call | flops 536870912 | bytes 2097152 | tf_op jit(solution)/shard_map/y_chunks/pallas_call | solution.py:69
  10.7 9.2 %all-to-all-start = ((f32[8,32,256]{2,1,0:T(8,128)}), f32[8,32,256]{2,1,0:T(8,128)S(1)}, u32[]{:S(2)}, u32[]{:S(2)}) async-start(f32[8,32,256]{2,1,0:T(8,128)} %y_chunks.1), calls=%async_computation | async-start | bytes 524288 | tf_op jit(solution)/shard_map/all_to_all | solution.py:346
  19.9 0.0 copy-start.2
  19.9 1.2 %copy-done.2 = bf16[1,1024,512]{2,1,0:T(8,128)(2,1)S(1)} copy-done((bf16[1,1024,512]{2,1,0:T(8,128)(2,1)S(1)}, bf16[1,1024,512]{2,1,0:T(8,128)(2,1)}, u32[]{:S(2)}) %copy-start.2) | copy-done | bytes 1048600
  21.2 0.0 copy-start.3
  21.2 0.8 copy-done.3
  21.9 0.4 error_term.1.e_ref
  22.3 3.7 %all-to-all-done.y_ref = f32[8,32,256]{2,1,0:T(8,128)S(1)} async-done(((f32[8,32,256]{2,1,0:T(8,128)}), f32[8,32,256]{2,1,0:T(8,128)S(1)}, u32[]{:S(2)}, u32[]{:S(2)}) %all-to-all-start) | async-done | bytes 262176 | tf_op jit(solution)/shard_map/all_to_all | solution.py:346
  26.1 0.0 copy-done.1
  26.1 0.2 p_chunks.1
  26.2 10.0 %all_to_all.40.x_ref = f32[8,32,128]{2,1,0:T(8,128)S(1)} all-to-all(f32[8,32,128]{2,1,0:T(8,128)S(1)} %p_chunks.1), channel_id=1, replica_groups=mesh['dp'=64,'tensor'=8] {'tensor'}, dimensions={0} | all-to-all | bytes 262144 | tf_op jit(solution)/shard_map/all_to_all | solution.py:346
  36.2 11.7 %all_to_all.41.x_ref = f32[8,32,128]{2,1,0:T(8,128)S(1)} all-to-all(f32[8,32,128]{2,1,0:T(8,128)S(1)} %total.5), channel_id=1, replica_groups={{0,64,128,192,256,320,384,448},{8,72,136,200,264,328,392,456},{16,80,14..., dimensions={0} | all-to-all | bytes 262144 | tf_op jit(solution)/shard_map/all_to_all | solution.py:349
  48.0 19.1 %all_to_all.42.x_ref = f32[8,32,128]{2,1,0:T(8,128)S(1)} all-to-all(f32[8,32,128]{2,1,0:T(8,128)S(1)} %total.6), channel_id=1, replica_groups={{0,8,16,24,32,40,48,56},{64,72,80,88,96,104,112,120},{128,136,144,152,1..., dimensions={0} | all-to-all | bytes 262144 | tf_op jit(solution)/shard_map/all_to_all | solution.py:352
  67.1 0.7 total.7.after_ref
  67.7 4.8 %all-to-all-start.4 = ((f32[8,32,128]{2,1,0:T(8,128)}), f32[8,32,128]{2,1,0:T(8,128)S(1)}, u32[]{:S(2)}, u32[]{:S(2)}) async-start(f32[8,32,128]{2,1,0:T(8,128)} %total.7.after_ref), calls=%async_computation.4 | async-start | bytes 262144 | tf_op jit(solution)/shard_map/all_to_all | solution.py:346
  72.6 0.0 all-gather.2.cloned.1.call-done.a_ref
  72.6 0.0 copy-start
  72.6 1.6 %copy-done = bf16[2048,512]{1,0:T(8,128)(2,1)S(1)} copy-done((bf16[2048,512]{1,0:T(8,128)(2,1)S(1)}, bf16[2048,512]{1,0:T(8,128)(2,1)}, u32[]{:S(2)}) %copy-start) | copy-done | bytes 2097176
  74.2 4.7 %merged_parts.1 = (bf16[1024,512]{1,0:T(8,128)(2,1)S(1)}, bf16[1024,512]{1,0:T(8,128)(2,1)S(1)}) custom-call(bf16[2048,1024]{1,0:T(8,128)(2,1)} %all-gather.2.cloned.1.call-done.a_ref, bf16[2048,512]{1,0:T(8,128)(2,1)S(1)} %copy-done, bf16[1024,512]{1,0:T(8,128)(2,1)} %bitcast.5, f32[8,32,128]{2,1,0:T(8,128)} %total.7.after_ref), custom_call_target="tpu_custom_call" | custom-call | flops 2147483648 | bytes 6291456 | tf_op jit(solution)/shard_map/merged_parts/pallas_call | solution.py:162
  78.9 0.0 all-to-all-done.4.p_ref
  78.9 0.4 q_pieces.1
  79.3 10.8 %all_to_all.43.x_ref = f32[8,4,512]{2,1,0:T(4,128)S(1)} all-to-all(f32[8,4,512]{2,1,0:T(4,128)S(1)} %q_pieces.1), channel_id=1, replica_groups={{0,64,128,192,256,320,384,448},{8,72,136,200,264,328,392,456},{16,80,14..., dimensions={0} | all-to-all | bytes 131072 | tf_op jit(solution)/shard_map/all_to_all | solution.py:349
  90.1 10.8 %all_to_all.44.x_ref = f32[8,4,512]{2,1,0:T(4,128)S(1)} all-to-all(f32[8,4,512]{2,1,0:T(4,128)S(1)} %total.8), channel_id=1, replica_groups={{0,8,16,24,32,40,48,56},{64,72,80,88,96,104,112,120},{128,136,144,152,1..., dimensions={0} | all-to-all | bytes 131072 | tf_op jit(solution)/shard_map/all_to_all | solution.py:352
  100.9 0.6 total.9.after_ref
  101.5 3.4 %all-to-all-start.7 = ((f32[8,4,512]{2,1,0:T(4,128)}), f32[8,4,512]{2,1,0:T(4,128)S(1)}, u32[]{:S(2)}, u32[]{:S(2)}) async-start(f32[8,4,512]{2,1,0:T(4,128)} %total.9.after_ref), calls=%async_computation.7 | async-start | bytes 131072 | tf_op jit(solution)/shard_map/all_to_all | solution.py:349
  104.9 4.0 %basis.1 = (f32[32,32]{1,0:T(8,128)S(1)}, f32[32,1024]{1,0:T(8,128)}, bf16[1024,128]{1,0:T(8,128)(2,1)S(1)}) custom-call(f32[8,32,128]{2,1,0:T(8,128)S(1)} %all-to-all-done.4.p_ref, f32[8,4,512]{2,1,0:T(4,128)} %total.9.after_ref), custom_call_target="tpu_custom_call" | custom-call | flops 4000000000 | bytes 4000000 | tf_op jit(solution)/shard_map/basis/pallas_call | solution.py:251
  108.9 4.3 %all-to-all-done.7.refs_0_ = f32[8,4,512]{2,1,0:T(4,128)S(1)} async-done(((f32[8,4,512]{2,1,0:T(4,128)}), f32[8,4,512]{2,1,0:T(4,128)S(1)}, u32[]{:S(2)}, u32[]{:S(2)}) %all-to-all-start.7) | async-done | bytes 65568 | tf_op jit(solution)/shard_map/all_to_all | solution.py:349
  113.2 1.4 %residual.1 = (bf16[1024,512]{1,0:T(8,128)(2,1)}, f32[32,512]{1,0:T(8,128)}) custom-call(f32[8,4,512]{2,1,0:T(4,128)S(1)} %all-to-all-done.7.refs_0_, f32[32,32]{1,0:T(8,128)S(1)} %get-tuple-element.12.refs_1_, bf16[1024,128]{1,0:T(8,128)(2,1)S(1)} %get-tuple-element.13.refs_2_, bf16[1024,512]{1,0:T(8,128)(2,1)S(1)} %get-tuple-element.10.hi_ref.refs_3_, ...), custom_call_target="tpu_custom_call" | custom-call | tf_op jit(solution)/shard_map/residual/pallas_call | solution.py:298
  (3 shorter events, 0.0 us)
Async XLA Ops:
  7.2 18.9 %copy-start.1 = (bf16[256,1024]{1,0:T(8,128)(2,1)S(1)}, bf16[256,1024]{1,0:T(8,128)(2,1)}, u32[]{:S(2)}) copy-start(bf16[256,1024]{1,0:T(8,128)(2,1)} %acts_ref.1) | copy-start | bytes 1572868
  7.2 65.4 %all-gather.2.cloned.1.call-start = ((), (), s32[]{:S(2)}) async-start(), calls=%async_computation.8 | async-start | bytes 4718592 | tf_op jit(solution)/shard_map/all_gather | solution.py:356
  10.7 15.3 %all-to-all-start = ((f32[8,32,256]{2,1,0:T(8,128)}), f32[8,32,256]{2,1,0:T(8,128)S(1)}, u32[]{:S(2)}, u32[]{:S(2)}) async-start(f32[8,32,256]{2,1,0:T(8,128)} %y_chunks.1), calls=%async_computation | async-start | bytes 524288 | tf_op jit(solution)/shard_map/all_to_all | solution.py:346
  19.9 1.2 %copy-start.2 = (bf16[1,1024,512]{2,1,0:T(8,128)(2,1)S(1)}, bf16[1,1024,512]{2,1,0:T(8,128)(2,1)}, u32[]{:S(2)}) copy-start(bf16[1,1024,512]{2,1,0:T(8,128)(2,1)} %param.6) | copy-start | bytes 3145732
  21.2 0.8 copy-start.3
  67.7 11.2 %all-to-all-start.4 = ((f32[8,32,128]{2,1,0:T(8,128)}), f32[8,32,128]{2,1,0:T(8,128)S(1)}, u32[]{:S(2)}, u32[]{:S(2)}) async-start(f32[8,32,128]{2,1,0:T(8,128)} %total.7.after_ref), calls=%async_computation.4 | async-start | bytes 262144 | tf_op jit(solution)/shard_map/all_to_all | solution.py:346
  72.6 1.6 %copy-start = (bf16[2048,512]{1,0:T(8,128)(2,1)S(1)}, bf16[2048,512]{1,0:T(8,128)(2,1)}, u32[]{:S(2)}) copy-start(bf16[2048,512]{1,0:T(8,128)(2,1)} %g_ref.3) | copy-start | bytes 6291460
  101.5 11.7 %all-to-all-start.7 = ((f32[8,4,512]{2,1,0:T(4,128)}), f32[8,4,512]{2,1,0:T(4,128)S(1)}, u32[]{:S(2)}, u32[]{:S(2)}) async-start(f32[8,4,512]{2,1,0:T(4,128)} %total.9.after_ref), calls=%async_computation.7 | async-start | bytes 131072 | tf_op jit(solution)/shard_map/all_to_all | solution.py:349
Sparse Core Ops, SparseCore 0:
  10.2 42.3 all-gather.1

commit v8 on v7

--- a/solution.py
+++ b/solution.py
@@ -127,7 +127,7 @@
     )(y_all, acts, e_term)
 
 
-def merged_kernel(a_ref, g_ref, e_ref, after_ref, hi_ref, lo_ref, a_buf, e_buf, a_sems, e_sems):
+def merged_kernel(a_ref, g_ref, e_ref, after_ref, hi_ref, lo_ref, a_buf, g_buf, e_buf, a_sems, g_sem, e_sems):
     del after_ref
     blocks, _, block = a_buf.shape
 
@@ -138,15 +138,18 @@
             pltpu.make_async_copy(e_ref.at[span, :], e_buf.at[i], e_sems.at[i]),
         )
 
+    g_load = pltpu.make_async_copy(g_ref, g_buf, g_sem)
+    g_load.start()
     for load in loads(0):
         load.start()
+    g_load.wait()
     for i in range(blocks):
         for load in loads(i):
             load.wait()
         if i + 1 < blocks:
             for load in loads(i + 1):
                 load.start()
-        merged = dot(a_buf[i], g_ref[...], 0, 0) + e_buf[i].astype(F32)
+        merged = dot(a_buf[i], g_buf[...], 0, 0) + e_buf[i].astype(F32)
         hi, lo = parts_of(merged, 2)
         span = slice(i * block, (i + 1) * block)
         hi_ref[span, :] = hi
@@ -161,22 +164,25 @@
     shape = jax.ShapeDtypeStruct((width, cols), BF16)
     return pl.pallas_call(
         merged_kernel,
-        in_specs=[HBM, VMEM, HBM, ANY],
+        in_specs=[HBM, HBM, HBM, ANY],
         out_specs=[VMEM, VMEM],
         out_shape=[shape, shape],
         scratch_shapes=[
             pltpu.VMEM((blocks, tokens, block), BF16),
+            pltpu.VMEM(grads.shape, BF16),
             pltpu.VMEM((blocks, block, cols), BF16),
             pltpu.SemaphoreType.DMA((blocks,)),
+            pltpu.SemaphoreType.DMA,
             pltpu.SemaphoreType.DMA((blocks,)),
         ],
         compiler_params=PARAMS,
         cost_estimate=cost(2 * tokens * width * cols, acts_all.size * 2 + grads.size * 2),
         name="merged_parts",
     )(
-        pltpu.with_memory_space_constraint(acts_all, pltpu.HBM),
-        grads,
-        pltpu.with_memory_space_constraint(error, pltpu.HBM),
+        *(
+            pltpu.with_memory_space_constraint(x, pltpu.HBM)
+            for x in (acts_all, grads, error)
+        ),
         after,
     )
 
@@ -353,9 +359,10 @@
 
     error = error_buffer[0]
     q_t = prior_q.T
-    acts_all = lax.all_gather(acts, "tensor", axis=0, tiled=True)
-
-    y_all = over_tensor(y_chunks(q_t, grads_out, tensor))
+    y_mine = y_chunks(q_t, grads_out, tensor)
+    late_acts, y_mine = lax.optimization_barrier((acts, y_mine))
+    acts_all = lax.all_gather(late_acts, "tensor", axis=0, tiled=True)
+    y_all = over_tensor(y_mine)
     p_terms = over_tensor(p_chunks(y_all, acts, error_term(q_t, error)))
     p_row = total_for(over_y(total_for(p_terms, side)), side)
     p_last = total_for(over_z(p_row), tensor)

time: 122 us -> 120 us (0.984)
  local copies, waits for them, and re-layouts: 3.58 us -> 1.99 us
    unnamed x8 -> x6, local copies, waits for them, and re-layouts: 3.58 us -> 1.99 us
  transfers between devices with their start and end apart: 4 -> 4, of which waited for: 2 -> 2; matrix products, arithmetic and copies ran while one was open for 0% -> 0% of each run, Pallas kernels for 11% -> 9%
where the time goes in v8:
time: 120 us
  blocking collectives  62.2 us (52%)
  starting transfers between devices  17.4 us (14%)
  Pallas kernels  16 us (13%)
  between operations  14.1 us (12%)
  waiting for transfers between devices  8.05 us (7%)
  local copies, waits for them, and re-layouts  1.99 us (2%)
    all_to_all x2, blocking collectives, over_z(): return lax.all_to_all(x, 'dp', 0, 0, axis_index_groups=along_z)  30.2 us
    all_to_all x2, blocking collectives, over_y(): return lax.all_to_all(x, 'dp', 0, 0, axis_index_groups=along_y)  22.2 us
    all_to_all x2, starting transfers between devices, over_tensor(): return lax.all_to_all(x, 'tensor', 0, 0)  14 us
    all_to_all x1, blocking collectives, over_tensor(): return lax.all_to_all(x, 'tensor', 0, 0)  9.76 us
    pallas_call x1, Pallas kernels, merged_parts(): pl.pallas_call(merged_kernel, in_specs=[HBM, HBM, HBM, ANY], out_specs=[V...  5.37 us
    all_to_all x1, waiting for transfers between devices, over_y(): return lax.all_to_all(x, 'dp', 0, 0, axis_index_groups=along_y)  4.31 us
    pallas_call x1, Pallas kernels, basis_of(): pl.pallas_call(basis_kernel, in_specs=[VMEM, ANY], out_specs=[VMEM] * 3,...  3.99 us
    all_to_all x2, waiting for transfers between devices, over_tensor(): return lax.all_to_all(x, 'tensor', 0, 0)  3.73 us
  transfers between devices with their start and end apart: 4, of which 2 were waited for; matrix products, arithmetic and copies ran while one was open for 0% of the time, Pallas kernels for 9%

profile of v8, /device:TPU:2, one launch (start us, length us, event | category | flops | bytes accessed | tf_op | source)
XLA Modules:
  0.0 119.7 jit_solution(2074143457627667472)
XLA Ops:
  7.2 0.0 copy-start
  7.2 0.0 all-gather.2.cloned.1.call-start
  7.2 2.8 %y_chunks.1 = f32[8,32,256]{2,1,0:T(8,128)} custom-call(bf16[32,512]{1,0:T(8,128)(2,1)} %bitcast.7, bf16[2048,512]{1,0:T(8,128)(2,1)} %g_ref.3), custom_call_target="tpu_custom_call" | custom-call | flops 536870912 | bytes 2097152 | tf_op jit(solution)/shard_map/y_chunks/pallas_call | solution.py:69
  10.1 0.0 all-gather.2.cloned.1.call-update
  10.1 9.2 %all-to-all-start = ((f32[8,32,256]{2,1,0:T(8,128)}), f32[8,32,256]{2,1,0:T(8,128)S(1)}, u32[]{:S(2)}, u32[]{:S(2)}) async-start(f32[8,32,256]{2,1,0:T(8,128)} %y_chunks.1), calls=%async_computation | async-start | bytes 524288 | tf_op jit(solution)/shard_map/all_to_all | solution.py:352
  19.3 0.0 copy-start.1
  19.3 1.2 %copy-done.1 = bf16[1,1024,512]{2,1,0:T(8,128)(2,1)S(1)} copy-done((bf16[1,1024,512]{2,1,0:T(8,128)(2,1)S(1)}, bf16[1,1024,512]{2,1,0:T(8,128)(2,1)}, u32[]{:S(2)}) %copy-start.1) | copy-done | bytes 1048600
  20.6 0.0 copy-start.2
  20.6 0.8 copy-done.2
  21.3 0.4 error_term.1.e_ref
  21.7 3.7 %all-to-all-done.y_ref = f32[8,32,256]{2,1,0:T(8,128)S(1)} async-done(((f32[8,32,256]{2,1,0:T(8,128)}), f32[8,32,256]{2,1,0:T(8,128)S(1)}, u32[]{:S(2)}, u32[]{:S(2)}) %all-to-all-start) | async-done | bytes 262176 | tf_op jit(solution)/shard_map/all_to_all | solution.py:352
  25.4 0.0 copy-done
  25.4 0.2 p_chunks.1
  25.6 9.8 %all_to_all.40.x_ref = f32[8,32,128]{2,1,0:T(8,128)S(1)} all-to-all(f32[8,32,128]{2,1,0:T(8,128)S(1)} %p_chunks.1), channel_id=1, replica_groups=mesh['dp'=64,'tensor'=8] {'tensor'}, dimensions={0} | all-to-all | bytes 262144 | tf_op jit(solution)/shard_map/all_to_all | solution.py:352
  35.4 11.5 %all_to_all.41.x_ref = f32[8,32,128]{2,1,0:T(8,128)S(1)} all-to-all(f32[8,32,128]{2,1,0:T(8,128)S(1)} %total.5), channel_id=1, replica_groups={{0,64,128,192,256,320,384,448},{8,72,136,200,264,328,392,456},{16,80,14..., dimensions={0} | all-to-all | bytes 262144 | tf_op jit(solution)/shard_map/all_to_all | solution.py:355
  46.9 19.5 %all_to_all.42.x_ref = f32[8,32,128]{2,1,0:T(8,128)S(1)} all-to-all(f32[8,32,128]{2,1,0:T(8,128)S(1)} %total.6), channel_id=1, replica_groups={{0,8,16,24,32,40,48,56},{64,72,80,88,96,104,112,120},{128,136,144,152,1..., dimensions={0} | all-to-all | bytes 262144 | tf_op jit(solution)/shard_map/all_to_all | solution.py:358
  66.4 0.7 total.7.after_ref
  67.1 4.7 %all-to-all-start.4 = ((f32[8,32,128]{2,1,0:T(8,128)}), f32[8,32,128]{2,1,0:T(8,128)S(1)}, u32[]{:S(2)}, u32[]{:S(2)}) async-start(f32[8,32,128]{2,1,0:T(8,128)} %total.7.after_ref), calls=%async_computation.4 | async-start | bytes 262144 | tf_op jit(solution)/shard_map/all_to_all | solution.py:352
  71.8 0.0 all-gather.2.cloned.1.call-done.a_ref
  71.8 5.4 %merged_parts.1 = (bf16[1024,512]{1,0:T(8,128)(2,1)S(1)}, bf16[1024,512]{1,0:T(8,128)(2,1)S(1)}) custom-call(bf16[2048,1024]{1,0:T(8,128)(2,1)} %all-gather.2.cloned.1.call-done.a_ref, bf16[2048,512]{1,0:T(8,128)(2,1)} %g_ref.3, bf16[1024,512]{1,0:T(8,128)(2,1)} %bitcast.5, f32[8,32,128]{2,1,0:T(8,128)} %total.7.after_ref), custom_call_target="tpu_custom_call" | custom-call | flops 2147483648 | bytes 6291456 | tf_op jit(solution)/shard_map/merged_parts/pallas_call | solution.py:165
  77.2 0.0 all-to-all-done.4.p_ref
  77.2 0.4 q_pieces.1
  77.6 10.8 %all_to_all.43.x_ref = f32[8,4,512]{2,1,0:T(4,128)S(1)} all-to-all(f32[8,4,512]{2,1,0:T(4,128)S(1)} %q_pieces.1), channel_id=1, replica_groups={{0,64,128,192,256,320,384,448},{8,72,136,200,264,328,392,456},{16,80,14..., dimensions={0} | all-to-all | bytes 131072 | tf_op jit(solution)/shard_map/all_to_all | solution.py:355
  88.4 10.8 %all_to_all.44.x_ref = f32[8,4,512]{2,1,0:T(4,128)S(1)} all-to-all(f32[8,4,512]{2,1,0:T(4,128)S(1)} %total.8), channel_id=1, replica_groups={{0,8,16,24,32,40,48,56},{64,72,80,88,96,104,112,120},{128,136,144,152,1..., dimensions={0} | all-to-all | bytes 131072 | tf_op jit(solution)/shard_map/all_to_all | solution.py:358
  99.1 0.6 total.9.after_ref
  99.8 3.4 %all-to-all-start.7 = ((f32[8,4,512]{2,1,0:T(4,128)}), f32[8,4,512]{2,1,0:T(4,128)S(1)}, u32[]{:S(2)}, u32[]{:S(2)}) async-start(f32[8,4,512]{2,1,0:T(4,128)} %total.9.after_ref), calls=%async_computation.7 | async-start | bytes 131072 | tf_op jit(solution)/shard_map/all_to_all | solution.py:355
  103.1 4.0 %basis.1 = (f32[32,32]{1,0:T(8,128)S(1)}, f32[32,1024]{1,0:T(8,128)}, bf16[1024,128]{1,0:T(8,128)(2,1)S(1)}) custom-call(f32[8,32,128]{2,1,0:T(8,128)S(1)} %all-to-all-done.4.p_ref, f32[8,4,512]{2,1,0:T(4,128)} %total.9.after_ref), custom_call_target="tpu_custom_call" | custom-call | flops 4000000000 | bytes 4000000 | tf_op jit(solution)/shard_map/basis/pallas_call | solution.py:257
  107.1 4.3 %all-to-all-done.7.refs_0_ = f32[8,4,512]{2,1,0:T(4,128)S(1)} async-done(((f32[8,4,512]{2,1,0:T(4,128)}), f32[8,4,512]{2,1,0:T(4,128)S(1)}, u32[]{:S(2)}, u32[]{:S(2)}) %all-to-all-start.7) | async-done | bytes 65568 | tf_op jit(solution)/shard_map/all_to_all | solution.py:355
  111.4 1.4 %residual.1 = (bf16[1024,512]{1,0:T(8,128)(2,1)}, f32[32,512]{1,0:T(8,128)}) custom-call(f32[8,4,512]{2,1,0:T(4,128)S(1)} %all-to-all-done.7.refs_0_, f32[32,32]{1,0:T(8,128)S(1)} %get-tuple-element.16.refs_1_, bf16[1024,128]{1,0:T(8,128)(2,1)S(1)} %get-tuple-element.17.refs_2_, bf16[1024,512]{1,0:T(8,128)(2,1)S(1)} %get-tuple-element.14.hi_ref.refs_3_, ...), custom_call_target="tpu_custom_call" | custom-call | tf_op jit(solution)/shard_map/residual/pallas_call | solution.py:304
  (3 shorter events, 0.0 us)
Async XLA Ops:
  7.2 18.3 %copy-start = (bf16[256,1024]{1,0:T(8,128)(2,1)S(1)}, bf16[256,1024]{1,0:T(8,128)(2,1)}, u32[]{:S(2)}) copy-start(bf16[256,1024]{1,0:T(8,128)(2,1)} %acts_ref.1) | copy-start | bytes 1572868
  7.2 64.6 %all-gather.2.cloned.1.call-start = ((), (), s32[]{:S(2)}) async-start(), calls=%async_computation.8 | async-start | bytes 4718592 | tf_op jit(solution)/shard_map/all_gather | solution.py:364
  10.1 15.3 %all-to-all-start = ((f32[8,32,256]{2,1,0:T(8,128)}), f32[8,32,256]{2,1,0:T(8,128)S(1)}, u32[]{:S(2)}, u32[]{:S(2)}) async-start(f32[8,32,256]{2,1,0:T(8,128)} %y_chunks.1), calls=%async_computation | async-start | bytes 524288 | tf_op jit(solution)/shard_map/all_to_all | solution.py:352
  19.3 1.2 %copy-start.1 = (bf16[1,1024,512]{2,1,0:T(8,128)(2,1)S(1)}, bf16[1,1024,512]{2,1,0:T(8,128)(2,1)}, u32[]{:S(2)}) copy-start(bf16[1,1024,512]{2,1,0:T(8,128)(2,1)} %param.6) | copy-start | bytes 3145732
  20.6 0.8 copy-start.2
  67.1 10.1 %all-to-all-start.4 = ((f32[8,32,128]{2,1,0:T(8,128)}), f32[8,32,128]{2,1,0:T(8,128)S(1)}, u32[]{:S(2)}, u32[]{:S(2)}) async-start(f32[8,32,128]{2,1,0:T(8,128)} %total.7.after_ref), calls=%async_computation.4 | async-start | bytes 262144 | tf_op jit(solution)/shard_map/all_to_all | solution.py:352
  99.8 11.7 %all-to-all-start.7 = ((f32[8,4,512]{2,1,0:T(4,128)}), f32[8,4,512]{2,1,0:T(4,128)S(1)}, u32[]{:S(2)}, u32[]{:S(2)}) async-start(f32[8,4,512]{2,1,0:T(4,128)} %total.9.after_ref), calls=%async_computation.7 | async-start | bytes 131072 | tf_op jit(solution)/shard_map/all_to_all | solution.py:355
Sparse Core Ops, SparseCore 0:
  10.2 41.9 all-gather.1

commit v9 on v8

--- a/solution.py
+++ b/solution.py
@@ -345,17 +345,25 @@
     tensor = lax.axis_size("tensor")
     replicas = lax.axis_size("dp")
     side = math.isqrt(replicas)
-    along_y = [[y * side + z for y in range(side)] for z in range(side)]
-    along_z = [[y * side + z for z in range(side)] for y in range(side)]
+    both = ("dp", "tensor")
+
+    def line(along, fixed, t):
+        pairs = [(i, fixed) if along == 0 else (fixed, i) for i in range(side)]
+        return [(y * side + z) * tensor + t for y, z in pairs]
+
+    first, second = (
+        [line((t + turn) % 2, k, t) for t in range(tensor) for k in range(side)]
+        for turn in range(2)
+    )
 
     def over_tensor(x):
         return lax.all_to_all(x, "tensor", 0, 0)
 
-    def over_y(x):
-        return lax.all_to_all(x, "dp", 0, 0, axis_index_groups=along_y)
-
-    def over_z(x):
-        return lax.all_to_all(x, "dp", 0, 0, axis_index_groups=along_z)
+    def over_first(x):
+        return lax.all_to_all(x, both, 0, 0, axis_index_groups=first)
+
+    def over_second(x):
+        return lax.all_to_all(x, both, 0, 0, axis_index_groups=second)
 
     error = error_buffer[0]
     q_t = prior_q.T
@@ -364,14 +372,14 @@
     acts_all = lax.all_gather(late_acts, "tensor", axis=0, tiled=True)
     y_all = over_tensor(y_mine)
     p_terms = over_tensor(p_chunks(y_all, acts, error_term(q_t, error)))
-    p_row = total_for(over_y(total_for(p_terms, side)), side)
-    p_last = total_for(over_z(p_row), tensor)
+    p_row = total_for(over_first(total_for(p_terms, side)), side)
+    p_last = total_for(over_second(p_row), tensor)
     p_all = over_tensor(p_last)
     hi, lo = merged_parts(acts_all, grads_out, error, p_last)
 
     pieces = q_pieces(p_all, hi, lo, side)
-    q_sum = total_for(over_z(total_for(over_y(pieces), side)), side)
-    q_all = over_y(q_sum)
+    q_sum = total_for(over_second(total_for(over_first(pieces), side)), side)
+    q_all = over_first(q_sum)
     inverse, basis, stack = basis_of(p_all, q_sum)
     residual, factor = residual_of(q_all, inverse, stack, hi, lo, replicas)
     return (residual[None], basis.T, factor.T)

time: 120 us -> 120 us (level)
  no operation moved by 1% of the time
where the time goes in v9:
time: 120 us
  blocking collectives  62.2 us (52%)
  starting transfers between devices  17.4 us (14%)
  Pallas kernels  16 us (13%)
  between operations  14.1 us (12%)
  waiting for transfers between devices  8.05 us (7%)
  local copies, waits for them, and re-layouts  1.99 us (2%)
    all_to_all x2, blocking collectives, over_second(): return lax.all_to_all(x, both, 0, 0, axis_index_groups=second)  30.2 us
    all_to_all x2, blocking collectives, over_first(): return lax.all_to_all(x, both, 0, 0, axis_index_groups=first)  22.2 us
    all_to_all x2, starting transfers between devices, over_tensor(): return lax.all_to_all(x, 'tensor', 0, 0)  14 us
    all_to_all x1, blocking collectives, over_tensor(): return lax.all_to_all(x, 'tensor', 0, 0)  9.76 us
    pallas_call x1, Pallas kernels, merged_parts(): pl.pallas_call(merged_kernel, in_specs=[HBM, HBM, HBM, ANY], out_specs=[V...  5.37 us
    all_to_all x1, waiting for transfers between devices, over_first(): return lax.all_to_all(x, both, 0, 0, axis_index_groups=first)  4.31 us
    pallas_call x1, Pallas kernels, basis_of(): pl.pallas_call(basis_kernel, in_specs=[VMEM, ANY], out_specs=[VMEM] * 3,...  3.99 us
    all_to_all x2, waiting for transfers between devices, over_tensor(): return lax.all_to_all(x, 'tensor', 0, 0)  3.73 us
  transfers between devices with their start and end apart: 4, of which 2 were waited for; matrix products, arithmetic and copies ran while one was open for 0% of the time, Pallas kernels for 9%

profile of v9, /device:TPU:2, one launch (start us, length us, event | category | flops | bytes accessed | tf_op | source)
XLA Modules:
  0.0 119.7 jit_solution(12818457905662117873)
XLA Ops:
  7.2 0.0 copy-start
  7.2 0.0 all-gather.2.cloned.1.call-start
  7.2 2.8 %y_chunks.1 = f32[8,32,256]{2,1,0:T(8,128)} custom-call(bf16[32,512]{1,0:T(8,128)(2,1)} %bitcast.7, bf16[2048,512]{1,0:T(8,128)(2,1)} %g_ref.3), custom_call_target="tpu_custom_call" | custom-call | flops 536870912 | bytes 2097152 | tf_op jit(solution)/shard_map/y_chunks/pallas_call | solution.py:69
  10.1 0.0 all-gather.2.cloned.1.call-update
  10.1 9.2 %all-to-all-start = ((f32[8,32,256]{2,1,0:T(8,128)}), f32[8,32,256]{2,1,0:T(8,128)S(1)}, u32[]{:S(2)}, u32[]{:S(2)}) async-start(f32[8,32,256]{2,1,0:T(8,128)} %y_chunks.1), calls=%async_computation | async-start | bytes 524288 | tf_op jit(solution)/shard_map/all_to_all | solution.py:360
  19.3 0.0 copy-start.1
  19.3 1.2 %copy-done.1 = bf16[1,1024,512]{2,1,0:T(8,128)(2,1)S(1)} copy-done((bf16[1,1024,512]{2,1,0:T(8,128)(2,1)S(1)}, bf16[1,1024,512]{2,1,0:T(8,128)(2,1)}, u32[]{:S(2)}) %copy-start.1) | copy-done | bytes 1048600
  20.6 0.0 copy-start.2
  20.6 0.8 copy-done.2
  21.3 0.4 error_term.1.e_ref
  21.7 3.7 %all-to-all-done.y_ref = f32[8,32,256]{2,1,0:T(8,128)S(1)} async-done(((f32[8,32,256]{2,1,0:T(8,128)}), f32[8,32,256]{2,1,0:T(8,128)S(1)}, u32[]{:S(2)}, u32[]{:S(2)}) %all-to-all-start) | async-done | bytes 262176 | tf_op jit(solution)/shard_map/all_to_all | solution.py:360
  25.4 0.0 copy-done
  25.4 0.2 p_chunks.1
  25.6 9.8 %all_to_all.40.x_ref = f32[8,32,128]{2,1,0:T(8,128)S(1)} all-to-all(f32[8,32,128]{2,1,0:T(8,128)S(1)} %p_chunks.1), channel_id=1, replica_groups=mesh['dp'=64,'tensor'=8] {'tensor'}, dimensions={0} | all-to-all | bytes 262144 | tf_op jit(solution)/shard_map/all_to_all | solution.py:360
  35.4 11.5 %all_to_all.41.x_ref = f32[8,32,128]{2,1,0:T(8,128)S(1)} all-to-all(f32[8,32,128]{2,1,0:T(8,128)S(1)} %total.5), channel_id=1, replica_groups={{0,64,128,192,256,320,384,448},{8,72,136,200,264,328,392,456},{16,80,14..., dimensions={0} | all-to-all | bytes 262144 | tf_op jit(solution)/shard_map/all_to_all | solution.py:363
  46.9 19.5 %all_to_all.42.x_ref = f32[8,32,128]{2,1,0:T(8,128)S(1)} all-to-all(f32[8,32,128]{2,1,0:T(8,128)S(1)} %total.6), channel_id=1, replica_groups={{0,8,16,24,32,40,48,56},{64,72,80,88,96,104,112,120},{128,136,144,152,1..., dimensions={0} | all-to-all | bytes 262144 | tf_op jit(solution)/shard_map/all_to_all | solution.py:366
  66.4 0.7 total.7.after_ref
  67.0 4.8 %all-to-all-start.4 = ((f32[8,32,128]{2,1,0:T(8,128)}), f32[8,32,128]{2,1,0:T(8,128)S(1)}, u32[]{:S(2)}, u32[]{:S(2)}) async-start(f32[8,32,128]{2,1,0:T(8,128)} %total.7.after_ref), calls=%async_computation.4 | async-start | bytes 262144 | tf_op jit(solution)/shard_map/all_to_all | solution.py:360
  71.8 0.0 all-gather.2.cloned.1.call-done.a_ref
  71.8 5.4 %merged_parts.1 = (bf16[1024,512]{1,0:T(8,128)(2,1)S(1)}, bf16[1024,512]{1,0:T(8,128)(2,1)S(1)}) custom-call(bf16[2048,1024]{1,0:T(8,128)(2,1)} %all-gather.2.cloned.1.call-done.a_ref, bf16[2048,512]{1,0:T(8,128)(2,1)} %g_ref.3, bf16[1024,512]{1,0:T(8,128)(2,1)} %bitcast.5, f32[8,32,128]{2,1,0:T(8,128)} %total.7.after_ref), custom_call_target="tpu_custom_call" | custom-call | flops 2147483648 | bytes 6291456 | tf_op jit(solution)/shard_map/merged_parts/pallas_call | solution.py:165
  77.2 0.0 all-to-all-done.4.p_ref
  77.2 0.4 q_pieces.1
  77.6 10.8 %all_to_all.43.x_ref = f32[8,4,512]{2,1,0:T(4,128)S(1)} all-to-all(f32[8,4,512]{2,1,0:T(4,128)S(1)} %q_pieces.1), channel_id=1, replica_groups={{0,64,128,192,256,320,384,448},{8,72,136,200,264,328,392,456},{16,80,14..., dimensions={0} | all-to-all | bytes 131072 | tf_op jit(solution)/shard_map/all_to_all | solution.py:363
  88.4 10.8 %all_to_all.44.x_ref = f32[8,4,512]{2,1,0:T(4,128)S(1)} all-to-all(f32[8,4,512]{2,1,0:T(4,128)S(1)} %total.8), channel_id=1, replica_groups={{0,8,16,24,32,40,48,56},{64,72,80,88,96,104,112,120},{128,136,144,152,1..., dimensions={0} | all-to-all | bytes 131072 | tf_op jit(solution)/shard_map/all_to_all | solution.py:366
  99.1 0.6 total.9.after_ref
  99.8 3.4 %all-to-all-start.7 = ((f32[8,4,512]{2,1,0:T(4,128)}), f32[8,4,512]{2,1,0:T(4,128)S(1)}, u32[]{:S(2)}, u32[]{:S(2)}) async-start(f32[8,4,512]{2,1,0:T(4,128)} %total.9.after_ref), calls=%async_computation.7 | async-start | bytes 131072 | tf_op jit(solution)/shard_map/all_to_all | solution.py:363
  103.1 4.0 %basis.1 = (f32[32,32]{1,0:T(8,128)S(1)}, f32[32,1024]{1,0:T(8,128)}, bf16[1024,128]{1,0:T(8,128)(2,1)S(1)}) custom-call(f32[8,32,128]{2,1,0:T(8,128)S(1)} %all-to-all-done.4.p_ref, f32[8,4,512]{2,1,0:T(4,128)} %total.9.after_ref), custom_call_target="tpu_custom_call" | custom-call | flops 4000000000 | bytes 4000000 | tf_op jit(solution)/shard_map/basis/pallas_call | solution.py:257
  107.1 4.3 %all-to-all-done.7.refs_0_ = f32[8,4,512]{2,1,0:T(4,128)S(1)} async-done(((f32[8,4,512]{2,1,0:T(4,128)}), f32[8,4,512]{2,1,0:T(4,128)S(1)}, u32[]{:S(2)}, u32[]{:S(2)}) %all-to-all-start.7) | async-done | bytes 65568 | tf_op jit(solution)/shard_map/all_to_all | solution.py:363
  111.4 1.4 %residual.1 = (bf16[1024,512]{1,0:T(8,128)(2,1)}, f32[32,512]{1,0:T(8,128)}) custom-call(f32[8,4,512]{2,1,0:T(4,128)S(1)} %all-to-all-done.7.refs_0_, f32[32,32]{1,0:T(8,128)S(1)} %get-tuple-element.16.refs_1_, bf16[1024,128]{1,0:T(8,128)(2,1)S(1)} %get-tuple-element.17.refs_2_, bf16[1024,512]{1,0:T(8,128)(2,1)S(1)} %get-tuple-element.14.hi_ref.refs_3_, ...), custom_call_target="tpu_custom_call" | custom-call | tf_op jit(solution)/shard_map/residual/pallas_call | solution.py:304
  (3 shorter events, 0.0 us)
Async XLA Ops:
  7.2 18.3 %copy-start = (bf16[256,1024]{1,0:T(8,128)(2,1)S(1)}, bf16[256,1024]{1,0:T(8,128)(2,1)}, u32[]{:S(2)}) copy-start(bf16[256,1024]{1,0:T(8,128)(2,1)} %acts_ref.1) | copy-start | bytes 1572868
  7.2 64.6 %all-gather.2.cloned.1.call-start = ((), (), s32[]{:S(2)}) async-start(), calls=%async_computation.8 | async-start | bytes 4718592 | tf_op jit(solution)/shard_map/all_gather | solution.py:372
  10.1 15.3 %all-to-all-start = ((f32[8,32,256]{2,1,0:T(8,128)}), f32[8,32,256]{2,1,0:T(8,128)S(1)}, u32[]{:S(2)}, u32[]{:S(2)}) async-start(f32[8,32,256]{2,1,0:T(8,128)} %y_chunks.1), calls=%async_computation | async-start | bytes 524288 | tf_op jit(solution)/shard_map/all_to_all | solution.py:360
  19.3 1.2 %copy-start.1 = (bf16[1,1024,512]{2,1,0:T(8,128)(2,1)S(1)}, bf16[1,1024,512]{2,1,0:T(8,128)(2,1)}, u32[]{:S(2)}) copy-start(bf16[1,1024,512]{2,1,0:T(8,128)(2,1)} %param.6) | copy-start | bytes 3145732
  20.6 0.8 copy-start.2
  67.0 10.1 %all-to-all-start.4 = ((f32[8,32,128]{2,1,0:T(8,128)}), f32[8,32,128]{2,1,0:T(8,128)S(1)}, u32[]{:S(2)}, u32[]{:S(2)}) async-start(f32[8,32,128]{2,1,0:T(8,128)} %total.7.after_ref), calls=%async_computation.4 | async-start | bytes 262144 | tf_op jit(solution)/shard_map/all_to_all | solution.py:360
  99.8 11.7 %all-to-all-start.7 = ((f32[8,4,512]{2,1,0:T(4,128)}), f32[8,4,512]{2,1,0:T(4,128)S(1)}, u32[]{:S(2)}, u32[]{:S(2)}) async-start(f32[8,4,512]{2,1,0:T(4,128)} %total.9.after_ref), calls=%async_computation.7 | async-start | bytes 131072 | tf_op jit(solution)/shard_map/all_to_all | solution.py:363
Sparse Core Ops, SparseCore 0:
  10.2 41.9 all-gather.1

commit v10 on v8

--- a/solution.py
+++ b/solution.py
@@ -9,6 +9,7 @@
 
 F32 = jnp.float32
 BF16 = jnp.bfloat16
+LANES = 128
 VMEM = pl.BlockSpec(memory_space=pltpu.VMEM)
 HBM = pl.BlockSpec(memory_space=pltpu.HBM)
 ANY = pl.BlockSpec(memory_space=pl.ANY)
@@ -197,8 +198,10 @@
         both = dot(jnp.concatenate([high, low], axis=0), hi_ref[span, :])
         term = both[:rank] + (both[rank:] + dot(high, lo_ref[span, :]))
         total = term if total is None else total + term
+    across = total.shape[1] // LANES
     for k in range(pieces):
-        out_ref[k] = total[k * rows : (k + 1) * rows, :]
+        r, c = k // across, k % across
+        out_ref[k] = total[r * rows : (r + 1) * rows, c * LANES : (c + 1) * LANES]
 
 
 def q_pieces(p_all, hi, lo, pieces):
@@ -208,7 +211,7 @@
         q_kernel,
         in_specs=[VMEM] * 3,
         out_specs=VMEM,
-        out_shape=jax.ShapeDtypeStruct((pieces, rank // pieces, cols), F32),
+        out_shape=jax.ShapeDtypeStruct((pieces, rank * cols // (pieces * LANES), LANES), F32),
         compiler_params=PARAMS,
         cost_estimate=cost(2 * hi.size * rank * 8, hi.size * 4),
         name="q_pieces",
@@ -272,8 +275,10 @@
 
 def residual_kernel(scale, q_ref, inv_ref, stack_ref, hi_ref, lo_ref, out_ref, factor_ref, raw, factor, out_buf, sems, factor_sem):
     pieces, rows, _ = q_ref.shape
+    across = raw.shape[1] // LANES
     for k in range(pieces):
-        raw[k * rows : (k + 1) * rows, :] = q_ref[k]
+        r, c = k // across, k % across
+        raw[r * rows : (r + 1) * rows, c * LANES : (c + 1) * LANES] = q_ref[k]
     factor[...] = scale * jnp.dot(
         inv_ref[...],
         raw[...],

time: 120 us -> 120 us (level)
  no operation moved by 1% of the time
where the time goes in v10:
time: 120 us
  blocking collectives  62.2 us (52%)
  starting transfers between devices  17.4 us (14%)
  Pallas kernels  16 us (13%)
  between operations  14.1 us (12%)
  waiting for transfers between devices  8.05 us (7%)
  local copies, waits for them, and re-layouts  1.99 us (2%)
    all_to_all x2, blocking collectives, over_z(): return lax.all_to_all(x, 'dp', 0, 0, axis_index_groups=along_z)  30.2 us
    all_to_all x2, blocking collectives, over_y(): return lax.all_to_all(x, 'dp', 0, 0, axis_index_groups=along_y)  22.2 us
    all_to_all x2, starting transfers between devices, over_tensor(): return lax.all_to_all(x, 'tensor', 0, 0)  14 us
    all_to_all x1, blocking collectives, over_tensor(): return lax.all_to_all(x, 'tensor', 0, 0)  9.76 us
    pallas_call x1, Pallas kernels, merged_parts(): pl.pallas_call(merged_kernel, in_specs=[HBM, HBM, HBM, ANY], out_specs=[V...  5.37 us
    all_to_all x1, waiting for transfers between devices, over_y(): return lax.all_to_all(x, 'dp', 0, 0, axis_index_groups=along_y)  4.31 us
    pallas_call x1, Pallas kernels, basis_of(): pl.pallas_call(basis_kernel, in_specs=[VMEM, ANY], out_specs=[VMEM] * 3,...  3.99 us
    all_to_all x2, waiting for transfers between devices, over_tensor(): return lax.all_to_all(x, 'tensor', 0, 0)  3.73 us
  transfers between devices with their start and end apart: 4, of which 2 were waited for; matrix products, arithmetic and copies ran while one was open for 0% of the time, Pallas kernels for 9%

profile of v10, /device:TPU:2, one launch (start us, length us, event | category | flops | bytes accessed | tf_op | source)
XLA Modules:
  0.0 119.7 jit_solution(10647470062135201874)
XLA Ops:
  7.2 0.0 copy-start
  7.2 0.0 all-gather.2.cloned.1.call-start
  7.2 2.8 %y_chunks.1 = f32[8,32,256]{2,1,0:T(8,128)} custom-call(bf16[32,512]{1,0:T(8,128)(2,1)} %bitcast.7, bf16[2048,512]{1,0:T(8,128)(2,1)} %g_ref.3), custom_call_target="tpu_custom_call" | custom-call | flops 536870912 | bytes 2097152 | tf_op jit(solution)/shard_map/y_chunks/pallas_call | solution.py:70
  10.1 0.0 all-gather.2.cloned.1.call-update
  10.1 9.2 %all-to-all-start = ((f32[8,32,256]{2,1,0:T(8,128)}), f32[8,32,256]{2,1,0:T(8,128)S(1)}, u32[]{:S(2)}, u32[]{:S(2)}) async-start(f32[8,32,256]{2,1,0:T(8,128)} %y_chunks.1), calls=%async_computation | async-start | bytes 524288 | tf_op jit(solution)/shard_map/all_to_all | solution.py:357
  19.3 0.0 copy-start.1
  19.3 1.2 %copy-done.1 = bf16[1,1024,512]{2,1,0:T(8,128)(2,1)S(1)} copy-done((bf16[1,1024,512]{2,1,0:T(8,128)(2,1)S(1)}, bf16[1,1024,512]{2,1,0:T(8,128)(2,1)}, u32[]{:S(2)}) %copy-start.1) | copy-done | bytes 1048600
  20.6 0.0 copy-start.2
  20.6 0.8 copy-done.2
  21.3 0.4 error_term.1.e_ref
  21.7 3.7 %all-to-all-done.y_ref = f32[8,32,256]{2,1,0:T(8,128)S(1)} async-done(((f32[8,32,256]{2,1,0:T(8,128)}), f32[8,32,256]{2,1,0:T(8,128)S(1)}, u32[]{:S(2)}, u32[]{:S(2)}) %all-to-all-start) | async-done | bytes 262176 | tf_op jit(solution)/shard_map/all_to_all | solution.py:357
  25.4 0.0 copy-done
  25.4 0.2 p_chunks.1
  25.6 9.8 %all_to_all.40.x_ref = f32[8,32,128]{2,1,0:T(8,128)S(1)} all-to-all(f32[8,32,128]{2,1,0:T(8,128)S(1)} %p_chunks.1), channel_id=1, replica_groups=mesh['dp'=64,'tensor'=8] {'tensor'}, dimensions={0} | all-to-all | bytes 262144 | tf_op jit(solution)/shard_map/all_to_all | solution.py:357
  35.4 11.5 %all_to_all.41.x_ref = f32[8,32,128]{2,1,0:T(8,128)S(1)} all-to-all(f32[8,32,128]{2,1,0:T(8,128)S(1)} %total.5), channel_id=1, replica_groups={{0,64,128,192,256,320,384,448},{8,72,136,200,264,328,392,456},{16,80,14..., dimensions={0} | all-to-all | bytes 262144 | tf_op jit(solution)/shard_map/all_to_all | solution.py:360
  46.9 19.5 %all_to_all.42.x_ref = f32[8,32,128]{2,1,0:T(8,128)S(1)} all-to-all(f32[8,32,128]{2,1,0:T(8,128)S(1)} %total.6), channel_id=1, replica_groups={{0,8,16,24,32,40,48,56},{64,72,80,88,96,104,112,120},{128,136,144,152,1..., dimensions={0} | all-to-all | bytes 262144 | tf_op jit(solution)/shard_map/all_to_all | solution.py:363
  66.4 0.7 total.7.after_ref
  67.1 4.7 %all-to-all-start.4 = ((f32[8,32,128]{2,1,0:T(8,128)}), f32[8,32,128]{2,1,0:T(8,128)S(1)}, u32[]{:S(2)}, u32[]{:S(2)}) async-start(f32[8,32,128]{2,1,0:T(8,128)} %total.7.after_ref), calls=%async_computation.4 | async-start | bytes 262144 | tf_op jit(solution)/shard_map/all_to_all | solution.py:357
  71.8 0.0 all-gather.2.cloned.1.call-done.a_ref
  71.8 5.4 %merged_parts.1 = (bf16[1024,512]{1,0:T(8,128)(2,1)S(1)}, bf16[1024,512]{1,0:T(8,128)(2,1)S(1)}) custom-call(bf16[2048,1024]{1,0:T(8,128)(2,1)} %all-gather.2.cloned.1.call-done.a_ref, bf16[2048,512]{1,0:T(8,128)(2,1)} %g_ref.3, bf16[1024,512]{1,0:T(8,128)(2,1)} %bitcast.5, f32[8,32,128]{2,1,0:T(8,128)} %total.7.after_ref), custom_call_target="tpu_custom_call" | custom-call | flops 2147483648 | bytes 6291456 | tf_op jit(solution)/shard_map/merged_parts/pallas_call | solution.py:166
  77.2 0.0 all-to-all-done.4.p_ref
  77.2 0.4 q_pieces.1
  77.6 10.8 %all_to_all.43.x_ref = f32[8,16,128]{2,1,0:T(8,128)S(1)} all-to-all(f32[8,16,128]{2,1,0:T(8,128)S(1)} %q_pieces.1), channel_id=1, replica_groups={{0,64,128,192,256,320,384,448},{8,72,136,200,264,328,392,456},{16,80,14..., dimensions={0} | all-to-all | bytes 131072 | tf_op jit(solution)/shard_map/all_to_all | solution.py:360
  88.4 10.8 %all_to_all.44.x_ref = f32[8,16,128]{2,1,0:T(8,128)S(1)} all-to-all(f32[8,16,128]{2,1,0:T(8,128)S(1)} %total.8), channel_id=1, replica_groups={{0,8,16,24,32,40,48,56},{64,72,80,88,96,104,112,120},{128,136,144,152,1..., dimensions={0} | all-to-all | bytes 131072 | tf_op jit(solution)/shard_map/all_to_all | solution.py:363
  99.1 0.6 total.9.after_ref
  99.8 3.4 %all-to-all-start.7 = ((f32[8,16,128]{2,1,0:T(8,128)}), f32[8,16,128]{2,1,0:T(8,128)S(1)}, u32[]{:S(2)}, u32[]{:S(2)}) async-start(f32[8,16,128]{2,1,0:T(8,128)} %total.9.after_ref), calls=%async_computation.7 | async-start | bytes 131072 | tf_op jit(solution)/shard_map/all_to_all | solution.py:360
  103.1 4.0 %basis.1 = (f32[32,32]{1,0:T(8,128)S(1)}, f32[32,1024]{1,0:T(8,128)}, bf16[1024,128]{1,0:T(8,128)(2,1)S(1)}) custom-call(f32[8,32,128]{2,1,0:T(8,128)S(1)} %all-to-all-done.4.p_ref, f32[8,16,128]{2,1,0:T(8,128)} %total.9.after_ref), custom_call_target="tpu_custom_call" | custom-call | flops 4000000000 | bytes 4000000 | tf_op jit(solution)/shard_map/basis/pallas_call | solution.py:260
  107.1 4.3 %all-to-all-done.7.refs_0_ = f32[8,16,128]{2,1,0:T(8,128)S(1)} async-done(((f32[8,16,128]{2,1,0:T(8,128)}), f32[8,16,128]{2,1,0:T(8,128)S(1)}, u32[]{:S(2)}, u32[]{:S(2)}) %all-to-all-start.7) | async-done | bytes 65568 | tf_op jit(solution)/shard_map/all_to_all | solution.py:360
  111.4 1.4 %residual.1 = (bf16[1024,512]{1,0:T(8,128)(2,1)}, f32[32,512]{1,0:T(8,128)}) custom-call(f32[8,16,128]{2,1,0:T(8,128)S(1)} %all-to-all-done.7.refs_0_, f32[32,32]{1,0:T(8,128)S(1)} %get-tuple-element.16.refs_1_, bf16[1024,128]{1,0:T(8,128)(2,1)S(1)} %get-tuple-element.17.refs_2_, bf16[1024,512]{1,0:T(8,128)(2,1)S(1)} %get-tuple-element.14.hi_ref.refs_3_, ...), custom_call_target="tpu_custom_call" | custom-call | tf_op jit(solution)/shard_map/residual/pallas_call | solution.py:309
  (3 shorter events, 0.0 us)
Async XLA Ops:
  7.2 18.3 %copy-start = (bf16[256,1024]{1,0:T(8,128)(2,1)S(1)}, bf16[256,1024]{1,0:T(8,128)(2,1)}, u32[]{:S(2)}) copy-start(bf16[256,1024]{1,0:T(8,128)(2,1)} %acts_ref.1) | copy-start | bytes 1572868
  7.2 64.6 %all-gather.2.cloned.1.call-start = ((), (), s32[]{:S(2)}) async-start(), calls=%async_computation.8 | async-start | bytes 4718592 | tf_op jit(solution)/shard_map/all_gather | solution.py:369
  10.1 15.3 %all-to-all-start = ((f32[8,32,256]{2,1,0:T(8,128)}), f32[8,32,256]{2,1,0:T(8,128)S(1)}, u32[]{:S(2)}, u32[]{:S(2)}) async-start(f32[8,32,256]{2,1,0:T(8,128)} %y_chunks.1), calls=%async_computation | async-start | bytes 524288 | tf_op jit(solution)/shard_map/all_to_all | solution.py:357
  19.3 1.2 %copy-start.1 = (bf16[1,1024,512]{2,1,0:T(8,128)(2,1)S(1)}, bf16[1,1024,512]{2,1,0:T(8,128)(2,1)}, u32[]{:S(2)}) copy-start(bf16[1,1024,512]{2,1,0:T(8,128)(2,1)} %param.6) | copy-start | bytes 3145732
  20.6 0.8 copy-start.2
  67.1 10.1 %all-to-all-start.4 = ((f32[8,32,128]{2,1,0:T(8,128)}), f32[8,32,128]{2,1,0:T(8,128)S(1)}, u32[]{:S(2)}, u32[]{:S(2)}) async-start(f32[8,32,128]{2,1,0:T(8,128)} %total.7.after_ref), calls=%async_computation.4 | async-start | bytes 262144 | tf_op jit(solution)/shard_map/all_to_all | solution.py:357
  99.8 11.7 %all-to-all-start.7 = ((f32[8,16,128]{2,1,0:T(8,128)}), f32[8,16,128]{2,1,0:T(8,128)S(1)}, u32[]{:S(2)}, u32[]{:S(2)}) async-start(f32[8,16,128]{2,1,0:T(8,128)} %total.9.after_ref), calls=%async_computation.7 | async-start | bytes 131072 | tf_op jit(solution)/shard_map/all_to_all | solution.py:360
Sparse Core Ops, SparseCore 0:
  10.2 41.9 all-gather.1

commit v11 on v10

--- a/solution.py
+++ b/solution.py
@@ -365,10 +365,12 @@
     error = error_buffer[0]
     q_t = prior_q.T
     y_mine = y_chunks(q_t, grads_out, tensor)
-    late_acts, y_mine = lax.optimization_barrier((acts, y_mine))
+    late_q, y_mine = lax.optimization_barrier((q_t, y_mine))
+    e_term = error_term(late_q, error)
+    late_acts, e_term = lax.optimization_barrier((acts, e_term))
     acts_all = lax.all_gather(late_acts, "tensor", axis=0, tiled=True)
     y_all = over_tensor(y_mine)
-    p_terms = over_tensor(p_chunks(y_all, acts, error_term(q_t, error)))
+    p_terms = over_tensor(p_chunks(y_all, acts, e_term))
     p_row = total_for(over_y(total_for(p_terms, side)), side)
     p_last = total_for(over_z(p_row), tensor)
     p_all = over_tensor(p_last)

time: 120 us -> 123 us (1.025)
  blocking collectives: 62.2 us -> 77.6 us
  starting transfers between devices: 17.4 us -> 8.13 us
  waiting for transfers between devices: 8.05 us -> 4.34 us
    all_to_all x1 -> x2, blocking collectives: 9.76 us -> 25 us  [over_tensor(): return lax.all_to_all(x, 'tensor', 0, 0)]
    all_to_all x2 -> x1, starting transfers between devices: 14 us -> 4.74 us  [over_tensor(): return lax.all_to_all(x, 'tensor', 0, 0)]
    all_to_all x2 -> x1, waiting for transfers between devices: 3.73 us -> 0.01 us  [over_tensor(): return lax.all_to_all(x, 'tensor', 0, 0)]
  transfers between devices with their start and end apart: 4 -> 3, of which waited for: 2 -> 1; matrix products, arithmetic and copies ran while one was open for 0% -> 0% of each run, Pallas kernels for 9% -> 8%
where the time goes in v11:
time: 123 us; the launch traced here: 122 us
  blocking collectives  77.6 us (63%)
  Pallas kernels  16 us (13%)
  between operations  14.1 us (11%)
  starting transfers between devices  8.13 us (7%)
  waiting for transfers between devices  4.34 us (4%)
  local copies, waits for them, and re-layouts  1.98 us (2%)
    all_to_all x2, blocking collectives, over_z(): return lax.all_to_all(x, 'dp', 0, 0, axis_index_groups=along_z)  30.3 us
    all_to_all x2, blocking collectives, over_tensor(): return lax.all_to_all(x, 'tensor', 0, 0)  25 us
    all_to_all x2, blocking collectives, over_y(): return lax.all_to_all(x, 'dp', 0, 0, axis_index_groups=along_y)  22.2 us
    pallas_call x1, Pallas kernels, merged_parts(): pl.pallas_call(merged_kernel, in_specs=[HBM, HBM, HBM, ANY], out_specs=[V...  5.38 us
    all_to_all x1, starting transfers between devices, over_tensor(): return lax.all_to_all(x, 'tensor', 0, 0)  4.74 us
    all_to_all x1, waiting for transfers between devices, over_y(): return lax.all_to_all(x, 'dp', 0, 0, axis_index_groups=along_y)  4.31 us
    pallas_call x1, Pallas kernels, basis_of(): pl.pallas_call(basis_kernel, in_specs=[VMEM, ANY], out_specs=[VMEM] * 3,...  3.99 us
    all_to_all x1, starting transfers between devices, over_y(): return lax.all_to_all(x, 'dp', 0, 0, axis_index_groups=along_y)  3.35 us
  transfers between devices with their start and end apart: 3, of which 1 were waited for; matrix products, arithmetic and copies ran while one was open for 0% of the time, Pallas kernels for 8%

profile of v11, /device:TPU:2, one launch (start us, length us, event | category | flops | bytes accessed | tf_op | source)
XLA Modules:
  0.0 122.1 jit_solution(16760191219423682513)
XLA Ops:
  7.2 0.0 copy-start
  7.2 0.0 all-gather.2.cloned.1.call-start
  7.2 2.8 %y_chunks.1 = f32[8,32,256]{2,1,0:T(8,128)} custom-call(bf16[32,512]{1,0:T(8,128)(2,1)} %bitcast.7, bf16[2048,512]{1,0:T(8,128)(2,1)} %g_ref.3), custom_call_target="tpu_custom_call" | custom-call | flops 536870912 | bytes 2097152 | tf_op jit(solution)/shard_map/y_chunks/pallas_call | solution.py:70
  10.1 0.0 copy-start.1
  10.1 1.2 copy-done.1
  11.3 0.0 copy-start.2
  11.3 0.8 copy-done.2
  12.0 0.4 error_term.1.e_ref
  12.4 0.0 all-gather.2.cloned.1.call-update
  12.5 15.3 %all_to_all.40.y_ref = f32[8,32,256]{2,1,0:T(8,128)S(1)} all-to-all(f32[8,32,256]{2,1,0:T(8,128)} %y_chunks.1), channel_id=1, replica_groups=mesh['dp'=64,'tensor'=8] {'tensor'}, dimensions={0} | all-to-all | bytes 524288 | tf_op jit(solution)/shard_map/all_to_all | solution.py:357
  27.8 0.0 copy-done
  27.8 0.2 p_chunks.1
  28.0 9.7 %all_to_all.41.x_ref = f32[8,32,128]{2,1,0:T(8,128)S(1)} all-to-all(f32[8,32,128]{2,1,0:T(8,128)S(1)} %p_chunks.1), channel_id=1, replica_groups=mesh['dp'=64,'tensor'=8] {'tensor'}, dimensions={0} | all-to-all | bytes 262144 | tf_op jit(solution)/shard_map/all_to_all | solution.py:357
  37.8 11.5 %all_to_all.42.x_ref = f32[8,32,128]{2,1,0:T(8,128)S(1)} all-to-all(f32[8,32,128]{2,1,0:T(8,128)S(1)} %total.5), channel_id=1, replica_groups={{0,64,128,192,256,320,384,448},{8,72,136,200,264,328,392,456},{16,80,14..., dimensions={0} | all-to-all | bytes 262144 | tf_op jit(solution)/shard_map/all_to_all | solution.py:360
  49.2 19.5 %all_to_all.43.x_ref = f32[8,32,128]{2,1,0:T(8,128)S(1)} all-to-all(f32[8,32,128]{2,1,0:T(8,128)S(1)} %total.6), channel_id=1, replica_groups={{0,8,16,24,32,40,48,56},{64,72,80,88,96,104,112,120},{128,136,144,152,1..., dimensions={0} | all-to-all | bytes 262144 | tf_op jit(solution)/shard_map/all_to_all | solution.py:363
  68.8 0.7 total.7.after_ref
  69.5 4.7 %all-to-all-start.4 = ((f32[8,32,128]{2,1,0:T(8,128)}), f32[8,32,128]{2,1,0:T(8,128)S(1)}, u32[]{:S(2)}, u32[]{:S(2)}) async-start(f32[8,32,128]{2,1,0:T(8,128)} %total.7.after_ref), calls=%async_computation.4 | async-start | bytes 262144 | tf_op jit(solution)/shard_map/all_to_all | solution.py:357
  74.2 0.0 all-gather.2.cloned.1.call-done.a_ref
  74.2 5.4 %merged_parts.1 = (bf16[1024,512]{1,0:T(8,128)(2,1)S(1)}, bf16[1024,512]{1,0:T(8,128)(2,1)S(1)}) custom-call(bf16[2048,1024]{1,0:T(8,128)(2,1)} %all-gather.2.cloned.1.call-done.a_ref, bf16[2048,512]{1,0:T(8,128)(2,1)} %g_ref.3, bf16[1024,512]{1,0:T(8,128)(2,1)} %bitcast.5, f32[8,32,128]{2,1,0:T(8,128)} %total.7.after_ref), custom_call_target="tpu_custom_call" | custom-call | flops 2147483648 | bytes 6291456 | tf_op jit(solution)/shard_map/merged_parts/pallas_call | solution.py:166
  79.6 0.0 all-to-all-done.4.p_ref
  79.6 0.4 q_pieces.1
  80.0 10.8 %all_to_all.44.x_ref = f32[8,16,128]{2,1,0:T(8,128)S(1)} all-to-all(f32[8,16,128]{2,1,0:T(8,128)S(1)} %q_pieces.1), channel_id=1, replica_groups={{0,64,128,192,256,320,384,448},{8,72,136,200,264,328,392,456},{16,80,14..., dimensions={0} | all-to-all | bytes 131072 | tf_op jit(solution)/shard_map/all_to_all | solution.py:360
  90.8 10.8 %all_to_all.45.x_ref = f32[8,16,128]{2,1,0:T(8,128)S(1)} all-to-all(f32[8,16,128]{2,1,0:T(8,128)S(1)} %total.8), channel_id=1, replica_groups={{0,8,16,24,32,40,48,56},{64,72,80,88,96,104,112,120},{128,136,144,152,1..., dimensions={0} | all-to-all | bytes 131072 | tf_op jit(solution)/shard_map/all_to_all | solution.py:363
  101.6 0.6 total.9.after_ref
  102.2 3.4 %all-to-all-start.7 = ((f32[8,16,128]{2,1,0:T(8,128)}), f32[8,16,128]{2,1,0:T(8,128)S(1)}, u32[]{:S(2)}, u32[]{:S(2)}) async-start(f32[8,16,128]{2,1,0:T(8,128)} %total.9.after_ref), calls=%async_computation.7 | async-start | bytes 131072 | tf_op jit(solution)/shard_map/all_to_all | solution.py:360
  105.6 4.0 %basis.1 = (f32[32,32]{1,0:T(8,128)S(1)}, f32[32,1024]{1,0:T(8,128)}, bf16[1024,128]{1,0:T(8,128)(2,1)S(1)}) custom-call(f32[8,32,128]{2,1,0:T(8,128)S(1)} %all-to-all-done.4.p_ref, f32[8,16,128]{2,1,0:T(8,128)} %total.9.after_ref), custom_call_target="tpu_custom_call" | custom-call | flops 4000000000 | bytes 4000000 | tf_op jit(solution)/shard_map/basis/pallas_call | solution.py:260
  109.5 4.3 %all-to-all-done.7.refs_0_ = f32[8,16,128]{2,1,0:T(8,128)S(1)} async-done(((f32[8,16,128]{2,1,0:T(8,128)}), f32[8,16,128]{2,1,0:T(8,128)S(1)}, u32[]{:S(2)}, u32[]{:S(2)}) %all-to-all-start.7) | async-done | bytes 65568 | tf_op jit(solution)/shard_map/all_to_all | solution.py:360
  113.8 1.4 %residual.1 = (bf16[1024,512]{1,0:T(8,128)(2,1)}, f32[32,512]{1,0:T(8,128)}) custom-call(f32[8,16,128]{2,1,0:T(8,128)S(1)} %all-to-all-done.7.refs_0_, f32[32,32]{1,0:T(8,128)S(1)} %get-tuple-element.20.refs_1_, bf16[1024,128]{1,0:T(8,128)(2,1)S(1)} %get-tuple-element.21.refs_2_, bf16[1024,512]{1,0:T(8,128)(2,1)S(1)} %get-tuple-element.18.hi_ref.refs_3_, ...), custom_call_target="tpu_custom_call" | custom-call | tf_op jit(solution)/shard_map/residual/pallas_call | solution.py:309
  (3 shorter events, 0.0 us)
Async XLA Ops:
  7.2 20.6 %copy-start = (bf16[256,1024]{1,0:T(8,128)(2,1)S(1)}, bf16[256,1024]{1,0:T(8,128)(2,1)}, u32[]{:S(2)}) copy-start(bf16[256,1024]{1,0:T(8,128)(2,1)} %acts_ref.1) | copy-start | bytes 1572868
  7.2 67.0 %all-gather.2.cloned.1.call-start = ((), (), s32[]{:S(2)}) async-start(), calls=%async_computation.8 | async-start | bytes 4718592 | tf_op jit(solution)/shard_map/all_gather | solution.py:371
  10.1 1.2 %copy-start.1 = (bf16[1,1024,512]{2,1,0:T(8,128)(2,1)S(1)}, bf16[1,1024,512]{2,1,0:T(8,128)(2,1)}, u32[]{:S(2)}) copy-start(bf16[1,1024,512]{2,1,0:T(8,128)(2,1)} %param.6) | copy-start | bytes 3145732
  11.3 0.8 copy-start.2
  69.5 10.1 %all-to-all-start.4 = ((f32[8,32,128]{2,1,0:T(8,128)}), f32[8,32,128]{2,1,0:T(8,128)S(1)}, u32[]{:S(2)}, u32[]{:S(2)}) async-start(f32[8,32,128]{2,1,0:T(8,128)} %total.7.after_ref), calls=%async_computation.4 | async-start | bytes 262144 | tf_op jit(solution)/shard_map/all_to_all | solution.py:357
  102.2 11.7 %all-to-all-start.7 = ((f32[8,16,128]{2,1,0:T(8,128)}), f32[8,16,128]{2,1,0:T(8,128)S(1)}, u32[]{:S(2)}, u32[]{:S(2)}) async-start(f32[8,16,128]{2,1,0:T(8,128)} %total.9.after_ref), calls=%async_computation.7 | async-start | bytes 131072 | tf_op jit(solution)/shard_map/all_to_all | solution.py:360
Sparse Core Ops, SparseCore 0:
  12.6 41.8 all-gather.1
